TPU v7x, 32 devices: a whole 2x2x4 slice. The times are simulated.
32 devices in a mesh: section: 2 (over x), tensor: 2 (over core), fsdp: 8 (over z, y).
Axes of the slice: x: 2, y: 2, z: 4, core: 2. Of those that a mesh axis runs over, the one named last changes fastest.
Arguments:
- tokens: bfloat16 [2, 16, 82, 384], P(None, ('fsdp', 'tensor')), may hold values from -6 to 6
- out_grad: bfloat16 [2, 16, 82, 384], P(None, ('fsdp', 'tensor')), may hold values from -6 to 6
- image_count: int32 [2, 8], P(None, 'fsdp'), may hold values from 1 to 2, as said below
- w_qkv: bfloat16 [2, 384, 3, 384], P('section', 'fsdp', None, 'tensor'), may hold values from -0.3125 to 0.3125
- w_out: bfloat16 [2, 384, 384], P('section', 'tensor', 'fsdp'), may hold values from -1.25 to 1.25
- w_up: bfloat16 [2, 384, 1536], P('section', 'fsdp', 'tensor'), may hold values from -0.3125 to 0.3125
- w_down: bfloat16 [2, 1536, 384], P('section', 'tensor', 'fsdp'), may hold values from -0.15625 to 0.15625
- head_bias: bfloat16 [2, 2, 384], P('section', None, ('tensor', 'fsdp')), may hold values from -3 to 3
- up_bias: bfloat16 [2, 1536], P('section', ('tensor', 'fsdp')), may hold values from -3 to 3
- gains: bfloat16 [2, 2, 384], P('section', None, ('tensor', 'fsdp')), may hold values from 0.5 to 1.5
- shifts: bfloat16 [2, 4, 384], P('section', None, ('tensor', 'fsdp')), may hold values from -2 to 2
Outputs:
- activations: bfloat16 [2, 2, 16, 82, 384], P('section', None, ('fsdp', 'tensor'))
- input_grads: bfloat16 [2, 2, 16, 82, 384], P('section', None, ('fsdp', 'tensor'))
- grad_qkv: float32 [2, 384, 3, 384], P('section', 'fsdp', None, 'tensor')
- grad_out: float32 [2, 384, 384], P('section', 'tensor', 'fsdp')
- grad_up: float32 [2, 384, 1536], P('section', 'fsdp', 'tensor')
- grad_down: float32 [2, 1536, 384], P('section', 'tensor', 'fsdp')
- grad_head_bias: float32 [2, 2, 384], P('section', None, ('tensor', 'fsdp'))
- grad_up_bias: float32 [2, 1536], P('section', ('tensor', 'fsdp'))
- grad_gains: float32 [2, 2, 384], P('section', None, ('tensor', 'fsdp'))
- grad_shifts: float32 [2, 4, 384], P('section', None, ('tensor', 'fsdp'))
Inputs may be any that keep to these rules, and one draw needn't show every extreme that they name: The first image_count[m, f] image slots of data shard f in micro-batch m hold images, the other slots are empty. In every draw some shard holds 2 images and some holds one.
All inputs are finite; a program needn't handle non-finite values.
Results may differ from a plain program's by a relative error of at most 0.015.
Values may be sent and summed in bfloat16 or wider, within the bound.
No kernel may reach another device: no remote copies, remote signals or barrier semaphores. Data moves between devices by JAX's collectives and lax.ppermute only.
A program may use at most 128 MiB of HBM per device.

v0:
```python
import math

import jax
import jax.numpy as jnp
from jax import lax
from jax.sharding import PartitionSpec as P

HD = 64


EPS = 1e-06
INV_ROOT_TWO = 0.7071067811865476
INV_ROOT_TWO_PI = 0.3989422804014327


def swapped(block, axis, distance):
    count = lax.axis_size(axis)
    route = []
    for low in range(count):
        high = low | 1 << distance
        if high != low and high < count:
            route += [(low, high), (high, low)]
    return lax.ppermute(block, axis, route)


def normalize(value):
    mean = jnp.mean(value, axis=-1, keepdims=True)
    centred = value - mean
    var = jnp.mean(centred * centred, axis=-1, keepdims=True)
    factor = lax.rsqrt(var + EPS)
    return (centred * factor, factor)


def norm_back(grad_norm, unit, factor, gain):
    scaled = grad_norm * gain
    mean_plain = jnp.mean(scaled, axis=-1, keepdims=True)
    mean_unit = jnp.mean(scaled * unit, axis=-1, keepdims=True)
    return (scaled - mean_plain - unit * mean_unit) * factor


def forward(state, weights, gain_all, shift_all):
    w_qkv, w_out, w_up, w_down, head_bias, up_bias = weights
    unit_one, factor_one = normalize(state)
    first = (unit_one * gain_all[0] + shift_all[0]).astype(jnp.bfloat16)
    first_all = lax.all_gather(first, "tensor", axis=0, tiled=True)
    proj = jnp.einsum("gsd,dke->gske", first_all, w_qkv, preferred_element_type=jnp.float32)
    count, seq = (proj.shape[0], proj.shape[1])
    local = w_qkv.shape[2]
    heads = local // HD
    scale = 1.0 / math.sqrt(HD)
    query = (proj[:, :, 0] + head_bias[0]).astype(jnp.bfloat16).reshape(count, seq, heads, HD)
    keys = proj[:, :, 1].astype(jnp.bfloat16).reshape(count, seq, heads, HD)
    values = (proj[:, :, 2] + head_bias[1]).astype(jnp.bfloat16).reshape(count, seq, heads, HD)
    scores = jnp.einsum("gqhe,gkhe->ghqk", query, keys, preferred_element_type=jnp.float32) * scale
    top = jnp.max(scores, axis=-1, keepdims=True)
    expo = jnp.exp(scores - top)
    total = jnp.sum(expo, axis=-1, keepdims=True)
    probs = expo / total
    log_total = top + jnp.log(total)
    mixed = jnp.einsum(
        "ghqk,gkhe->gqhe", probs.astype(jnp.bfloat16), values, preferred_element_type=jnp.float32
    )
    mixed = mixed.astype(jnp.bfloat16).reshape(count, seq, local)
    piece = mixed
    attn = (
        lax.psum_scatter(
            jnp.einsum("gsd,de->gse", piece, w_out, preferred_element_type=jnp.float32).astype(
                jnp.bfloat16
            ),
            "tensor",
            scatter_dimension=0,
            tiled=True,
        ).astype(jnp.float32)
        + shift_all[1]
    )
    resid = state + attn
    unit_two, factor_two = normalize(resid)
    second = (unit_two * gain_all[1] + shift_all[2]).astype(jnp.bfloat16)
    second_all = lax.all_gather(second, "tensor", axis=0, tiled=True)
    hidden = (
        jnp.einsum("gsd,df->gsf", second_all, w_up, preferred_element_type=jnp.float32) + up_bias
    )
    active = jax.nn.gelu(hidden, approximate=False).astype(jnp.bfloat16)
    piece = active
    branch = (
        lax.psum_scatter(
            jnp.einsum("gsf,fd->gsd", piece, w_down, preferred_element_type=jnp.float32).astype(
                jnp.bfloat16
            ),
            "tensor",
            scatter_dimension=0,
            tiled=True,
        ).astype(jnp.float32)
        + shift_all[3]
    )
    output = resid + branch
    kept = (
        unit_one,
        factor_one,
        first_all,
        query,
        keys,
        values,
        log_total,
        mixed,
        unit_two,
        factor_two,
        second_all,
        hidden,
        active,
    )
    return (output, kept)


def backward(grad_output, kept, weights, gain_all):
    w_qkv, w_out, w_up, w_down, head_bias, up_bias = weights
    (
        unit_one,
        factor_one,
        first_all,
        query,
        keys,
        values,
        log_total,
        mixed,
        unit_two,
        factor_two,
        second_all,
        hidden,
        active,
    ) = kept
    count, seq, heads = (query.shape[0], query.shape[1], query.shape[2])
    local = heads * HD
    scale = 1.0 / math.sqrt(HD)
    branch_low = grad_output.astype(jnp.bfloat16)
    branch_all = lax.all_gather(branch_low, "tensor", axis=0, tiled=True)
    grad_down = jnp.einsum("gsf,gsd->fd", active, branch_all, preferred_element_type=jnp.float32)
    grad_active = jnp.einsum("gsd,fd->gsf", branch_all, w_down, preferred_element_type=jnp.float32)
    slope = (
        0.5 * (1.0 + lax.erf(hidden * INV_ROOT_TWO))
        + hidden * jnp.exp(-0.5 * hidden * hidden) * INV_ROOT_TWO_PI
    )
    grad_hidden = (grad_active * slope).astype(jnp.bfloat16)
    grad_up_bias = jnp.sum(grad_hidden.astype(jnp.float32), axis=(0, 1))
    grad_up = jnp.einsum("gsd,gsf->df", second_all, grad_hidden, preferred_element_type=jnp.float32)
    piece = grad_hidden
    grad_second = lax.psum_scatter(
        jnp.einsum("gsf,df->gsd", piece, w_up, preferred_element_type=jnp.float32).astype(
            jnp.bfloat16
        ),
        "tensor",
        scatter_dimension=0,
        tiled=True,
    ).astype(jnp.float32)
    gain_two = jnp.sum(grad_second * unit_two, axis=(0, 1))
    shift_two = jnp.sum(grad_second, axis=(0, 1))
    grad_resid = grad_output + norm_back(grad_second, unit_two, factor_two, gain_all[1])
    attn_low = grad_resid.astype(jnp.bfloat16)
    shift_attn = jnp.sum(attn_low.astype(jnp.float32), axis=(0, 1))
    shift_branch = jnp.sum(branch_low.astype(jnp.float32), axis=(0, 1))
    attn_all = lax.all_gather(attn_low, "tensor", axis=0, tiled=True)
    grad_out_w = jnp.einsum("gsd,gse->de", mixed, attn_all, preferred_element_type=jnp.float32)
    grad_mixed = jnp.einsum("gse,de->gsd", attn_all, w_out, preferred_element_type=jnp.float32)
    grad_mixed = grad_mixed.astype(jnp.bfloat16).reshape(count, seq, heads, HD)
    scores = jnp.einsum("gqhe,gkhe->ghqk", query, keys, preferred_element_type=jnp.float32) * scale
    probs = jnp.exp(scores - log_total)
    grad_values = jnp.einsum(
        "ghqk,gqhe->gkhe",
        probs.astype(jnp.bfloat16),
        grad_mixed,
        preferred_element_type=jnp.float32,
    )
    grad_values = grad_values.astype(jnp.bfloat16)
    grad_probs = jnp.einsum(
        "gqhe,gkhe->ghqk", grad_mixed, values, preferred_element_type=jnp.float32
    )
    inner = jnp.sum(grad_probs * probs, axis=-1, keepdims=True)
    grad_scores = (probs * (grad_probs - inner)).astype(jnp.bfloat16)
    grad_query = (
        jnp.einsum("ghqk,gkhe->gqhe", grad_scores, keys, preferred_element_type=jnp.float32) * scale
    )
    grad_keys = (
        jnp.einsum("ghqk,gqhe->gkhe", grad_scores, query, preferred_element_type=jnp.float32)
        * scale
    )
    grad_query = grad_query.astype(jnp.bfloat16).reshape(count, seq, local)
    grad_keys = grad_keys.astype(jnp.bfloat16).reshape(count, seq, local)
    grad_values = grad_values.reshape(count, seq, local)
    grad_proj = jnp.stack([grad_query, grad_keys, grad_values], axis=2)
    grad_head_bias = jnp.stack(
        [
            jnp.sum(grad_query.astype(jnp.float32), axis=(0, 1)),
            jnp.sum(grad_values.astype(jnp.float32), axis=(0, 1)),
        ]
    )
    grad_qkv = jnp.einsum("gsd,gske->dke", first_all, grad_proj, preferred_element_type=jnp.float32)
    piece = grad_proj
    grad_first = lax.psum_scatter(
        jnp.einsum("gske,dke->gsd", piece, w_qkv, preferred_element_type=jnp.float32).astype(
            jnp.bfloat16
        ),
        "tensor",
        scatter_dimension=0,
        tiled=True,
    ).astype(jnp.float32)
    gain_one = jnp.sum(grad_first * unit_one, axis=(0, 1))
    shift_one = jnp.sum(grad_first, axis=(0, 1))
    grad_state = grad_resid + norm_back(grad_first, unit_one, factor_one, gain_all[0])
    grads = (grad_qkv, grad_out_w, grad_up, grad_down, grad_head_bias, grad_up_bias)
    norm_grads = (
        jnp.stack([gain_one, gain_two]),
        jnp.stack([shift_one, shift_attn, shift_two, shift_branch]),
    )
    return (grad_state, grads, norm_grads)


def add_trees(left, right):
    if left is None:
        return right
    return jax.tree.map(lambda u, v: u + v, left, right)


def per_device(
    tokens, out_grad, image_count, w_qkv, w_out, w_up, w_down, head_bias, up_bias, gains, shifts
):
    section = lax.axis_index("section")
    tensor_index = lax.axis_index("tensor")
    weights = (
        lax.all_gather(w_qkv[0], "fsdp", axis=0, tiled=True),
        lax.all_gather(w_out[0], "fsdp", axis=1, tiled=True),
        lax.all_gather(w_up[0], "fsdp", axis=0, tiled=True),
        lax.all_gather(w_down[0], "fsdp", axis=1, tiled=True),
        lax.all_gather(head_bias[0], "fsdp", axis=1, tiled=True),
        lax.all_gather(up_bias[0], "fsdp", axis=0, tiled=True),
    )
    gain_low, shift_low = (
        lax.all_gather(gains[0], ("tensor", "fsdp"), axis=1, tiled=True),
        lax.all_gather(shifts[0], ("tensor", "fsdp"), axis=1, tiled=True),
    )
    gain_all = gain_low.astype(jnp.float32)
    shift_all = shift_low.astype(jnp.float32)
    micro = tokens.shape[0]
    own = tokens.shape[1]
    slot_ids = tensor_index * own + jnp.arange(own, dtype=jnp.int32)
    counts = image_count[:, 0]

    def live_rows(index):
        number = lax.dynamic_index_in_dim(counts, index, 0, keepdims=False)
        return (slot_ids < number).astype(jnp.float32)[:, None, None]

    incoming = jnp.zeros(tokens.shape[1:], jnp.bfloat16)
    acts = jnp.zeros(tokens.shape, jnp.bfloat16)
    in_grads = jnp.zeros(tokens.shape, jnp.bfloat16)
    saved = []
    totals = None
    norm_totals = None
    for tick in range(micro + 2):
        ahead = tick - section
        ahead_ok = (ahead >= 0) & (ahead < micro)
        ahead_idx = jnp.clip(ahead, 0, micro - 1)
        first_in = lax.dynamic_index_in_dim(tokens, ahead_idx, 0, keepdims=False)
        state = jnp.where(section == 0, first_in, incoming).astype(jnp.float32)
        output, kept = forward(state, weights, gain_all, shift_all)
        out_low = output.astype(jnp.bfloat16)
        shown = out_low * live_rows(ahead_idx).astype(jnp.bfloat16)
        acts = jnp.where(ahead_ok, lax.dynamic_update_index_in_dim(acts, shown, ahead_idx, 0), acts)
        saved.append(kept)
        behind = tick - 2 + section
        behind_ok = (behind >= 0) & (behind < micro)
        behind_idx = jnp.clip(behind, 0, micro - 1)
        earlier = saved[tick - 2] if tick >= 2 else kept
        kept_back = jax.tree.map(lambda u, v: jnp.where(section == 0, u, v), earlier, kept)
        last_grad = lax.dynamic_index_in_dim(out_grad, behind_idx, 0, keepdims=False).astype(
            jnp.float32
        )
        last_grad = last_grad * live_rows(behind_idx)
        cotangent = jnp.where(section == 0, incoming.astype(jnp.float32), last_grad)
        cotangent = jnp.where(behind_ok, cotangent, 0.0)
        grad_state, grads, norm_grads = backward(cotangent, kept_back, weights, gain_all)
        grad_low = grad_state.astype(jnp.bfloat16)
        in_grads = jnp.where(
            behind_ok, lax.dynamic_update_index_in_dim(in_grads, grad_low, behind_idx, 0), in_grads
        )
        totals = add_trees(totals, grads)
        norm_totals = add_trees(norm_totals, norm_grads)
        outgoing = jnp.where(section == 0, out_low, grad_low)
        incoming = swapped(outgoing, "section", 0)
    totals = (
        lax.psum_scatter(totals[0], "fsdp", scatter_dimension=0, tiled=True),
        lax.psum_scatter(totals[1], "fsdp", scatter_dimension=1, tiled=True),
        lax.psum_scatter(totals[2], "fsdp", scatter_dimension=0, tiled=True),
        lax.psum_scatter(totals[3], "fsdp", scatter_dimension=1, tiled=True),
        lax.psum_scatter(totals[4], "fsdp", scatter_dimension=1, tiled=True),
        lax.psum_scatter(totals[5], "fsdp", scatter_dimension=0, tiled=True),
    )
    gain_grad, shift_grad = (
        lax.psum_scatter(norm_totals[0], ("tensor", "fsdp"), scatter_dimension=1, tiled=True),
        lax.psum_scatter(norm_totals[1], ("tensor", "fsdp"), scatter_dimension=1, tiled=True),
    )
    return (
        acts[None],
        in_grads[None],
        totals[0][None],
        totals[1][None],
        totals[2][None],
        totals[3][None],
        totals[4][None],
        totals[5][None],
        gain_grad[None],
        shift_grad[None],
    )


def solution(mesh):
    return jax.shard_map(
        per_device,
        mesh=mesh,
        in_specs=(
            P(None, ("fsdp", "tensor"), None, None),
            P(None, ("fsdp", "tensor"), None, None),
            P(None, "fsdp"),
            P("section", "fsdp", None, "tensor"),
            P("section", "tensor", "fsdp"),
            P("section", "fsdp", "tensor"),
            P("section", "tensor", "fsdp"),
            P("section", None, ("tensor", "fsdp")),
            P("section", ("tensor", "fsdp")),
            P("section", None, ("tensor", "fsdp")),
            P("section", None, ("tensor", "fsdp")),
        ),
        out_specs=(
            P("section", None, ("fsdp", "tensor"), None, None),
            P("section", None, ("fsdp", "tensor"), None, None),
            P("section", "fsdp", None, "tensor"),
            P("section", "tensor", "fsdp"),
            P("section", "fsdp", "tensor"),
            P("section", "tensor", "fsdp"),
            P("section", None, ("tensor", "fsdp")),
            P("section", ("tensor", "fsdp")),
            P("section", None, ("tensor", "fsdp")),
            P("section", None, ("tensor", "fsdp")),
        ),
        check_vma=False,
    )
```

profile of v0, /device:TPU:0, one launch (start us, length us, event | category | flops | bytes accessed | tf_op | source)
XLA Modules:
  0.0 821.9 jit_solution(15970789892317533209)
XLA Ops:
  8.0 35.5 %all-gather.1 = bf16[1,4,384]{1,0,2:T(2,128)(2,1)S(1)} all-gather(bf16[1,4,24]{1,0,2:T(2,128)(2,1)S(1)} %copy.252), channel_id=3, replica_groups=mesh['section'=2,'tensor'=2,'fsdp'=8] {'tensor','fsdp'}, dimensions={2}, use_global_device_ids=true | all-gather | bytes 3264 | tf_op jit(solution)/shard_map/all_gather | solution.py:238
  43.7 5.1 slice_reduce_fusion
  48.9 29.5 %all-gather = bf16[1,2,384]{1,0,2:T(2,128)(2,1)S(1)} all-gather(bf16[1,2,24]{1,0,2:T(2,128)(2,1)S(1)} %copy.251), channel_id=2, replica_groups=mesh['section'=2,'tensor'=2,'fsdp'=8] {'tensor','fsdp'}, dimensions={2}, use_global_device_ids=true | all-gather | bytes 1632 | tf_op jit(solution)/shard_map/all_gather | solution.py:237
  80.4 31.6 %all-gather.2 = bf16[1,384,3,192]{3,1,2,0:T(8,128)(2,1)S(1)} all-gather(bf16[1,48,3,192]{3,1,2,0:T(8,128)(2,1)S(1)} %copy-done.126), channel_id=4, replica_groups=mesh['section'=2,'tensor'=2,'fsdp'=8] {'fsdp'}, dimensions={1}, use_global_device_ids=true | all-gather | bytes 497664 | tf_op jit(solution)/shard_map/all_gather | solution.py:229
  116.8 30.5 %all-gather.3 = bf16[1,2,192]{1,0,2:T(2,128)(2,1)S(1)} all-gather(bf16[1,2,24]{1,0,2:T(2,128)(2,1)S(1)} %copy.255), channel_id=5, replica_groups=mesh['section'=2,'tensor'=2,'fsdp'=8] {'fsdp'}, dimensions={2}, use_global_device_ids=true | all-gather | bytes 864 | tf_op jit(solution)/shard_map/all_gather | solution.py:233
  147.4 3.0 fusion.264
  150.8 30.6 %all-gather.4 = bf16[1,192,384]{1,2,0:T(8,128)(2,1)S(1)} all-gather(bf16[1,192,48]{1,2,0:T(8,128)(2,1)S(1)} %copy-done.140), channel_id=6, replica_groups=mesh['section'=2,'tensor'=2,'fsdp'=8] {'fsdp'}, dimensions={2}, use_global_device_ids=true | all-gather | bytes 165888 | tf_op jit(solution)/shard_map/all_gather | solution.py:230
  184.8 19.8 %all-reduce = bf16[768]{0:T(1024)(128)(2,1)S(1)} all-reduce(bf16[768]{0:T(1024)(128)(2,1)S(1)} %dynamic-update-slice.10), channel_id=8, replica_groups=mesh['section'=2,'tensor'=2,'fsdp'=8] {'fsdp'}, use_global_device_ids=true, to_apply=%add | all-reduce | flops 768 | bytes 3072
  204.7 31.4 %all-gather.5 = bf16[1,384,768]{2,1,0:T(8,128)(2,1)S(1)} all-gather(bf16[1,48,768]{2,1,0:T(8,128)(2,1)S(1)} %copy-done.127), channel_id=7, replica_groups=mesh['section'=2,'tensor'=2,'fsdp'=8] {'fsdp'}, dimensions={1}, use_global_device_ids=true | all-gather | bytes 663552 | tf_op jit(solution)/shard_map/all_gather | solution.py:231
  239.2 2.0 all_gather.82
  241.2 31.6 %all-gather.7 = bf16[1,768,384]{1,2,0:T(8,128)(2,1)S(1)} all-gather(bf16[1,768,48]{1,2,0:T(8,128)(2,1)S(1)} %copy-done.128), channel_id=9, replica_groups=mesh['section'=2,'tensor'=2,'fsdp'=8] {'fsdp'}, dimensions={2}, use_global_device_ids=true | all-gather | bytes 663552 | tf_op jit(solution)/shard_map/all_gather | solution.py:232
  276.1 1.9 all_gather.78
  281.1 4.7 reduce-scatter.84.cloned.1.call-done
  287.4 2.2 convert_reduce_fusion.31
  298.0 2.0 fusion.20
  303.2 5.5 reduce-scatter.86.cloned.1.call-done
  311.3 8.5 %reduce-scatter.82.cloned.1.call-done = bf16[1,82,384]{2,1,0:T(8,128)(2,1)} async-done(((bf16[2,82,384]{2,1,0:T(8,128)(2,1)}), bf16[1,82,384]{2,1,0:T(8,128)(2,1)}) %reduce-scatter.82.cloned.1.call-update) | async-done | bytes 62992
  323.8 2.0 collective-permute-done
  326.7 1.9 all_gather.84
  332.1 2.0 all_gather.86
  334.2 6.6 reduce-scatter.88.cloned.1.call-done
  349.0 8.6 %reduce-scatter.92.cloned.1.call-done = bf16[1,82,384]{2,1,0:T(8,128)(2,1)} async-done(((bf16[2,82,384]{2,1,0:T(8,128)(2,1)}), bf16[1,82,384]{2,1,0:T(8,128)(2,1)}) %reduce-scatter.92.cloned.1.call-update) | async-done | bytes 62992
  359.2 2.3 convert_reduce_fusion.29
  371.5 2.3 fusion.69
  375.8 4.2 reduce-scatter.94.cloned.1.call-done
  382.7 8.7 %reduce-scatter.90.cloned.1.call-done = bf16[1,82,384]{2,1,0:T(8,128)(2,1)} async-done(((bf16[2,82,384]{2,1,0:T(8,128)(2,1)}), bf16[1,82,384]{2,1,0:T(8,128)(2,1)}) %reduce-scatter.90.cloned.1.call-update) | async-done | bytes 62992
  409.1 3.4 all_gather.90
  412.5 2.5 reduce-scatter.96.cloned.1.call-done
  426.9 1.9 fusion.19
  428.8 5.0 reduce-scatter.100.cloned.1.call-done
  435.5 2.3 convert_reduce_fusion.27
  442.9 2.5 convert_reduce_fusion.17
  454.2 2.0 fusion.22
  456.3 2.3 fusion.76
  460.5 4.4 reduce-scatter.102.cloned.1.call-done
  468.3 7.8 reduce-scatter.98.cloned.1.call-done
  479.4 2.0 convolution_bitcast_fusion.13
  498.1 2.0 all_gather.94
  503.6 3.0 reduce-scatter.104.cloned.1.call-done
  517.9 2.3 fusion.83
  522.1 4.2 reduce-scatter.108.cloned.1.call-done
  527.4 2.3 convert_reduce_fusion.25
  535.8 1.9 fusion.23
  561.5 21.9 %all-reduce.22 = (f32[2,192]{1,0:T(2,128)S(1)}, f32[768]{0:T(1024)S(1)}) all-reduce(f32[2,192]{1,0:T(2,128)S(1)} %fusion.299, f32[768]{0:T(1024)S(1)} %add_add_fusion), channel_id=30, replica_groups=mesh['section'=2,'tensor'=2,'fsdp'=8] {'fsdp'}, use_global_device_ids=true, to_apply=%region_72.73.clone | all-reduce | flops 1152 | bytes 9216
  587.7 30.7 %all-reduce.21 = (f32[2,384]{1,0:T(2,128)S(1)}, f32[4,384]{1,0:T(4,128)S(1)}) all-reduce(f32[2,384]{1,0:T(2,128)S(1)} %fusion.297, f32[4,384]{1,0:T(4,128)S(1)} %fusion.295), channel_id=32, replica_groups=mesh['section'=2,'tensor'=2,'fsdp'=8] {'tensor','fsdp'}, use_global_device_ids=true, to_apply=%region_86.87.clone | all-reduce | flops 2304 | bytes 18432
  619.7 61.0 %reduce-scatter.72.cloned.1.call-done = f32[48,3,192]{2,0,1:T(8,128)} async-done(((f32[384,3,192]{2,0,1:T(8,128)}), f32[48,3,192]{2,0,1:T(8,128)}) %reduce-scatter.72.cloned.1.call-update) | async-done | bytes 110608 | tf_op jit(solution)/shard_map/reduce_scatter | solution.py:289
  680.6 67.2 %reduce-scatter.76.cloned.1.call-done = f32[48,768]{1,0:T(8,128)} async-done(((f32[384,768]{1,0:T(8,128)}), f32[48,768]{1,0:T(8,128)}) %reduce-scatter.76.cloned.1.call-update) | async-done | bytes 147472 | tf_op jit(solution)/shard_map/reduce_scatter | solution.py:291
  747.8 66.9 %reduce-scatter.78.cloned.1.call-done = f32[768,48]{0,1:T(8,128)} async-done(((f32[768,384]{0,1:T(8,128)}), f32[768,48]{0,1:T(8,128)}) %reduce-scatter.78.cloned.1.call-update) | async-done | bytes 147472 | tf_op jit(solution)/shard_map/reduce_scatter | solution.py:292
  (769 shorter events, 182.9 us)
Async XLA Ops:
  7.2 41.7 %copy-start.219 = (bf16[1,2,24]{2,1,0:T(2,128)(2,1)S(1)}, bf16[1,2,24]{2,1,0:T(2,128)(2,1)}, u32[]{:S(2)}) copy-start(bf16[1,2,24]{2,1,0:T(2,128)(2,1)} %param.20) | copy-start | bytes 292
  7.2 265.7 %reduce-scatter.80.cloned.1.call-start = ((), (), s32[]{:S(2)}) async-start(), calls=%async_computation.24 | async-start | bytes 202752
  8.0 72.3 %copy-start.126 = (bf16[1,48,3,192]{3,1,2,0:T(8,128)(2,1)S(1)}, bf16[1,48,3,192]{3,1,2,0:T(8,128)(2,1)}, u32[]{:S(2)}) copy-start(bf16[1,48,3,192]{3,1,2,0:T(8,128)(2,1)} %param.14) | copy-start | bytes 165892
  43.7 68.3 %copy-start.24 = (bf16[2,1,82,384]{3,0,2,1:T(2,128)(2,1)S(1)}, bf16[2,1,82,384]{3,0,2,1:T(2,128)(2,1)}, u32[]{:S(2)}) copy-start(bf16[2,1,82,384]{3,0,2,1:T(2,128)(2,1)} %param.11) | copy-start | bytes 377860
  116.4 34.4 %copy-start.140 = (bf16[1,192,48]{1,2,0:T(8,128)(2,1)S(1)}, bf16[1,192,48]{1,2,0:T(8,128)(2,1)}, u32[]{:S(2)}) copy-start(bf16[1,192,48]{1,2,0:T(8,128)(2,1)} %param.15) | copy-start | bytes 55300
  150.4 179.4 %copy-start.133 = (f32[3,64]{1,0:T(4,128)}, f32[3,64]{1,0:T(4,128)S(1)}, u32[]{:S(2)}) copy-start(f32[3,64]{1,0:T(4,128)S(1)} %reshape.1015) | copy-start | bytes 2308
  150.7 31.6 %copy-start.136 = (f32[3,64]{1,0:T(4,128)}, f32[3,64]{1,0:T(4,128)S(1)}, u32[]{:S(2)}) copy-start(f32[3,64]{1,0:T(4,128)S(1)} %reshape.1016) | copy-start | bytes 2308
  150.8 145.3 %copy-start.8 = (bf16[2,82,1,192]{1,3,0,2:T(8,128)(2,1)}, bf16[2,82,1,192]{1,3,0,2:T(8,128)(2,1)S(1)}, u32[]{:S(2)}) copy-start(bf16[2,82,1,192]{1,3,0,2:T(8,128)(2,1)S(1)} %copy.257) | copy-start | bytes 188932
  181.5 114.0 %copy-start.70 = (bf16[2,82,3,64]{1,3,2,0:T(8,128)(2,1)}, bf16[2,82,3,64]{1,3,2,0:T(8,128)(2,1)S(1)}, u32[]{:S(2)}) copy-start(bf16[2,82,3,64]{1,3,2,0:T(8,128)(2,1)S(1)} %add_convert_fusion.7) | copy-start | bytes 188932
  181.7 114.2 %copy-start.10 = (bf16[2,82,3,64]{1,3,2,0:T(8,128)(2,1)}, bf16[2,82,3,64]{1,3,2,0:T(8,128)(2,1)S(1)}, u32[]{:S(2)}) copy-start(bf16[2,82,3,64]{1,3,2,0:T(8,128)(2,1)S(1)} %add_convert_fusion.6) | copy-start | bytes 188932
  182.1 54.0 %copy-start.139 = (s32[2,1]{0,1:T(1,128)S(1)}, s32[2,1]{0,1:T(1,128)}, u32[]{:S(2)}) copy-start(s32[2,1]{0,1:T(1,128)} %param.13) | copy-start | bytes 28
  182.1 55.3 %copy-start.25 = (bf16[2,1,82,384]{3,0,2,1:T(2,128)(2,1)S(1)}, bf16[2,1,82,384]{3,0,2,1:T(2,128)(2,1)}, u32[]{:S(2)}) copy-start(bf16[2,1,82,384]{3,0,2,1:T(2,128)(2,1)} %param.12) | copy-start | bytes 377860
  182.3 55.1 %copy-start.64 = (bf16[2,3,64,82]{3,2,1,0:T(8,128)(2,1)}, bf16[2,3,64,82]{3,2,1,0:T(8,128)(2,1)S(1)}, u32[]{:S(2)}) copy-start(bf16[2,3,64,82]{3,2,1,0:T(8,128)(2,1)S(1)} %convolution_convert_fusion.19) | copy-start | bytes 188932
  183.2 58.0 %copy-start.128 = (bf16[1,768,48]{1,2,0:T(8,128)(2,1)S(1)}, bf16[1,768,48]{1,2,0:T(8,128)(2,1)}, u32[]{:S(2)}) copy-start(bf16[1,768,48]{1,2,0:T(8,128)(2,1)} %param.17) | copy-start | bytes 221188
  183.2 102.6 %reduce-scatter.84.cloned.1.call-start = ((), (), s32[]{:S(2)}) async-start(), calls=%async_computation.26 | async-start | bytes 202752
  204.7 73.3 %copy-start.206 = (f32[768]{0:T(1024)}, f32[768]{0:T(1024)S(1)}, u32[]{:S(2)}) copy-start(f32[768]{0:T(1024)S(1)} %convert_element_type.843) | copy-start | bytes 9220
  238.6 158.9 %copy-start.55 = (bf16[1,1,82,384]{3,0,2,1:T(2,128)(2,1)}, bf16[1,1,82,384]{3,0,2,1:T(2,128)(2,1)S(1)}, u32[]{:S(2)}) copy-start(bf16[1,1,82,384]{3,0,2,1:T(2,128)(2,1)S(1)} %get-tuple-element.153) | copy-start | bytes 188932
  281.1 27.6 %reduce-scatter.86.cloned.1.call-start = ((), (), s32[]{:S(2)}) async-start(), calls=%async_computation.27 | async-start | bytes 202752
  300.0 19.9 %reduce-scatter.82.cloned.1.call-start = ((), (), s32[]{:S(2)}) async-start(), calls=%async_computation.25 | async-start | bytes 202752
  302.0 23.7 %copy-start.99 = (bf16[1,1,82,384]{3,0,2,1:T(2,128)(2,1)S(1)}, bf16[1,1,82,384]{3,0,2,1:T(2,128)(2,1)}, u32[]{:S(2)}) copy-start(bf16[1,1,82,384]{3,0,2,1:T(2,128)(2,1)} %get-tuple-element.158) | copy-start | bytes 188932
  303.1 37.7 %reduce-scatter.88.cloned.1.call-start = ((), (), s32[]{:S(2)}) async-start(), calls=%async_computation.28 | async-start | bytes 202752
  321.4 4.3 collective-permute-start
  330.4 37.5 %copy-start.14 = (bf16[2,82,3,64]{1,3,2,0:T(8,128)(2,1)}, bf16[2,82,3,64]{1,3,2,0:T(8,128)(2,1)S(1)}, u32[]{:S(2)}) copy-start(bf16[2,82,3,64]{1,3,2,0:T(8,128)(2,1)S(1)} %add_convert_fusion.4) | copy-start | bytes 188932
  330.6 37.6 %copy-start.12 = (bf16[2,82,1,192]{1,3,0,2:T(8,128)(2,1)}, bf16[2,82,1,192]{1,3,0,2:T(8,128)(2,1)S(1)}, u32[]{:S(2)}) copy-start(bf16[2,82,1,192]{1,3,0,2:T(8,128)(2,1)S(1)} %copy.273) | copy-start | bytes 188932
  332.1 25.5 %reduce-scatter.92.cloned.1.call-start = ((), (), s32[]{:S(2)}) async-start(), calls=%async_computation.30 | async-start | bytes 202752
  349.0 31.1 %reduce-scatter.94.cloned.1.call-start = ((), (), s32[]{:S(2)}) async-start(), calls=%async_computation.31 | async-start | bytes 202752
  371.4 20.0 %reduce-scatter.90.cloned.1.call-start = ((), (), s32[]{:S(2)}) async-start(), calls=%async_computation.29 | async-start | bytes 202752
  375.5 23.4 %copy-start.210 = (f32[82]{0:T(128)S(1)}, f32[82]{0:T(128)}, u32[]{:S(2)}) copy-start(f32[82]{0:T(128)} %copy-done.209) | copy-start | bytes 988
  375.6 39.5 %reduce-scatter.96.cloned.1.call-start = ((), (), s32[]{:S(2)}) async-start(), calls=%async_computation.32 | async-start | bytes 202752
  392.9 4.6 collective-permute-start.1
  406.6 27.2 %reduce-scatter.100.cloned.1.call-start = ((), (), s32[]{:S(2)}) async-start(), calls=%async_computation.34 | async-start | bytes 202752
  425.2 39.7 %reduce-scatter.102.cloned.1.call-start = ((), (), s32[]{:S(2)}) async-start(), calls=%async_computation.35 | async-start | bytes 202752
  456.3 19.8 %reduce-scatter.98.cloned.1.call-start = ((), (), s32[]{:S(2)}) async-start(), calls=%async_computation.33 | async-start | bytes 202752
  460.4 46.3 %reduce-scatter.104.cloned.1.call-start = ((), (), s32[]{:S(2)}) async-start(), calls=%async_computation.36 | async-start | bytes 202752
  477.7 4.4 collective-permute-start.2
  498.0 28.2 %reduce-scatter.108.cloned.1.call-start = ((), (), s32[]{:S(2)}) async-start(), calls=%async_computation.38 | async-start | bytes 202752
  517.6 42.0 %reduce-scatter.106.cloned.1.call-start = ((), (), s32[]{:S(2)}) async-start(), calls=%async_computation.37 | async-start | bytes 202752
  522.0 62.6 %reduce-scatter.110.cloned.1.call-start = ((), (), s32[]{:S(2)}) async-start(), calls=%async_computation.39 | async-start | bytes 202752
  537.7 81.9 %reduce-scatter.74.cloned.1.call-start = ((), (), s32[]{:S(2)}) async-start(), calls=%async_computation.21 | async-start | bytes 442368 | tf_op jit(solution)/shard_map/reduce_scatter | solution.py:290
  540.1 140.5 %reduce-scatter.72.cloned.1.call-start = ((), (), s32[]{:S(2)}) async-start(), calls=%async_computation.20 | async-start | bytes 1327104 | tf_op jit(solution)/shard_map/reduce_scatter | solution.py:289
  544.0 203.8 %reduce-scatter.76.cloned.1.call-start = ((), (), s32[]{:S(2)}) async-start(), calls=%async_computation.22 | async-start | bytes 1327104 | tf_op jit(solution)/shard_map/reduce_scatter | solution.py:291
  548.9 265.7 %reduce-scatter.78.cloned.1.call-start = ((), (), s32[]{:S(2)}) async-start(), calls=%async_computation.23 | async-start | bytes 1327104 | tf_op jit(solution)/shard_map/reduce_scatter | solution.py:292
  558.3 26.3 %copy-start.146 = (f32[82]{0:T(128)S(1)}, f32[82]{0:T(128)}, u32[]{:S(2)}) copy-start(f32[82]{0:T(128)} %copy-done.144) | copy-start | bytes 988
  558.3 26.3 %copy-start.156 = (f32[82]{0:T(128)S(1)}, f32[82]{0:T(128)}, u32[]{:S(2)}) copy-start(f32[82]{0:T(128)} %copy-done.154) | copy-start | bytes 988
  558.3 26.3 %copy-start.187 = (f32[82]{0:T(128)S(1)}, f32[82]{0:T(128)}, u32[]{:S(2)}) copy-start(f32[82]{0:T(128)} %copy-done.186) | copy-start | bytes 988
  558.4 26.3 %copy-start.191 = (f32[82]{0:T(128)S(1)}, f32[82]{0:T(128)}, u32[]{:S(2)}) copy-start(f32[82]{0:T(128)} %copy-done.190) | copy-start | bytes 988
  558.4 27.4 %copy-start.93 = (f32[1,82,384]{2,1,0:T(8,128)S(1)}, f32[1,82,384]{2,1,0:T(8,128)}, u32[]{:S(2)}) copy-start(f32[1,82,384]{2,1,0:T(8,128)} %get-tuple-element.104) | copy-start | bytes 377860
  558.4 27.4 %copy-start.217 = (f32[82]{0:T(128)S(1)}, f32[82]{0:T(128)}, u32[]{:S(2)}) copy-start(f32[82]{0:T(128)} %get-tuple-element.168) | copy-start | bytes 988
  (198 other events, 957.4 us)
Sparse Core Ops, SparseCore 0:
  183.4 6.6 reduce-scatter.79
  281.2 4.5 reduce-scatter.83
  300.1 8.5 reduce-scatter.85
  311.3 8.5 reduce-scatter.81
  332.2 8.5 reduce-scatter.87
  349.1 8.4 reduce-scatter.91
  371.5 8.4 reduce-scatter.93
  382.8 8.5 reduce-scatter.89
  406.7 8.2 reduce-scatter.95
  425.3 8.5 reduce-scatter.99
  456.4 8.4 reduce-scatter.101
  467.5 8.4 reduce-scatter.97
  498.1 8.5 reduce-scatter.103
  517.7 8.5 reduce-scatter.107
  528.3 8.5 reduce-scatter.105
  539.0 8.4 reduce-scatter.109
  551.2 62.6 reduce-scatter.73
  617.7 62.9 reduce-scatter.71
  684.6 63.1 reduce-scatter.75
  751.6 63.0 reduce-scatter.77
where the time goes:
time: 834 us; the launch traced here: 822 us
  blocking collectives  325 us (39%)
  waiting for transfers between devices  272 us (33%)
  matrix products  69 us (8%)
  other arithmetic  66.9 us (8%)
  local copies, waits for them, and re-layouts  57.1 us (7%)
  between operations  25.4 us (3%)
    unnamed x36, waiting for transfers between devices  74.1 us
    unnamed x3, blocking collectives  72.4 us
    reduce_scatter x1, waiting for transfers between devices, per_device(): lax.psum_scatter(totals[2], 'fsdp', scatter_dimension=0, tiled=True)  67.2 us
    reduce_scatter x1, waiting for transfers between devices, per_device(): lax.psum_scatter(totals[3], 'fsdp', scatter_dimension=1, tiled=True)  66.9 us
    reduce_scatter x1, waiting for transfers between devices, per_device(): lax.psum_scatter(totals[0], 'fsdp', scatter_dimension=0, tiled=True)  61 us
    all_gather x1, blocking collectives, per_device(): lax.all_gather(shifts[0], ('tensor', 'fsdp'), axis=1, tiled=True)  35.5 us
    all_gather x1, blocking collectives, per_device(): lax.all_gather(w_down[0], 'fsdp', axis=1, tiled=True)  31.6 us
    all_gather x1, blocking collectives, per_device(): lax.all_gather(w_qkv[0], 'fsdp', axis=0, tiled=True)  31.6 us
  transfers between devices with their start and end apart: 23, of which 18 were waited for; matrix products, arithmetic and copies ran while one was open for 8% of the time, Pallas kernels for 0%

commit v1 on v0

v1 whole, which is shorter than its diff:
```python
import functools
import math

import jax
import jax.numpy as jnp
from jax import lax
from jax.experimental import pallas as pl
from jax.experimental.pallas import tpu as pltpu
from jax.sharding import PartitionSpec as P

HD = 64
EPS = 1e-06
INV_ROOT_TWO = 0.7071067811865476
INV_ROOT_TWO_PI = 0.3989422804014327
SCALE = 1.0 / math.sqrt(HD)
BF = jnp.bfloat16
F32 = jnp.float32
GRID_RING = (0, 1, 3, 5, 7, 6, 4, 2)
ROW_STEP = 88
EXT = 128


def dot(a, b, dims):
    return lax.dot_general(a, b, (dims, ((), ())), preferred_element_type=F32)


def nn(a, b):
    return dot(a, b, ((1,), (0,)))


def nt(a, b):
    return dot(a, b, ((1,), (1,)))


def tn(a, b):
    return dot(a, b, ((0,), (0,)))


def norm(value):
    mean = jnp.mean(value, axis=-1, keepdims=True)
    centred = value - mean
    var = jnp.mean(centred * centred, axis=-1, keepdims=True)
    factor = lax.rsqrt(var + EPS)
    return centred * factor, factor


def norm_back(grad, unit, factor, gain):
    scaled = grad * gain
    plain = jnp.mean(scaled, axis=-1, keepdims=True)
    along = jnp.mean(scaled * unit, axis=-1, keepdims=True)
    return (scaled - plain - unit * along) * factor


class Dims:
    def __init__(self, seq, width, hidden, shards):
        self.seq, self.width, self.hidden, self.shards = seq, width, hidden, shards
        self.half = width // 2
        self.fh = hidden // 2
        self.heads = self.half // HD
        self.o_out = 3 * self.half
        self.o_up = self.o_out + self.half
        self.o_down = self.o_up + self.fh
        self.cols = self.o_down + self.fh
        self.packed = self.cols + EXT
        self.rows = 2 * ROW_STEP
        self.groups = width // 128

    def state_shapes(self):
        r, w = self.rows, self.width
        return dict(
            unit_one=((r, w), F32),
            factors=((2, r, 1), F32),
            first=((r, w), BF),
            proj=((2, r, 3 * self.half), F32),
            probs=((4 * self.heads, ROW_STEP, ROW_STEP), F32),
            mixed=((2, r, self.half), F32),
            unit_two=((r, w), F32),
            second=((r, w), BF),
            slope=((2, r, self.fh), F32),
            active=((2, r, self.fh), BF),
        )


def layer_forward(dm, state, w, vecs, st):
    half, fh = dm.half, dm.fh
    unit, factor = norm(state)
    st["unit_one"][...] = unit
    st["factors"][0] = factor
    first = (unit * vecs[0:1, :] + vecs[2:3, :]).astype(BF)
    st["first"][...] = first
    attn = None
    for t in range(2):
        proj = nn(first, w[t, :, 0 : 3 * half])
        query = proj[:, 0:half] + vecs[6:7, t * half : (t + 1) * half]
        keys = proj[:, half : 2 * half]
        values = proj[:, 2 * half :] + vecs[7:8, t * half : (t + 1) * half]
        st["proj"][t, :, 0:half] = query
        st["proj"][t, :, half : 2 * half] = keys
        st["proj"][t, :, 2 * half :] = values
        column = lax.broadcasted_iota(jnp.int32, (ROW_STEP, ROW_STEP), 1)
        for m in range(2):
            rows = slice(m * ROW_STEP, (m + 1) * ROW_STEP)
            for h in range(dm.heads):
                cols = slice(h * HD, (h + 1) * HD)
                scores = nt(query[rows, cols].astype(BF), keys[rows, cols].astype(BF)) * SCALE
                scores = jnp.where(column < dm.seq, scores, -1e30)
                top = jnp.max(scores, axis=-1, keepdims=True)
                expo = jnp.exp(scores - top)
                probs = expo / jnp.sum(expo, axis=-1, keepdims=True)
                st["probs"][(t * 2 + m) * dm.heads + h] = probs
                st["mixed"][t, rows, cols] = nn(probs.astype(BF), values[rows, cols].astype(BF))
        part = nt(st["mixed"][t].astype(BF), w[t, :, dm.o_out : dm.o_out + half])
        attn = part if attn is None else attn + part
    resid = state + attn + vecs[3:4, :]
    unit, factor = norm(resid)
    st["unit_two"][...] = unit
    st["factors"][1] = factor
    second = (unit * vecs[1:2, :] + vecs[4:5, :]).astype(BF)
    st["second"][...] = second
    output = resid + vecs[5:6, :]
    per = fh // dm.width
    for t in range(2):
        bias = jnp.concatenate([vecs[8 + t * per + j : 9 + t * per + j, :] for j in range(per)], axis=1)
        hidden = nn(second, w[t, :, dm.o_up : dm.o_up + fh]) + bias
        curve = 0.5 * (1.0 + lax.erf(hidden * INV_ROOT_TWO))
        st["slope"][t] = curve + hidden * jnp.exp(-0.5 * hidden * hidden) * INV_ROOT_TWO_PI
        active = (hidden * curve).astype(BF)
        st["active"][t] = active
        output += nt(active, w[t, :, dm.o_down : dm.o_down + fh])
    return output


def total_rows(value):
    return jnp.sum(value, axis=0, keepdims=True)


def layer_backward(dm, grad, w, vecs, st, grads, gproj, tensor):
    half, fh = dm.half, dm.fh
    low = grad.astype(BF)
    shift_branch = total_rows(low.astype(F32))
    second = st["second"][...]
    up_bias = []
    grad_second = None
    for t in range(2):
        grads[t][:, dm.o_down : dm.o_down + fh] = tn(low, st["active"][t]).astype(BF)
        raw = nn(low, w[t, :, dm.o_down : dm.o_down + fh]) * st["slope"][t]
        up_bias.append(total_rows(raw))
        grad_hidden = raw.astype(BF)
        grads[t][:, dm.o_up : dm.o_up + fh] = tn(second, grad_hidden).astype(BF)
        part = nt(grad_hidden, w[t, :, dm.o_up : dm.o_up + fh])
        grad_second = part if grad_second is None else grad_second + part
    unit = st["unit_two"][...]
    gain_two, shift_two = total_rows(grad_second * unit), total_rows(grad_second)
    grad_resid = grad + norm_back(grad_second, unit, st["factors"][1], vecs[1:2, :])
    low = grad_resid.astype(BF)
    shift_attn = total_rows(low.astype(F32))
    first = st["first"][...]
    bias_query, bias_values = [], []
    grad_first = None
    for t in range(2):
        grads[t][:, dm.o_out : dm.o_out + half] = tn(low, st["mixed"][t].astype(BF)).astype(BF)
        grad_mixed = nn(low, w[t, :, dm.o_out : dm.o_out + half])
        for m in range(2):
            rows = slice(m * ROW_STEP, (m + 1) * ROW_STEP)
            for h in range(dm.heads):
                cols = slice(h * HD, (h + 1) * HD)
                query = st["proj"][t, rows, h * HD : (h + 1) * HD].astype(BF)
                keys = st["proj"][t, rows, half + h * HD : half + (h + 1) * HD].astype(BF)
                values = st["proj"][t, rows, 2 * half + h * HD : 2 * half + (h + 1) * HD].astype(BF)
                probs = st["probs"][(t * 2 + m) * dm.heads + h]
                gm = grad_mixed[rows, cols].astype(BF)
                gproj[rows, 2 * half + h * HD : 2 * half + (h + 1) * HD] = tn(probs.astype(BF), gm)
                gp = nt(gm, values)
                inner = jnp.sum(gp * probs, axis=-1, keepdims=True)
                gs = (probs * (gp - inner)).astype(BF)
                gproj[rows, h * HD : (h + 1) * HD] = nn(gs, keys) * SCALE
                gproj[rows, half + h * HD : half + (h + 1) * HD] = tn(gs, query) * SCALE
        bias_query.append(total_rows(gproj[:, 0:half]))
        bias_values.append(total_rows(gproj[:, 2 * half :]))
        grad_proj = gproj[...].astype(BF)
        grads[t][:, 0 : 3 * half] = tn(first, grad_proj).astype(BF)
        part = nt(grad_proj, w[t, :, 0 : 3 * half])
        grad_first = part if grad_first is None else grad_first + part
    unit = st["unit_one"][...]
    gain_one, shift_one = total_rows(grad_first * unit), total_rows(grad_first)
    grad_state = grad_resid + norm_back(grad_first, unit, st["factors"][0], vecs[0:1, :])
    own_first = tensor == 0

    def by_half(vec):
        low_half, high_half = vec[:, 0:half], vec[:, half:]
        return jnp.where(own_first, low_half, high_half), jnp.where(own_first, high_half, low_half)

    plain = [by_half(v) for v in (gain_one, gain_two, shift_one, shift_attn, shift_two, shift_branch)]
    share, up_share = half // dm.shards, fh // dm.shards
    block = dm.width // dm.shards
    for t in range(2):
        rows = [v[t] for v in plain] + [bias_query[t], bias_values[t]]
        stack = jnp.concatenate(rows, axis=0)
        for f in range(dm.shards):
            grads[t][f * block : (f + 1) * block, dm.cols :] = jnp.zeros((block, EXT), BF)
            piece = jnp.concatenate([stack[:, f * share : (f + 1) * share], jnp.zeros((8, EXT - share), F32)], axis=1)
            up_piece = up_bias[t][:, f * up_share : (f + 1) * up_share]
            up_piece = jnp.concatenate([up_piece, jnp.zeros((1, EXT - up_share), F32)], axis=1)
            piece = jnp.concatenate([piece, up_piece, jnp.zeros((7, EXT), F32)], axis=0)
            grads[t][f * block : f * block + 16, dm.cols :] = piece.astype(BF)
    return grad_state


def spread(dm, ref, get):
    pad = jnp.zeros((ROW_STEP - dm.seq, dm.width), F32)
    for m in range(2):
        ref[m * ROW_STEP : m * ROW_STEP + dm.seq, :] = get(m)
        ref[m * ROW_STEP + dm.seq : (m + 1) * ROW_STEP, :] = pad


def image(dm, value, m):
    return value[m * ROW_STEP : m * ROW_STEP + dm.seq, :]


def kernel_first(dm, count, order, tokens, *refs):
    pieces, refs = refs[: 2 * count], refs[2 * count :]
    w, vecs, out = refs[0:3]
    names = list(dm.state_shapes())
    st = dict(zip(names, refs[3 : 3 + len(names)]))
    rows = refs[3 + len(names)]
    block = dm.width // dm.shards
    ext = jnp.zeros((block, EXT), F32)
    for t in range(2):
        for i in range(count):
            ref = pieces[t * count + i]
            place = pl.ds(pl.multiple_of(order[i] * block, 16), block)
            w[t, place, :] = ref[:, 0 : dm.cols]
            ext += ref[:, dm.cols :].astype(F32)
    g = dm.groups
    for v in range(6):
        vecs[v : v + 1, :] = jnp.concatenate([ext[v * g + j : v * g + j + 1, :] for j in range(g)], axis=1)
    own_first = lax.axis_index("tensor") == 0
    for v in (6, 7):
        row = jnp.concatenate([ext[v * g + j : v * g + j + 1, :] for j in range(g)], axis=1)
        turned = jnp.concatenate([row[:, dm.half :], row[:, 0 : dm.half]], axis=1)
        vecs[v : v + 1, :] = jnp.where(own_first, row, turned)
    per = dm.hidden // dm.width
    up = [
        jnp.concatenate([ext[(8 + v) * g + j : (8 + v) * g + j + 1, :] for j in range(g)], axis=1)
        for v in range(per)
    ]
    for v in range(per):
        vecs[8 + v : 9 + v, :] = jnp.where(own_first, up[v], up[(v + per // 2) % per])
    spread(dm, rows, lambda m: tokens[m, 0].astype(F32))
    output = layer_forward(dm, rows[...], w, vecs, st)
    for m in range(2):
        out[m, 0] = image(dm, output, m).astype(BF)


def live_of(count_ref, m):
    return (lax.axis_index("tensor") < count_ref[m, 0]).astype(F32)


def kernel_second(dm, count_ref, h0, h1, out_grad, w, vecs, acts, grad_in, grad_own, grad_other, *scratch):
    names = list(dm.state_shapes())
    st = dict(zip(names, scratch[: len(names)]))
    rows, gproj = scratch[len(names) :]
    section = lax.axis_index("section")

    @pl.when(section == 0)
    def _():
        for m in range(2):
            acts[m, 0] = (h0[m, 0].astype(F32) * live_of(count_ref, m)).astype(BF)

    @pl.when(section != 0)
    def _():
        spread(dm, rows, lambda m: h1[m, 0].astype(F32))
        output = layer_forward(dm, rows[...], w, vecs, st)
        for m in range(2):
            acts[m, 0] = (image(dm, output, m) * live_of(count_ref, m)).astype(BF)
        spread(dm, rows, lambda m: out_grad[m, 0].astype(F32) * live_of(count_ref, m))
        grad = layer_backward(
            dm, rows[...], w, vecs, st, (grad_own, grad_other), gproj, lax.axis_index("tensor")
        )
        for m in range(2):
            grad_in[m, 0] = image(dm, grad, m).astype(BF)


def kernel_third(dm, incoming, w, vecs, own, given_own, given_other, *refs):
    names = list(dm.state_shapes())
    st = dict(zip(names, refs[: len(names)]))
    grad_in, grad_own, grad_other, rows, gproj = refs[len(names) :]

    @pl.when(lax.axis_index("section") == 0)
    def _():
        spread(dm, rows, lambda m: incoming[m, 0].astype(F32))
        grad = layer_backward(
            dm, rows[...], w, vecs, st, (grad_own, grad_other), gproj, lax.axis_index("tensor")
        )
        for m in range(2):
            grad_in[m, 0] = image(dm, grad, m).astype(BF)

    @pl.when(lax.axis_index("section") != 0)
    def _():
        grad_in[...] = own[...]
        grad_own[...] = given_own[...]
        grad_other[...] = given_other[...]


def kernel_pack(dm, w_qkv, w_out, w_up, w_down, head_bias, up_bias, gains, shifts, packed):
    half, fh = dm.half, dm.fh
    block = dm.width // dm.shards
    for k in range(3):
        packed[:, k * half : (k + 1) * half] = w_qkv[0, :, k, :]
    row = lax.broadcasted_iota(jnp.int32, (block, block), 0)
    column = lax.broadcasted_iota(jnp.int32, (block, block), 1)
    eye = (row == column).astype(BF)
    packed[:, dm.o_out : dm.o_out + half] = nt(eye, w_out[0]).astype(BF)
    packed[:, dm.o_up : dm.o_up + fh] = w_up[0]
    packed[:, dm.o_down : dm.o_down + fh] = nt(eye, w_down[0]).astype(BF)
    place = lax.axis_index("tensor") * dm.shards + lax.axis_index("fsdp")

    def placed(values, total):
        share = values.shape[1]
        row = lax.broadcasted_iota(jnp.int32, (share, total), 0)
        column = lax.broadcasted_iota(jnp.int32, (share, total), 1)
        return nn(values, (column == row + place * share).astype(BF))

    small = jnp.concatenate([gains[0], shifts[0], head_bias[0]], axis=0)
    small = placed(small, dm.width)
    up = placed(up_bias[...], dm.hidden)
    rows = []
    for v in range(8):
        rows += [small[v : v + 1, j * 128 : (j + 1) * 128] for j in range(dm.groups)]
    rows += [up[:, j * 128 : (j + 1) * 128] for j in range(dm.hidden // 128)]
    rows.append(jnp.zeros((block - len(rows), EXT), F32))
    packed[:, dm.cols :] = jnp.concatenate(rows, axis=0).astype(BF)


def kernel_unpack(dm, mine, left, right, g_qkv, g_out, g_up, g_down, g_head, g_upb, g_gain, g_shift, scratch):
    half, fh = dm.half, dm.fh
    block = dm.width // dm.shards
    value = mine[...].astype(F32) + left[...].astype(F32) + right[...].astype(F32)
    for k in range(3):
        g_qkv[0, :, k, :] = value[:, k * half : (k + 1) * half]
    g_up[0] = value[:, dm.o_up : dm.o_up + fh]
    scratch[...] = jnp.zeros_like(scratch)
    scratch[0:block, 0:half] = value[:, dm.o_out : dm.o_out + half]
    scratch[0:block, 2 * 128 : 2 * 128 + fh] = value[:, dm.o_down : dm.o_down + fh]
    turned = scratch[...].T
    g_out[0] = turned[0:half, 0:block]
    g_down[0] = turned[256 : 256 + fh, 0:block]
    ext = value[0:16, dm.cols :]
    share, up_share = half // dm.shards, fh // dm.shards
    g_gain[0] = ext[0:2, 0:share]
    g_shift[0] = ext[2:6, 0:share]
    g_head[0] = ext[6:8, 0:share]
    g_upb[...] = ext[8:9, 0:up_share]


VM = pl.BlockSpec(memory_space=pltpu.VMEM)
SM = pl.BlockSpec(memory_space=pltpu.SMEM)


def call(kernel, ins, outs, args, scratch=(), limit=48):
    return pl.pallas_call(
        kernel,
        in_specs=ins,
        out_specs=[VM] * len(outs),
        out_shape=[jax.ShapeDtypeStruct(s, d) for s, d in outs],
        scratch_shapes=list(scratch),
        compiler_params=pltpu.CompilerParams(vmem_limit_bytes=limit * 2**20),
    )(*args)


def shifted(value, cycle, step):
    count = len(cycle)
    return lax.ppermute(value, "fsdp", [(cycle[i], cycle[(i + step) % count]) for i in range(count)])


def gather_ring(block, cycle):
    count = len(cycle)
    ahead = behind = block
    found = [block]
    offsets = [0]
    for step in range(1, count // 2 + 1):
        if step < count - step:
            ahead, behind = shifted(ahead, cycle, 1), shifted(behind, cycle, -1)
            found += [ahead, behind]
            offsets += [-step, step]
        else:
            cut = block.shape[1] // 256 * 128
            low, high = shifted(ahead[:, :cut], cycle, 1), shifted(behind[:, cut:], cycle, -1)
            found.append(jnp.concatenate([low, high], axis=1))
            offsets.append(step)
    return found, offsets


def reduce_ring(parts, place, cycle):
    count = len(cycle)
    table = jnp.array(cycle, jnp.int32)
    cut = parts.shape[2] // 256 * 128

    def part(offset, lo, hi):
        dest = table[lax.rem(place + offset + count, count)]
        return lax.dynamic_index_in_dim(parts, dest, 0, keepdims=False)[:, lo:hi]

    def add(a, b):
        return (a.astype(F32) + b.astype(F32)).astype(BF)

    far = count // 2
    low = shifted(part(far, 0, cut), cycle, 1)
    high = shifted(part(-far, cut, None), cycle, -1)
    for step in range(far - 1, 0, -1):
        ahead, behind = part(step, 0, None), part(-step, 0, None)
        if step == far - 1:
            ahead = jnp.concatenate([add(ahead[:, :cut], low), ahead[:, cut:]], axis=1)
            behind = jnp.concatenate([behind[:, :cut], add(behind[:, cut:], high)], axis=1)
        else:
            ahead, behind = add(ahead, left), add(behind, right)
        left, right = shifted(ahead, cycle, 1), shifted(behind, cycle, -1)
    return part(0, 0, None), left, right


def per_device(tokens, out_grad, image_count, w_qkv, w_out, w_up, w_down, head_bias, up_bias, gains, shifts):
    seq, width = tokens.shape[2:]
    shards = lax.axis_size("fsdp")
    ring = shards == len(GRID_RING)
    hidden = w_up.shape[2] * 2
    dm = Dims(seq, width, hidden, len(GRID_RING))
    block = width // dm.shards
    swap = [(0, 1), (1, 0)]
    vectors = (head_bias, up_bias, gains, shifts)
    if ring:
        packed = call(
            functools.partial(kernel_pack, dm),
            [VM] * 8,
            [((block, dm.packed), BF)],
            (w_qkv, w_out, w_up, w_down) + vectors,
        )[0]
        found, offsets = gather_ring(packed, GRID_RING)
        table = jnp.array(GRID_RING, jnp.int32)
        inverse = [GRID_RING.index(i) for i in range(len(GRID_RING))]
        place = jnp.array(inverse, jnp.int32)[lax.axis_index("fsdp")]
        order = table[lax.rem(place + jnp.array(offsets, jnp.int32) + dm.shards, dm.shards)]
    else:
        rows = jnp.concatenate(
            [
                w_qkv[0].reshape(w_qkv.shape[1], -1),
                w_out[0].T,
                w_up[0],
                w_down[0].T,
            ],
            axis=1,
        )
        rows = lax.all_gather(rows, "fsdp", axis=0, tiled=True)
        whole = [
            lax.all_gather(v[0], ("tensor", "fsdp"), axis=v.ndim - 2, tiled=True).reshape(-1, 128)
            for v in (gains, shifts, head_bias, up_bias)
        ]
        ext = jnp.concatenate(whole, axis=0)
        ext = jnp.pad(ext, ((0, block - ext.shape[0]), (0, 0)))
        ext = jnp.where(lax.axis_index("tensor") == 0, ext, jnp.zeros_like(ext))
        ext = jnp.pad(ext, ((0, width - block), (0, 0)))
        rows = jnp.concatenate([rows, ext], axis=1)
        found = [rows[i * block : (i + 1) * block] for i in range(dm.shards)]
        order = jnp.arange(dm.shards, dtype=jnp.int32)
    others = [lax.ppermute(b, "tensor", swap) for b in found]
    states = list(dm.state_shapes().values())
    shape = tokens.shape
    scratch_rows = pltpu.VMEM((dm.rows, width), F32)
    scratch_proj = pltpu.VMEM((dm.rows, 3 * dm.half), F32)
    w, vecs, low0, *state = call(
        functools.partial(kernel_first, dm, len(found)),
        [SM] + [VM] * (1 + 2 * len(found)),
        [((2, width, dm.cols), BF), ((16, width), F32), (shape, BF)] + states,
        (order, tokens) + tuple(found) + tuple(others),
        scratch=[scratch_rows],
    )
    h1 = lax.ppermute(low0, "section", [(0, 1)])
    packed_grads = [((width, dm.packed), BF)] * 2
    acts, grad1, own, other = call(
        functools.partial(kernel_second, dm),
        [SM] + [VM] * 5,
        [(shape, BF), (shape, BF)] + packed_grads,
        (image_count, low0, h1, out_grad, w, vecs),
        scratch=[pltpu.VMEM(s, d) for s, d in states] + [scratch_rows, scratch_proj],
    )
    incoming = lax.ppermute(grad1, "section", [(1, 0)])
    in_grads, own, other = call(
        functools.partial(kernel_third, dm),
        [VM] * (6 + len(states)),
        [(shape, BF)] + packed_grads,
        (incoming, w, vecs, grad1, own, other) + tuple(state),
        scratch=[scratch_rows, scratch_proj],
    )
    mine = own.astype(F32) + lax.ppermute(other, "tensor", swap).astype(F32)
    if ring:
        parts = mine.astype(BF).reshape(dm.shards, block, dm.packed)
        terms = reduce_ring(parts, place, GRID_RING)
        grads = call(
            functools.partial(kernel_unpack, dm),
            [VM] * 3,
            [(v.shape, F32) for v in (w_qkv, w_out, w_up, w_down) + vectors],
            terms,
            scratch=[pltpu.VMEM((128, 256 + dm.fh), F32)],
        )
    else:
        half = dm.half
        body = lax.psum_scatter(mine[:, : dm.cols], "fsdp", scatter_dimension=0, tiled=True)
        share, up_share = half // dm.shards, dm.fh // dm.shards
        ext = mine[:, dm.cols :].reshape(dm.shards, block, EXT)
        small = jnp.moveaxis(ext[:, 0:8, 0:share], 0, 1).reshape(8, half)
        small = lax.psum_scatter(small, "fsdp", scatter_dimension=1, tiled=True)
        up = lax.psum_scatter(ext[:, 8, 0:up_share].reshape(-1), "fsdp", scatter_dimension=0, tiled=True)
        grads = [
            body[:, : 3 * half].reshape(w_qkv.shape),
            body[:, dm.o_out : dm.o_up].T[None],
            body[:, dm.o_up : dm.o_down][None],
            body[:, dm.o_down :].T[None],
            small[6:8][None],
            up[None],
            small[0:2][None],
            small[2:6][None],
        ]
    return (acts[None], in_grads[None], *grads)


def solution(mesh):
    both = ("tensor", "fsdp")
    params = (
        P("section", "fsdp", None, "tensor"),
        P("section", "tensor", "fsdp"),
        P("section", "fsdp", "tensor"),
        P("section", "tensor", "fsdp"),
        P("section", None, both),
        P("section", both),
        P("section", None, both),
        P("section", None, both),
    )
    images = P(None, ("fsdp", "tensor"), None, None)
    layered = P("section", None, ("fsdp", "tensor"), None, None)
    return jax.shard_map(
        per_device,
        mesh=mesh,
        in_specs=(images, images, P(None, "fsdp")) + params,
        out_specs=(layered, layered) + params,
        check_vma=False,
    )
```

time: 834 us -> 162 us (0.19); the launches traced: 822 us -> 161 us
  blocking collectives: 325 us -> 0 us
  waiting for transfers between devices: 272 us -> 55.9 us
  matrix products: 69 us -> 0 us
  other arithmetic: 66.9 us -> 3.51 us
  local copies, waits for them, and re-layouts: 57.1 us -> 27.7 us
  Pallas kernels: 0 us -> 24.1 us
  starting transfers between devices: 6.44 us -> 25.9 us
    all_gather x23 -> x0, blocking collectives: 253 us -> none  [the longest x1 35.5 us: per_device(): lax.all_gather(shifts[0], ('tensor', 'fsdp'), axis=1, tiled=True)]
    reduce_scatter x4 -> x0, waiting for transfers between devices: 195 us -> none  [the longest x1 67.2 us: per_device(): lax.psum_scatter(totals[2], 'fsdp', scatter_dimension=0, tiled=True)]
    unnamed x36 -> x0, waiting for transfers between devices: 74.1 us -> none
    unnamed x3 -> x0, blocking collectives: 72.4 us -> none
    dot_general x74 -> x0, matrix products: 69 us -> none  [the longest x4 6.92 us: backward(): jnp.einsum('gske,dke->gsd', piece, w_qkv, preferred_element_type=jnp.floa...]
    ppermute x3 -> x27, waiting for transfers between devices: 2.65 us -> 55.9 us  [the longest x16 35.9 us: shifted(): lax.ppermute(value, 'fsdp', [(cycle[i], cycle[(i + step) % count]) for i...]
    reduce_sum x33 -> x0, other arithmetic: 34.1 us -> none  [the longest x4 9.11 us: backward(): shift_attn = jnp.sum(attn_low.astype(jnp.float32), axis=(0, 1))]
    pallas_call x0 -> x5, Pallas kernels: none -> 24.1 us  [call(): pl.pallas_call(kernel, in_specs=ins, out_specs=[VM] * len(outs), out_shap...]
  transfers between devices with their start and end apart: 23 -> 27, of which waited for: 18 -> 12; matrix products, arithmetic and copies ran while one was open for 8% -> 4% of each run, Pallas kernels for 0% -> 0%
where the time goes in v1:
time: 162 us; the launch traced here: 161 us
  waiting for transfers between devices  55.9 us (35%)
  local copies, waits for them, and re-layouts  27.7 us (17%)
  starting transfers between devices  25.9 us (16%)
  between operations  24.4 us (15%)
  Pallas kernels  24.1 us (15%)
  other arithmetic  3.51 us (2%)
    ppermute x16, waiting for transfers between devices, shifted(): lax.ppermute(value, 'fsdp', [(cycle[i], cycle[(i + step) % count]) for i...  35.9 us
    unnamed x74, local copies, waits for them, and re-layouts  25 us
    pallas_call x5, Pallas kernels, call(): pl.pallas_call(kernel, in_specs=ins, out_specs=[VM] * len(outs), out_shap...  24.1 us
    ppermute x16, starting transfers between devices, shifted(): lax.ppermute(value, 'fsdp', [(cycle[i], cycle[(i + step) % count]) for i...  19.1 us
    ppermute x1, waiting for transfers between devices, per_device(): incoming = lax.ppermute(grad1, 'section', [(1, 0)])  17.6 us
    ppermute x1, starting transfers between devices, per_device(): h1 = lax.ppermute(low0, 'section', [(0, 1)])  3.39 us
  transfers between devices with their start and end apart: 27, of which 12 were waited for; matrix products, arithmetic and copies ran while one was open for 4% of the time, Pallas kernels for 0%

profile of v1, /device:TPU:0, one launch (start us, length us, event | category | flops | bytes accessed | tf_op | source)
XLA Modules:
  0.0 161.5 jit_solution(451445092209881122)
XLA Ops:
  0.7 0.9 copy.36.w_qkv
  1.6 0.8 copy.37.w_out
  2.5 1.1 copy.38.w_down
  3.5 0.9 copy-done.23
  7.4 3.0 %collective-permute-start = (bf16[48,2432]{1,0:T(8,128)(2,1)S(1)}, bf16[48,2432]{1,0:T(8,128)(2,1)S(1)}, u32[]{:S(2)}, u32[]{:S(2)}) collective-permute-start(bf16[48,2432]{1,0:T(8,128)(2,1)S(1)} %shard_map.222.refs_0_), channel_id=1, source_target_pairs={{0,1},{1,3},{3,5},{5,7},{7,6},{6,4},{4,2},{2,0},{8,9},{9,11},{11,1... | collective-permute-start | bytes 700424 | tf_op jit(solution)/shard_map/ppermute | solution.py:373
  10.5 5.6 %collective-permute-done.refs_1_ = bf16[48,2432]{1,0:T(8,128)(2,1)S(1)} collective-permute-done((bf16[48,2432]{1,0:T(8,128)(2,1)S(1)}, bf16[48,2432]{1,0:T(8,128)(2,1)S(1)}, u32[]{:S(2)}, u32[]{:S(2)}) %collective-permute-start) | collective-permute-done | bytes 233504 | tf_op jit(solution)/shard_map/ppermute | solution.py:373
  16.1 1.7 %collective-permute-start.2 = (bf16[48,2432]{1,0:T(8,128)(2,1)S(1)}, bf16[48,2432]{1,0:T(8,128)(2,1)S(1)}, u32[]{:S(2)}, u32[]{:S(2)}) collective-permute-start(bf16[48,2432]{1,0:T(8,128)(2,1)S(1)} %collective-permute-done.refs_1_), channel_id=1, source_target_pairs={{0,1},{1,3},{3,5},{5,7},{7,6},{6,4},{4,2},{2,0},{8,9},{9,11},{11,1... | collective-permute-start | bytes 700424 | tf_op jit(solution)/shard_map/ppermute | solution.py:373
  18.2 4.8 %collective-permute-done.2.refs_3_ = bf16[48,2432]{1,0:T(8,128)(2,1)S(1)} collective-permute-done((bf16[48,2432]{1,0:T(8,128)(2,1)S(1)}, bf16[48,2432]{1,0:T(8,128)(2,1)S(1)}, u32[]{:S(2)}, u32[]{:S(2)}) %collective-permute-start.2) | collective-permute-done | bytes 233504 | tf_op jit(solution)/shard_map/ppermute | solution.py:373
  23.0 1.4 collective-permute-start.4
  25.0 4.1 %collective-permute-done.4.refs_5_ = bf16[48,2432]{1,0:T(8,128)(2,1)S(1)} collective-permute-done((bf16[48,2432]{1,0:T(8,128)(2,1)S(1)}, bf16[48,2432]{1,0:T(8,128)(2,1)S(1)}, u32[]{:S(2)}, u32[]{:S(2)}) %collective-permute-start.4) | collective-permute-done | bytes 233504 | tf_op jit(solution)/shard_map/ppermute | solution.py:373
  29.2 1.7 %collective-permute-start.6 = (bf16[48,1152]{1,0:T(8,128)(2,1)S(1)}, bf16[48,1152]{1,0:T(8,128)(2,1)S(1)}, u32[]{:S(2)}, u32[]{:S(2)}) collective-permute-start(bf16[48,1152]{1,0:T(8,128)(2,1)S(1)} %slice.34), channel_id=1, source_target_pairs={{0,1},{1,3},{3,5},{5,7},{7,6},{6,4},{4,2},{2,0},{8,9},{9,11},{11,1... | collective-permute-start | bytes 331784 | tf_op jit(solution)/shard_map/ppermute | solution.py:373
  30.9 0.9 copy.39.tokens
  31.8 1.2 dynamic_slice.58
  34.1 1.6 collective-permute-start.7
  35.7 3.7 %collective-permute-done.7 = bf16[48,1280]{1,0:T(8,128)(2,1)S(1)} collective-permute-done((bf16[48,1280]{1,0:T(8,128)(2,1)S(1)}, bf16[48,1280]{1,0:T(8,128)(2,1)S(1)}, u32[]{:S(2)}, u32[]{:S(2)}) %collective-permute-start.7) | collective-permute-done | bytes 122912 | tf_op jit(solution)/shard_map/ppermute | solution.py:373
  43.3 0.7 copy-done.13
  44.7 0.9 copy-done.6
  45.6 0.9 copy-done.8
  46.6 0.9 copy-done.10
  47.5 0.9 copy-done.12
  48.5 0.9 copy-done.14
  49.4 0.9 copy-done.16
  50.3 8.4 %shard_map.223 = (bf16[2,384,2304]{2,1,0:T(8,128)(2,1)}, f32[16,384]{1,0:T(8,128)S(1)}, bf16[2,1,82,384]{3,2,1,0:T(8,128)(2,1)}, f32[176,384]{1,0:T(8,128)S(1)},...) custom-call(s32[8]{0:T(128)S(1)} %gather_fusion, ...), custom_call_target="tpu_custom_call" | custom-call | tf_op jit(solution)/shard_map/pallas_call | solution.py:361
  60.8 3.4 %collective-permute-start.16 = (bf16[2,1,82,384]{3,2,1,0:T(8,128)(2,1)}, bf16[2,1,82,384]{3,2,1,0:T(8,128)(2,1)S(1)}, u32[]{:S(2)}, u32[]{:S(2)}) collective-permute-start(bf16[2,1,82,384]{3,2,1,0:T(8,128)(2,1)} %get-tuple-element.38.h0), channel_id=1, source_target_pairs={{0,16},{1,17},{2,18},{3,19},{4,20},{5,21},{6,22},{7,23},{8,24},{9,... | collective-permute-start | bytes 377864 | tf_op jit(solution)/shard_map/ppermute | solution.py:475
  64.3 0.9 copy.41.out_grad
  65.2 2.4 %collective-permute-done.16.h1 = bf16[2,1,82,384]{3,2,1,0:T(8,128)(2,1)S(1)} collective-permute-done((bf16[2,1,82,384]{3,2,1,0:T(8,128)(2,1)}, bf16[2,1,82,384]{3,2,1,0:T(8,128)(2,1)S(1)}, u32[]{:S(2)}, u32[]{:S(2)}) %collective-permute-start.16) | collective-permute-done | bytes 125984 | tf_op jit(solution)/shard_map/ppermute | solution.py:475
  67.6 2.5 %shard_map.224 = (bf16[2,1,82,384]{3,2,1,0:T(8,128)(2,1)S(1)}, bf16[2,1,82,384]{3,2,1,0:T(8,128)(2,1)S(1)}, bf16[384,2432]{1,0:T(8,128)(2,1)S(1)}, bf16[384,2432]{1,0:T(8,128)(2,1)S(1)}) custom-call(s32[2,1]{1,0:T(2,128)S(1)} %copy.40.count_ref, bf16[2,1,82,384]{3,2,1,0:T(8,128)(2,1)} %get-tuple-element.38.h0, ...), custom_call_target="tpu_custom_call" | custom-call | tf_op jit(solution)/shard_map/pallas_call | solution.py:361
  70.1 1.3 copy-done
  71.3 1.3 copy-done.1
  72.6 1.3 collective-permute-start.17
  73.9 17.6 %collective-permute-done.17.incoming = bf16[2,1,82,384]{3,2,1,0:T(8,128)(2,1)S(1)} collective-permute-done((bf16[2,1,82,384]{3,2,1,0:T(8,128)(2,1)S(1)}, bf16[2,1,82,384]{3,2,1,0:T(8,128)(2,1)S(1)}, u32[]{:S(2)}, u32[]{:S(2)}) %collective-permute-start.17) | collective-permute-done | bytes 125984 | tf_op jit(solution)/shard_map/ppermute | solution.py:484
  91.5 12.0 %shard_map.225 = (bf16[2,1,82,384]{3,2,1,0:T(8,128)(2,1)S(1)}, bf16[384,2432]{1,0:T(8,128)(2,1)}, bf16[384,2432]{1,0:T(8,128)(2,1)}) custom-call(bf16[2,1,82,384]{3,2,1,0:T(8,128)(2,1)S(1)} %collective-permute-done.17.incoming, bf16[2,384,2304]{2,1,0:T(8,128)(2,1)} %get-tuple-element.39.w, f32[16,384]{1,0:T(8,128)S(1)} %get-tuple-element.40.vecs, ...), custom_call_target="tpu_custom_call" | custom-call | tf_op jit(solution)/shard_map/pallas_call | solution.py:361
  119.7 2.5 %add_convert_fusion = bf16[384,2432]{1,0:T(8,128)(2,1)S(1)} fusion(bf16[384,2432]{1,0:T(8,128)(2,1)} %collective-permute-done.18, bf16[384,2432]{1,0:T(8,128)(2,1)} %get-tuple-element.56), kind=kLoop, calls=%fused_computation.1 | loop fusion | flops 3735552 | bytes 5603328 | tf_op jit(solution)/shard_map/convert_element_type | solution.py:494
  122.4 1.6 collective-permute-start.19
  126.5 1.4 collective-permute-done.19
  128.0 3.5 %collective-permute-done.23 = bf16[48,1280]{1,0:T(8,128)(2,1)S(1)} collective-permute-done((bf16[48,1280]{1,0:T(8,128)(2,1)S(1)}, bf16[48,1280]{1,0:T(8,128)(2,1)S(1)}, u32[]{:S(2)}, u32[]{:S(2)}) %collective-permute-start.23) | collective-permute-done | bytes 122912 | tf_op jit(solution)/shard_map/ppermute | solution.py:373
  132.1 1.6 collective-permute-start.20
  133.7 4.9 %collective-permute-done.24 = bf16[48,2432]{1,0:T(8,128)(2,1)S(1)} collective-permute-done((bf16[48,2432]{1,0:T(8,128)(2,1)S(1)}, bf16[48,2432]{1,0:T(8,128)(2,1)S(1)}, u32[]{:S(2)}, u32[]{:S(2)}) %collective-permute-start.24) | collective-permute-done | bytes 233504 | tf_op jit(solution)/shard_map/ppermute | solution.py:373
  143.1 1.7 %collective-permute-done.25 = bf16[48,2432]{1,0:T(8,128)(2,1)S(1)} collective-permute-done((bf16[48,2432]{1,0:T(8,128)(2,1)S(1)}, bf16[48,2432]{1,0:T(8,128)(2,1)S(1)}, u32[]{:S(2)}, u32[]{:S(2)}) %collective-permute-start.25) | collective-permute-done | bytes 233504 | tf_op jit(solution)/shard_map/ppermute | solution.py:373
  144.9 1.6 %collective-permute-start.21 = (bf16[48,2432]{1,0:T(8,128)(2,1)S(1)}, bf16[48,2432]{1,0:T(8,128)(2,1)S(1)}, u32[]{:S(2)}, u32[]{:S(2)}) collective-permute-start(bf16[48,2432]{1,0:T(8,128)(2,1)S(1)} %get-tuple-element.87), channel_id=1, source_target_pairs={{0,1},{1,3},{3,5},{5,7},{7,6},{6,4},{4,2},{2,0},{8,9},{9,11},{11,1... | collective-permute-start | bytes 700424 | tf_op jit(solution)/shard_map/ppermute | solution.py:373
  149.0 3.1 %collective-permute-done.21 = bf16[48,2432]{1,0:T(8,128)(2,1)S(1)} collective-permute-done((bf16[48,2432]{1,0:T(8,128)(2,1)S(1)}, bf16[48,2432]{1,0:T(8,128)(2,1)S(1)}, u32[]{:S(2)}, u32[]{:S(2)}) %collective-permute-start.21) | collective-permute-done | bytes 233504 | tf_op jit(solution)/shard_map/ppermute | solution.py:373
  152.2 1.6 %collective-permute-start.22 = (bf16[48,2432]{1,0:T(8,128)(2,1)S(1)}, bf16[48,2432]{1,0:T(8,128)(2,1)S(1)}, u32[]{:S(2)}, u32[]{:S(2)}) collective-permute-start(bf16[48,2432]{1,0:T(8,128)(2,1)S(1)} %fusion.3), channel_id=1, source_target_pairs={{0,1},{1,3},{3,5},{5,7},{7,6},{6,4},{4,2},{2,0},{8,9},{9,11},{11,1... | collective-permute-start | bytes 700424 | tf_op jit(solution)/shard_map/ppermute | solution.py:373
  153.8 0.7 copy.42
  154.6 0.7 copy.43
  155.3 3.0 %collective-permute-done.22.left = bf16[48,2432]{1,0:T(8,128)(2,1)S(1)} collective-permute-done((bf16[48,2432]{1,0:T(8,128)(2,1)S(1)}, bf16[48,2432]{1,0:T(8,128)(2,1)S(1)}, u32[]{:S(2)}, u32[]{:S(2)}) %collective-permute-start.22) | collective-permute-done | bytes 233504 | tf_op jit(solution)/shard_map/ppermute | solution.py:373
  158.3 1.0 shard_map.226
  160.0 0.7 copy.45
  160.7 0.8 copy.46
  (106 shorter events, 15.7 us)
Async XLA Ops:
  0.6 40.6 %copy-start.30 = (s32[8]{0:T(128)S(1)}, s32[8]{0:T(128)}, u32[]{:S(2)}) copy-start(s32[8]{0:T(128)} %constant.82.clone) | copy-start | bytes 100
  0.7 41.2 %copy-start.28 = (s32[8]{0:T(128)S(1)}, s32[8]{0:T(128)}, u32[]{:S(2)}) copy-start(s32[8]{0:T(128)} %constant.80.clone) | copy-start | bytes 100
  3.5 0.9 copy-start.23
  7.4 8.8 %collective-permute-start = (bf16[48,2432]{1,0:T(8,128)(2,1)S(1)}, bf16[48,2432]{1,0:T(8,128)(2,1)S(1)}, u32[]{:S(2)}, u32[]{:S(2)}) collective-permute-start(bf16[48,2432]{1,0:T(8,128)(2,1)S(1)} %shard_map.222.refs_0_), channel_id=1, source_target_pairs={{0,1},{1,3},{3,5},{5,7},{7,6},{6,4},{4,2},{2,0},{8,9},{9,11},{11,1... | collective-permute-start | bytes 700424 | tf_op jit(solution)/shard_map/ppermute | solution.py:373
  10.4 7.4 %collective-permute-start.1 = (bf16[48,2432]{1,0:T(8,128)(2,1)S(1)}, bf16[48,2432]{1,0:T(8,128)(2,1)S(1)}, u32[]{:S(2)}, u32[]{:S(2)}) collective-permute-start(bf16[48,2432]{1,0:T(8,128)(2,1)S(1)} %shard_map.222.refs_0_), channel_id=1, source_target_pairs={{0,2},{1,0},{3,1},{5,3},{7,5},{6,7},{4,6},{2,4},{8,10},{9,8},{11,9... | collective-permute-start | bytes 700424 | tf_op jit(solution)/shard_map/ppermute | solution.py:373
  16.1 6.9 %collective-permute-start.2 = (bf16[48,2432]{1,0:T(8,128)(2,1)S(1)}, bf16[48,2432]{1,0:T(8,128)(2,1)S(1)}, u32[]{:S(2)}, u32[]{:S(2)}) collective-permute-start(bf16[48,2432]{1,0:T(8,128)(2,1)S(1)} %collective-permute-done.refs_1_), channel_id=1, source_target_pairs={{0,1},{1,3},{3,5},{5,7},{7,6},{6,4},{4,2},{2,0},{8,9},{9,11},{11,1... | collective-permute-start | bytes 700424 | tf_op jit(solution)/shard_map/ppermute | solution.py:373
  17.8 6.6 %collective-permute-start.3 = (bf16[48,2432]{1,0:T(8,128)(2,1)S(1)}, bf16[48,2432]{1,0:T(8,128)(2,1)S(1)}, u32[]{:S(2)}, u32[]{:S(2)}) collective-permute-start(bf16[48,2432]{1,0:T(8,128)(2,1)S(1)} %collective-permute-done.1.refs_2_), channel_id=1, source_target_pairs={{0,2},{1,0},{3,1},{5,3},{7,5},{6,7},{4,6},{2,4},{8,10},{9,8},{11,9... | collective-permute-start | bytes 700424 | tf_op jit(solution)/shard_map/ppermute | solution.py:373
  23.0 6.1 %collective-permute-start.4 = (bf16[48,2432]{1,0:T(8,128)(2,1)S(1)}, bf16[48,2432]{1,0:T(8,128)(2,1)S(1)}, u32[]{:S(2)}, u32[]{:S(2)}) collective-permute-start(bf16[48,2432]{1,0:T(8,128)(2,1)S(1)} %collective-permute-done.2.refs_3_), channel_id=1, source_target_pairs={{0,1},{1,3},{3,5},{5,7},{7,6},{6,4},{4,2},{2,0},{8,9},{9,11},{11,1... | collective-permute-start | bytes 700424 | tf_op jit(solution)/shard_map/ppermute | solution.py:373
  24.4 9.2 %collective-permute-start.5 = (bf16[48,2432]{1,0:T(8,128)(2,1)S(1)}, bf16[48,2432]{1,0:T(8,128)(2,1)S(1)}, u32[]{:S(2)}, u32[]{:S(2)}) collective-permute-start(bf16[48,2432]{1,0:T(8,128)(2,1)S(1)} %collective-permute-done.3.refs_4_), channel_id=1, source_target_pairs={{0,2},{1,0},{3,1},{5,3},{7,5},{6,7},{4,6},{2,4},{8,10},{9,8},{11,9... | collective-permute-start | bytes 700424 | tf_op jit(solution)/shard_map/ppermute | solution.py:373
  29.2 4.9 %collective-permute-start.6 = (bf16[48,1152]{1,0:T(8,128)(2,1)S(1)}, bf16[48,1152]{1,0:T(8,128)(2,1)S(1)}, u32[]{:S(2)}, u32[]{:S(2)}) collective-permute-start(bf16[48,1152]{1,0:T(8,128)(2,1)S(1)} %slice.34), channel_id=1, source_target_pairs={{0,1},{1,3},{3,5},{5,7},{7,6},{6,4},{4,2},{2,0},{8,9},{9,11},{11,1... | collective-permute-start | bytes 331784 | tf_op jit(solution)/shard_map/ppermute | solution.py:373
  30.9 8.5 %collective-permute-start.8 = (bf16[48,2432]{1,0:T(8,128)(2,1)S(1)}, bf16[48,2432]{1,0:T(8,128)(2,1)S(1)}, u32[]{:S(2)}, u32[]{:S(2)}) collective-permute-start(bf16[48,2432]{1,0:T(8,128)(2,1)S(1)} %shard_map.222.refs_0_), channel_id=1, source_target_pairs={{0,8},{8,0},{1,9},{9,1},{2,10},{10,2},{3,11},{11,3},{4,12},{12,4},... | collective-permute-start | bytes 700424 | tf_op jit(solution)/shard_map/ppermute | solution.py:463
  33.1 6.9 %collective-permute-start.9 = (bf16[48,2432]{1,0:T(8,128)(2,1)S(1)}, bf16[48,2432]{1,0:T(8,128)(2,1)S(1)}, u32[]{:S(2)}, u32[]{:S(2)}) collective-permute-start(bf16[48,2432]{1,0:T(8,128)(2,1)S(1)} %collective-permute-done.refs_1_), channel_id=1, source_target_pairs={{0,8},{8,0},{1,9},{9,1},{2,10},{10,2},{3,11},{11,3},{4,12},{12,4},... | collective-permute-start | bytes 700424 | tf_op jit(solution)/shard_map/ppermute | solution.py:463
  33.6 6.5 %collective-permute-start.10 = (bf16[48,2432]{1,0:T(8,128)(2,1)S(1)}, bf16[48,2432]{1,0:T(8,128)(2,1)S(1)}, u32[]{:S(2)}, u32[]{:S(2)}) collective-permute-start(bf16[48,2432]{1,0:T(8,128)(2,1)S(1)} %collective-permute-done.1.refs_2_), channel_id=1, source_target_pairs={{0,8},{8,0},{1,9},{9,1},{2,10},{10,2},{3,11},{11,3},{4,12},{12,4},... | collective-permute-start | bytes 700424 | tf_op jit(solution)/shard_map/ppermute | solution.py:463
  33.6 9.0 %collective-permute-start.11 = (bf16[48,2432]{1,0:T(8,128)(2,1)S(1)}, bf16[48,2432]{1,0:T(8,128)(2,1)S(1)}, u32[]{:S(2)}, u32[]{:S(2)}) collective-permute-start(bf16[48,2432]{1,0:T(8,128)(2,1)S(1)} %collective-permute-done.2.refs_3_), channel_id=1, source_target_pairs={{0,8},{8,0},{1,9},{9,1},{2,10},{10,2},{3,11},{11,3},{4,12},{12,4},... | collective-permute-start | bytes 700424 | tf_op jit(solution)/shard_map/ppermute | solution.py:463
  34.1 5.3 %collective-permute-start.7 = (bf16[48,1280]{1,0:T(8,128)(2,1)S(1)}, bf16[48,1280]{1,0:T(8,128)(2,1)S(1)}, u32[]{:S(2)}, u32[]{:S(2)}) collective-permute-start(bf16[48,1280]{1,0:T(8,128)(2,1)S(1)} %slice.35), channel_id=1, source_target_pairs={{0,2},{1,0},{3,1},{5,3},{7,5},{6,7},{4,6},{2,4},{8,10},{9,8},{11,9... | collective-permute-start | bytes 368648 | tf_op jit(solution)/shard_map/ppermute | solution.py:373
  39.4 3.9 %collective-permute-start.12 = (bf16[48,2432]{1,0:T(8,128)(2,1)S(1)}, bf16[48,2432]{1,0:T(8,128)(2,1)S(1)}, u32[]{:S(2)}, u32[]{:S(2)}) collective-permute-start(bf16[48,2432]{1,0:T(8,128)(2,1)S(1)} %collective-permute-done.3.refs_4_), channel_id=1, source_target_pairs={{0,8},{8,0},{1,9},{9,1},{2,10},{10,2},{3,11},{11,3},{4,12},{12,4},... | collective-permute-start | bytes 700424 | tf_op jit(solution)/shard_map/ppermute | solution.py:463
  39.4 4.6 %copy-start.5 = (bf16[48,2432]{1,0:T(8,128)(2,1)}, bf16[48,2432]{1,0:T(8,128)(2,1)S(1)}, u32[]{:S(2)}) copy-start(bf16[48,2432]{1,0:T(8,128)(2,1)S(1)} %collective-permute-done.8.refs_8_) | copy-start | bytes 700420
  39.4 4.5 %collective-permute-start.13 = (bf16[48,2432]{1,0:T(8,128)(2,1)S(1)}, bf16[48,2432]{1,0:T(8,128)(2,1)}, u32[]{:S(2)}, u32[]{:S(2)}) collective-permute-start(bf16[48,2432]{1,0:T(8,128)(2,1)S(1)} %collective-permute-done.4.refs_5_), channel_id=1, source_target_pairs={{0,8},{8,0},{1,9},{9,1},{2,10},{10,2},{3,11},{11,3},{4,12},{12,4},... | collective-permute-start | bytes 700424 | tf_op jit(solution)/shard_map/ppermute | solution.py:463
  40.0 4.0 %copy-start.7 = (bf16[48,2432]{1,0:T(8,128)(2,1)}, bf16[48,2432]{1,0:T(8,128)(2,1)S(1)}, u32[]{:S(2)}) copy-start(bf16[48,2432]{1,0:T(8,128)(2,1)S(1)} %collective-permute-done.9.refs_9_) | copy-start | bytes 700420
  40.0 4.0 %collective-permute-start.14 = (bf16[48,2432]{1,0:T(8,128)(2,1)S(1)}, bf16[48,2432]{1,0:T(8,128)(2,1)}, u32[]{:S(2)}, u32[]{:S(2)}) collective-permute-start(bf16[48,2432]{1,0:T(8,128)(2,1)S(1)} %collective-permute-done.5.refs_6_), channel_id=1, source_target_pairs={{0,8},{8,0},{1,9},{9,1},{2,10},{10,2},{3,11},{11,3},{4,12},{12,4},... | collective-permute-start | bytes 700424 | tf_op jit(solution)/shard_map/ppermute | solution.py:463
  40.8 3.2 %collective-permute-start.15 = (bf16[48,2432]{1,0:T(8,128)(2,1)S(1)}, bf16[48,2432]{1,0:T(8,128)(2,1)S(1)}, u32[]{:S(2)}, u32[]{:S(2)}) collective-permute-start(bf16[48,2432]{1,0:T(8,128)(2,1)S(1)} %constant_dynamic-update-slice_fusion.refs_7_), channel_id=1, source_target_pairs={{0,8},{8,0},{1,9},{9,1},{2,10},{10,2},{3,11},{11,3},{4,12},{12,4},... | collective-permute-start | bytes 700424 | tf_op jit(solution)/shard_map/ppermute | solution.py:463
  41.9 22.3 %copy-start.29 = (s32[2,1]{0,1:T(1,128)S(1)}, s32[2,1]{0,1:T(1,128)}, u32[]{:S(2)}) copy-start(s32[2,1]{0,1:T(1,128)} %param.17) | copy-start | bytes 28
  43.3 0.7 copy-start.13
  44.7 0.9 copy-start.6
  45.6 0.9 copy-start.8
  46.6 0.9 copy-start.10
  47.5 0.9 copy-start.12
  48.5 0.9 copy-start.14
  49.4 0.9 copy-start.16
  60.8 6.8 %collective-permute-start.16 = (bf16[2,1,82,384]{3,2,1,0:T(8,128)(2,1)}, bf16[2,1,82,384]{3,2,1,0:T(8,128)(2,1)S(1)}, u32[]{:S(2)}, u32[]{:S(2)}) collective-permute-start(bf16[2,1,82,384]{3,2,1,0:T(8,128)(2,1)} %get-tuple-element.38.h0), channel_id=1, source_target_pairs={{0,16},{1,17},{2,18},{3,19},{4,20},{5,21},{6,22},{7,23},{8,24},{9,... | collective-permute-start | bytes 377864 | tf_op jit(solution)/shard_map/ppermute | solution.py:475
  67.6 23.9 %copy-start.2 = (f32[2,176,768]{2,1,0:T(8,128)S(1)}, f32[2,176,768]{2,1,0:T(8,128)}, u32[]{:S(2)}) copy-start(f32[2,176,768]{2,1,0:T(8,128)} %get-tuple-element.53.refs_8_) | copy-start | bytes 3244036
  67.6 23.9 %copy-start.3 = (f32[2,176,576]{2,1,0:T(8,128)S(1)}, f32[2,176,576]{2,1,0:T(8,128)}, u32[]{:S(2)}) copy-start(f32[2,176,576]{2,1,0:T(8,128)} %get-tuple-element.48.refs_3_) | copy-start | bytes 2433028
  67.6 23.9 %copy-start.4 = (bf16[2,176,768]{2,1,0:T(8,128)(2,1)S(1)}, bf16[2,176,768]{2,1,0:T(8,128)(2,1)}, u32[]{:S(2)}) copy-start(bf16[2,176,768]{2,1,0:T(8,128)(2,1)} %get-tuple-element.54.refs_9_) | copy-start | bytes 1622020
  67.6 23.9 %copy-start.18 = (f32[2,176,1]{2,1,0:T(8,128)S(1)}, f32[2,176,1]{2,1,0:T(8,128)}, u32[]{:S(2)}) copy-start(f32[2,176,1]{2,1,0:T(8,128)} %copy-done.17) | copy-start | bytes 4228
  67.6 23.9 %copy-start.20 = (bf16[176,384]{1,0:T(8,128)(2,1)S(1)}, bf16[176,384]{1,0:T(8,128)(2,1)}, u32[]{:S(2)}) copy-start(bf16[176,384]{1,0:T(8,128)(2,1)} %copy-done.19) | copy-start | bytes 405508
  67.6 23.9 %copy-start.22 = (bf16[176,384]{1,0:T(8,128)(2,1)S(1)}, bf16[176,384]{1,0:T(8,128)(2,1)}, u32[]{:S(2)}) copy-start(bf16[176,384]{1,0:T(8,128)(2,1)} %copy-done.21) | copy-start | bytes 405508
  70.1 1.3 copy-start
  71.3 1.3 copy-start.1
  72.6 18.9 %collective-permute-start.17 = (bf16[2,1,82,384]{3,2,1,0:T(8,128)(2,1)S(1)}, bf16[2,1,82,384]{3,2,1,0:T(8,128)(2,1)S(1)}, u32[]{:S(2)}, u32[]{:S(2)}) collective-permute-start(bf16[2,1,82,384]{3,2,1,0:T(8,128)(2,1)S(1)} %get-tuple-element.42.own), channel_id=1, source_target_pairs={{16,0},{17,1},{18,2},{19,3},{20,4},{21,5},{22,6},{23,7},{24,8},{25... | collective-permute-start | bytes 377864 | tf_op jit(solution)/shard_map/ppermute | solution.py:484
  103.5 16.3 %collective-permute-start.18 = (bf16[384,2432]{1,0:T(8,128)(2,1)}, bf16[384,2432]{1,0:T(8,128)(2,1)}, u32[]{:S(2)}, u32[]{:S(2)}) collective-permute-start(bf16[384,2432]{1,0:T(8,128)(2,1)} %get-tuple-element.57), channel_id=1, source_target_pairs={{0,8},{8,0},{1,9},{9,1},{2,10},{10,2},{3,11},{11,3},{4,12},{12,4},... | collective-permute-start | bytes 5603336 | tf_op jit(solution)/shard_map/ppermute | solution.py:492
  122.4 5.5 %collective-permute-start.19 = (bf16[48,1152]{1,0:T(8,128)(2,1)S(1)}, bf16[48,1152]{1,0:T(8,128)(2,1)S(1)}, u32[]{:S(2)}, u32[]{:S(2)}) collective-permute-start(bf16[48,1152]{1,0:T(8,128)(2,1)S(1)} %slice.37), channel_id=1, source_target_pairs={{0,1},{1,3},{3,5},{5,7},{7,6},{6,4},{4,2},{2,0},{8,9},{9,11},{11,1... | collective-permute-start | bytes 331784 | tf_op jit(solution)/shard_map/ppermute | solution.py:373
  126.0 5.5 %collective-permute-start.23 = (bf16[48,1280]{1,0:T(8,128)(2,1)S(1)}, bf16[48,1280]{1,0:T(8,128)(2,1)S(1)}, u32[]{:S(2)}, u32[]{:S(2)}) collective-permute-start(bf16[48,1280]{1,0:T(8,128)(2,1)S(1)} %slice.41), channel_id=1, source_target_pairs={{0,2},{1,0},{3,1},{5,3},{7,5},{6,7},{4,6},{2,4},{8,10},{9,8},{11,9... | collective-permute-start | bytes 368648 | tf_op jit(solution)/shard_map/ppermute | solution.py:373
  131.6 7.1 %collective-permute-start.24 = (bf16[48,2432]{1,0:T(8,128)(2,1)S(1)}, bf16[48,2432]{1,0:T(8,128)(2,1)S(1)}, u32[]{:S(2)}, u32[]{:S(2)}) collective-permute-start(bf16[48,2432]{1,0:T(8,128)(2,1)S(1)} %pad_maximum_fusion.1), channel_id=1, source_target_pairs={{0,2},{1,0},{3,1},{5,3},{7,5},{6,7},{4,6},{2,4},{8,10},{9,8},{11,9... | collective-permute-start | bytes 700424 | tf_op jit(solution)/shard_map/ppermute | solution.py:373
  132.1 11.0 %collective-permute-start.20 = (bf16[48,2432]{1,0:T(8,128)(2,1)S(1)}, bf16[48,2432]{1,0:T(8,128)(2,1)S(1)}, u32[]{:S(2)}, u32[]{:S(2)}) collective-permute-start(bf16[48,2432]{1,0:T(8,128)(2,1)S(1)} %pad_maximum_fusion), channel_id=1, source_target_pairs={{0,1},{1,3},{3,5},{5,7},{7,6},{6,4},{4,2},{2,0},{8,9},{9,11},{11,1... | collective-permute-start | bytes 700424 | tf_op jit(solution)/shard_map/ppermute | solution.py:373
  138.7 6.1 %collective-permute-start.25 = (bf16[48,2432]{1,0:T(8,128)(2,1)S(1)}, bf16[48,2432]{1,0:T(8,128)(2,1)S(1)}, u32[]{:S(2)}, u32[]{:S(2)}) collective-permute-start(bf16[48,2432]{1,0:T(8,128)(2,1)S(1)} %fusion), channel_id=1, source_target_pairs={{0,2},{1,0},{3,1},{5,3},{7,5},{6,7},{4,6},{2,4},{8,10},{9,8},{11,9... | collective-permute-start | bytes 700424 | tf_op jit(solution)/shard_map/ppermute | solution.py:373
  144.9 7.2 %collective-permute-start.21 = (bf16[48,2432]{1,0:T(8,128)(2,1)S(1)}, bf16[48,2432]{1,0:T(8,128)(2,1)S(1)}, u32[]{:S(2)}, u32[]{:S(2)}) collective-permute-start(bf16[48,2432]{1,0:T(8,128)(2,1)S(1)} %get-tuple-element.87), channel_id=1, source_target_pairs={{0,1},{1,3},{3,5},{5,7},{7,6},{6,4},{4,2},{2,0},{8,9},{9,11},{11,1... | collective-permute-start | bytes 700424 | tf_op jit(solution)/shard_map/ppermute | solution.py:373
  148.5 6.8 %collective-permute-start.26 = (bf16[48,2432]{1,0:T(8,128)(2,1)S(1)}, bf16[48,2432]{1,0:T(8,128)(2,1)S(1)}, u32[]{:S(2)}, u32[]{:S(2)}) collective-permute-start(bf16[48,2432]{1,0:T(8,128)(2,1)S(1)} %get-tuple-element.86), channel_id=1, source_target_pairs={{0,2},{1,0},{3,1},{5,3},{7,5},{6,7},{4,6},{2,4},{8,10},{9,8},{11,9... | collective-permute-start | bytes 700424 | tf_op jit(solution)/shard_map/ppermute | solution.py:373
  152.2 6.1 %collective-permute-start.22 = (bf16[48,2432]{1,0:T(8,128)(2,1)S(1)}, bf16[48,2432]{1,0:T(8,128)(2,1)S(1)}, u32[]{:S(2)}, u32[]{:S(2)}) collective-permute-start(bf16[48,2432]{1,0:T(8,128)(2,1)S(1)} %fusion.3), channel_id=1, source_target_pairs={{0,1},{1,3},{3,5},{5,7},{7,6},{6,4},{4,2},{2,0},{8,9},{9,11},{11,1... | collective-permute-start | bytes 700424 | tf_op jit(solution)/shard_map/ppermute | solution.py:373
  (10 other events, 6.7 us)

commit v2 on v1

v2 whole, which is shorter than its diff:
```python
import functools
import math

import jax
import jax.numpy as jnp
from jax import lax
from jax.experimental import pallas as pl
from jax.experimental.pallas import tpu as pltpu
from jax.sharding import PartitionSpec as P

HD = 64
EPS = 1e-06
INV_ROOT_TWO = 0.7071067811865476
INV_ROOT_TWO_PI = 0.3989422804014327
SCALE = 1.0 / math.sqrt(HD)
BF = jnp.bfloat16
F32 = jnp.float32
GRID_RING = (0, 1, 3, 5, 7, 6, 4, 2)
RING_PLACE = tuple(GRID_RING.index(i) for i in range(len(GRID_RING)))
NEAR = 2
ROW_STEP = 88
EXT = 128


def dot(a, b, dims):
    return lax.dot_general(a, b, (dims, ((), ())), preferred_element_type=F32)


def nn(a, b):
    return dot(a, b, ((1,), (0,)))


def nt(a, b):
    return dot(a, b, ((1,), (1,)))


def tn(a, b):
    return dot(a, b, ((0,), (0,)))


def norm(value):
    mean = jnp.mean(value, axis=-1, keepdims=True)
    centred = value - mean
    var = jnp.mean(centred * centred, axis=-1, keepdims=True)
    factor = lax.rsqrt(var + EPS)
    return centred * factor, factor


def norm_back(grad, unit, factor, gain):
    scaled = grad * gain
    plain = jnp.mean(scaled, axis=-1, keepdims=True)
    along = jnp.mean(scaled * unit, axis=-1, keepdims=True)
    return (scaled - plain - unit * along) * factor


def picked(options, index):
    value = jnp.int32(options[0])
    for i in range(1, len(options)):
        value = jnp.where(index == i, jnp.int32(options[i]), value)
    return value


class Dims:
    def __init__(self, seq, width, hidden, shards):
        self.seq, self.width, self.hidden, self.shards = seq, width, hidden, shards
        self.half = width // 2
        self.fh = hidden // 2
        self.heads = self.half // HD
        self.o_out = 3 * self.half
        self.o_up = self.o_out + self.half
        self.o_down = self.o_up + self.fh
        self.cols = self.o_down + self.fh
        self.packed = self.cols + EXT
        self.rows = 2 * ROW_STEP
        self.groups = width // 128

    def state_shapes(self):
        r, w = self.rows, self.width
        return dict(
            proj=((2, r, 3 * self.half), F32),
            probs=((4 * self.heads, ROW_STEP, ROW_STEP), F32),
            mixed=((2, r, self.half), F32),
            unit_one=((r, w), F32),
            factors=((2, r, 1), F32),
            first=((r, w), BF),
            unit_two=((r, w), F32),
            second=((r, w), BF),
            slope=((2, r, self.fh), F32),
            active=((2, r, self.fh), BF),
        )

    def cotangent_shapes(self):
        r, w = self.rows, self.width
        return dict(
            branch=((r, w), BF),
            hidden=((2, r, self.fh), BF),
            attn=((r, w), BF),
            proj=((2, r, 3 * self.half), F32),
            vecs=((16, w), F32),
        )

    def work_shapes(self):
        return dict(
            rows=((self.rows, self.width), F32),
            mixed=((2, self.rows, self.half), F32),
            scores=((4 * self.heads, ROW_STEP, ROW_STEP), F32),
        )

    def cells(self):
        for t in range(2):
            for m in range(2):
                for h in range(self.heads):
                    rows = slice(m * ROW_STEP, (m + 1) * ROW_STEP)
                    yield (t * 2 + m) * self.heads + h, t, rows, h * HD


def layer_forward(dm, state, w, vecs, st, keep, weights_ready=None):
    half, fh = dm.half, dm.fh
    unit, factor = norm(state)
    first = (unit * vecs[0:1, :] + vecs[2:3, :]).astype(BF)
    if keep:
        st["unit_one"][...] = unit
        st["factors"][0] = factor
        st["first"][...] = first
    proj, mixed = st["proj"], st["mixed"]
    for t in range(2):
        value = nn(first, w[t, :, 0 : 3 * half])
        proj[t, :, 0:half] = value[:, 0:half] + vecs[6:7, t * half : (t + 1) * half]
        proj[t, :, half : 2 * half] = value[:, half : 2 * half]
        proj[t, :, 2 * half :] = value[:, 2 * half :] + vecs[7:8, t * half : (t + 1) * half]
    for i, t, rows, c in dm.cells():
        query, keys = proj[t, rows, c : c + HD], proj[t, rows, half + c : half + c + HD]
        st["probs"][i] = nt(query.astype(BF), keys.astype(BF))
    scores = st["probs"][...] * SCALE
    column = lax.broadcasted_iota(jnp.int32, scores.shape, 2)
    scores = jnp.where(column < dm.seq, scores, -1e30)
    expo = jnp.exp(scores - jnp.max(scores, axis=-1, keepdims=True))
    st["probs"][...] = expo * (1.0 / jnp.sum(expo, axis=-1, keepdims=True))
    for i, t, rows, c in dm.cells():
        values = proj[t, rows, 2 * half + c : 2 * half + c + HD]
        mixed[t, rows, c : c + HD] = nn(st["probs"][i].astype(BF), values.astype(BF))
    resid = state + vecs[3:4, :]
    for t in range(2):
        resid += nt(mixed[t].astype(BF), w[t, :, dm.o_out : dm.o_out + half])
    unit, factor = norm(resid)
    second = (unit * vecs[1:2, :] + vecs[4:5, :]).astype(BF)
    if keep:
        st["unit_two"][...] = unit
        st["factors"][1] = factor
        st["second"][...] = second
    output = resid + vecs[5:6, :]
    per = fh // dm.width
    if weights_ready is not None:
        weights_ready()
    for t in range(2):
        bias = jnp.concatenate([vecs[8 + t * per + j : 9 + t * per + j, :] for j in range(per)], axis=1)
        hidden = nn(second, w[t, :, dm.o_up : dm.o_up + fh]) + bias
        curve = 0.5 * (1.0 + lax.erf(hidden * INV_ROOT_TWO))
        active = (hidden * curve).astype(BF)
        if keep:
            st["slope"][t] = curve + hidden * jnp.exp(-0.5 * hidden * hidden) * INV_ROOT_TWO_PI
            st["active"][t] = active
        output += nt(active, w[t, :, dm.o_down : dm.o_down + fh])
    return output


def total_rows(value):
    return jnp.sum(value, axis=0, keepdims=True)


def layer_backward(dm, grad, w, vecs, st, ct, work):
    half, fh = dm.half, dm.fh
    low = grad.astype(BF)
    ct["branch"][...] = low
    shift_branch = total_rows(low.astype(F32))
    per = fh // dm.width
    grad_second = None
    for t in range(2):
        raw = nn(low, w[t, :, dm.o_down : dm.o_down + fh]) * st["slope"][t]
        up_bias = total_rows(raw)
        for j in range(per):
            ct["vecs"][8 + t * per + j : 9 + t * per + j, :] = up_bias[:, j * dm.width : (j + 1) * dm.width]
        grad_hidden = raw.astype(BF)
        ct["hidden"][t] = grad_hidden
        part = nt(grad_hidden, w[t, :, dm.o_up : dm.o_up + fh])
        grad_second = part if grad_second is None else grad_second + part
    unit = st["unit_two"][...]
    gain_two, shift_two = total_rows(grad_second * unit), total_rows(grad_second)
    grad_resid = grad + norm_back(grad_second, unit, st["factors"][1], vecs[1:2, :])
    low = grad_resid.astype(BF)
    ct["attn"][...] = low
    shift_attn = total_rows(low.astype(F32))
    proj, gproj, gmix, scores = st["proj"], ct["proj"], work["mixed"], work["scores"]
    for t in range(2):
        gmix[t] = nn(low, w[t, :, dm.o_out : dm.o_out + half])
    for i, t, rows, c in dm.cells():
        values = proj[t, rows, 2 * half + c : 2 * half + c + HD].astype(BF)
        gm = gmix[t, rows, c : c + HD].astype(BF)
        scores[i] = nt(gm, values)
        gproj[t, rows, 2 * half + c : 2 * half + c + HD] = tn(st["probs"][i].astype(BF), gm)
    probs, gp = st["probs"][...], scores[...]
    scores[...] = probs * (gp - jnp.sum(gp * probs, axis=-1, keepdims=True)) * SCALE
    for i, t, rows, c in dm.cells():
        query = proj[t, rows, c : c + HD].astype(BF)
        keys = proj[t, rows, half + c : half + c + HD].astype(BF)
        gs = scores[i].astype(BF)
        gproj[t, rows, c : c + HD] = nn(gs, keys)
        gproj[t, rows, half + c : half + c + HD] = tn(gs, query)
    grad_first = None
    for t in range(2):
        ct["vecs"][6:7, t * half : (t + 1) * half] = total_rows(gproj[t, :, 0:half])
        ct["vecs"][7:8, t * half : (t + 1) * half] = total_rows(gproj[t, :, 2 * half :])
        part = nt(gproj[t].astype(BF), w[t, :, 0 : 3 * half])
        grad_first = part if grad_first is None else grad_first + part
    unit = st["unit_one"][...]
    gain_one, shift_one = total_rows(grad_first * unit), total_rows(grad_first)
    for i, v in enumerate((gain_one, gain_two, shift_one, shift_attn, shift_two, shift_branch)):
        ct["vecs"][i : i + 1, :] = v
    return grad_resid + norm_back(grad_first, unit, st["factors"][0], vecs[0:1, :])


def parameter_grads(dm, st, ct, grads, slots):
    half, fh = dm.half, dm.fh
    block = dm.width // dm.shards

    def keep(t, column, value):
        for f in range(dm.shards):
            rows = value[f * block : (f + 1) * block].astype(BF)
            grads[t][slots[f], :, column : column + value.shape[1]] = rows

    for t in range(2):
        keep(t, dm.o_down, tn(ct["branch"][...], st["active"][t]))
        keep(t, dm.o_up, tn(st["second"][...], ct["hidden"][t]))
        keep(t, dm.o_out, tn(ct["attn"][...], st["mixed"][t].astype(BF)))
        keep(t, 0, tn(st["first"][...], ct["proj"][t].astype(BF)))
    own_first = lax.axis_index("tensor") == 0
    plain = ct["vecs"][0:6, :]
    turned = jnp.concatenate([plain[:, half:], plain[:, 0:half]], axis=1)
    plain = jnp.where(own_first, plain, turned)
    share, up_share = half // dm.shards, fh // dm.shards
    per = fh // dm.width
    for t in range(2):
        stack = jnp.concatenate([plain, ct["vecs"][6:8, :]], axis=0)[:, t * half : (t + 1) * half]
        up = jnp.concatenate([ct["vecs"][8 + t * per + j : 9 + t * per + j, :] for j in range(per)], axis=1)
        for f in range(dm.shards):
            piece = jnp.concatenate([stack[:, f * share : (f + 1) * share], jnp.zeros((8, EXT - share), F32)], axis=1)
            up_piece = up[:, f * up_share : (f + 1) * up_share]
            up_piece = jnp.concatenate([up_piece, jnp.zeros((1, EXT - up_share), F32)], axis=1)
            piece = jnp.concatenate([piece, up_piece, jnp.zeros((block - 9, EXT), F32)], axis=0)
            grads[t][slots[f], :, dm.cols :] = piece.astype(BF)


def spread(dm, ref, get):
    pad = jnp.zeros((ROW_STEP - dm.seq, dm.width), F32)
    for m in range(2):
        ref[m * ROW_STEP : m * ROW_STEP + dm.seq, :] = get(m)
        ref[m * ROW_STEP + dm.seq : (m + 1) * ROW_STEP, :] = pad


def image(dm, value, m):
    return value[m * ROW_STEP : m * ROW_STEP + dm.seq, :]


def named(shapes, refs):
    return dict(zip(shapes, refs)), refs[len(shapes) :]


def kernel_first(dm, layout, ring, tokens, *refs):
    count = len(layout)
    pieces, refs = refs[: 2 * count], refs[2 * count :]
    w, vecs, out, proj, probs, mixed, rows, extra, sems = refs
    st = dict(proj=proj, probs=probs, mixed=mixed)
    block = dm.width // dm.shards
    early, late = [], []
    if ring:
        place = picked(RING_PLACE, lax.axis_index("fsdp"))
    for t in range(2):
        for i, (offset, start) in enumerate(layout):
            piece = pieces[t * count + i]
            if ring:
                owner = picked([GRID_RING[(p + offset) % dm.shards] for p in range(dm.shards)], place)
                where = pl.ds(pl.multiple_of(owner * block, 16), block)
            else:
                owner = offset
                where = pl.ds(offset * block, block)
            stop = start + piece.shape[1]
            bounds = (0, dm.o_up, dm.cols, dm.packed)
            for j in range(3):
                lo, hi = max(start, bounds[j]), min(stop, bounds[j + 1])
                if lo < hi:
                    target = extra.at[t, owner] if j == 2 else w.at[t, where, pl.ds(lo, hi - lo)]
                    copy = pltpu.make_async_copy(
                        piece.at[:, pl.ds(lo - start, hi - lo)], target, sems.at[j, t * count + i]
                    )
                    (late if j == 1 else early).append(copy)
    for copy in early + late:
        copy.start()
    spread(dm, rows, lambda m: tokens[m, 0].astype(F32))
    for copy in early:
        copy.wait()
    share, up_share = dm.half // dm.shards, dm.fh // dm.shards
    small = [
        jnp.concatenate([extra[t, f].astype(F32)[0:8, 0:share] for f in range(dm.shards)], axis=1) for t in range(2)
    ]
    own_first = lax.axis_index("tensor") == 0
    straight = jnp.concatenate(small, axis=1)
    turned = jnp.concatenate(small[::-1], axis=1)
    vecs[0:6, :] = jnp.where(own_first, straight, turned)[0:6]
    vecs[6:8, :] = straight[6:8]
    per = dm.fh // dm.width
    for t in range(2):
        up = jnp.concatenate([extra[t, f].astype(F32)[8:9, 0:up_share] for f in range(dm.shards)], axis=1)
        for j in range(per):
            vecs[8 + t * per + j : 9 + t * per + j, :] = up[:, j * dm.width : (j + 1) * dm.width]

    def weights_ready():
        for copy in late:
            copy.wait()

    output = layer_forward(dm, rows[...], w, vecs, st, False, weights_ready)
    for m in range(2):
        out[m, 0] = image(dm, output, m).astype(BF)


def live_of(count_ref, m):
    return (lax.axis_index("tensor") < count_ref[m, 0]).astype(F32)


def ring_slots(dm, ring):
    if not ring:
        return range(dm.shards)
    place = picked(RING_PLACE, lax.axis_index("fsdp"))
    return [lax.rem(RING_PLACE[f] + NEAR + dm.shards - place, dm.shards) for f in range(dm.shards)]


def kernel_second(dm, count_ref, tokens, h1, out_grad, w, vecs, acts, grad_in, *refs):
    st, refs = named(dm.state_shapes(), refs)
    ct, refs = named(dm.cotangent_shapes(), refs)
    work, _ = named(dm.work_shapes(), refs)
    rows = work["rows"]
    last = lax.axis_index("section") != 0

    @pl.when(jnp.logical_not(last))
    def _():
        spread(dm, rows, lambda m: tokens[m, 0].astype(F32))

    @pl.when(last)
    def _():
        spread(dm, rows, lambda m: h1[m, 0].astype(F32))

    output = layer_forward(dm, rows[...], w, vecs, st, True)
    for m in range(2):
        acts[m, 0] = (image(dm, output, m) * live_of(count_ref, m)).astype(BF)

    @pl.when(last)
    def _():
        spread(dm, rows, lambda m: out_grad[m, 0].astype(F32) * live_of(count_ref, m))
        grad = layer_backward(dm, rows[...], w, vecs, st, ct, work)
        for m in range(2):
            grad_in[m, 0] = image(dm, grad, m).astype(BF)


def kernel_third(dm, ring, incoming, w, vecs, own, *refs):
    st, refs = named(dm.state_shapes(), refs)
    given, refs = named(dm.cotangent_shapes(), refs)
    grad_in, grad_own, grad_other, *refs = refs
    ct, refs = named(dm.cotangent_shapes(), refs)
    work, _ = named(dm.work_shapes(), refs)
    rows = work["rows"]
    last = lax.axis_index("section") != 0

    @pl.when(jnp.logical_not(last))
    def _():
        spread(dm, rows, lambda m: incoming[m, 0].astype(F32))
        grad = layer_backward(dm, rows[...], w, vecs, st, ct, work)
        for m in range(2):
            grad_in[m, 0] = image(dm, grad, m).astype(BF)

    @pl.when(last)
    def _():
        grad_in[...] = own[...]
        for name in ct:
            ct[name][...] = given[name][...]

    parameter_grads(dm, st, ct, (grad_own, grad_other), ring_slots(dm, ring))


def kernel_unpack(dm, *refs):
    terms, (g_qkv, g_out, g_up, g_down, g_head, g_upb, g_gain, g_shift) = refs[:-8], refs[-8:]
    half, fh = dm.half, dm.fh

    def total(rows, lo, count):
        return sum(ref[rows, lo : lo + count].astype(F32) for ref in terms)

    every = slice(None)
    for k in range(3):
        g_qkv[k] = total(every, k * half, half)
    g_out[...] = total(every, dm.o_out, half)
    g_up[...] = total(every, dm.o_up, fh)
    g_down[...] = total(every, dm.o_down, fh)
    ext = total(slice(0, 16), dm.cols, EXT)
    share, up_share = half // dm.shards, fh // dm.shards
    g_gain[0] = ext[0:2, 0:share]
    g_shift[0] = ext[2:6, 0:share]
    g_head[0] = ext[6:8, 0:share]
    g_upb[...] = ext[8:9, 0:up_share]


VM = pl.BlockSpec(memory_space=pltpu.VMEM)
AN = pl.BlockSpec(memory_space=pl.ANY)
SM = pl.BlockSpec(memory_space=pltpu.SMEM)


def call(kernel, ins, outs, args, scratch=(), limit=16):
    return pl.pallas_call(
        kernel,
        in_specs=ins,
        out_specs=[VM] * len(outs),
        out_shape=[jax.ShapeDtypeStruct(s, d) for s, d in outs],
        scratch_shapes=list(scratch),
        compiler_params=pltpu.CompilerParams(vmem_limit_bytes=limit * 2**20),
    )(*args)


def shifted(value, cycle, step):
    count = len(cycle)
    return lax.ppermute(value, "fsdp", [(cycle[i], cycle[(i + step) % count]) for i in range(count)])


def gather_ring(block, cycle):
    count = len(cycle)
    ahead = behind = block
    found, layout = [block], [(0, 0)]
    for step in range(1, count // 2):
        ahead, behind = shifted(ahead, cycle, 1), shifted(behind, cycle, -1)
        found += [ahead, behind]
        layout += [(-step, 0), (step, 0)]
    cut = block.shape[1] // 256 * 128
    found += [shifted(ahead[:, :cut], cycle, 1), shifted(behind[:, cut:], cycle, -1)]
    layout += [(-(count // 2), 0), (count // 2, cut)]
    return found, layout


def both_ways(ahead, behind, cycle):
    ahead, behind = lax.optimization_barrier((ahead, behind))
    return lax.optimization_barrier((shifted(ahead, cycle, 1), shifted(behind, cycle, -1)))


def reduce_ring(own, other, cycle, swap):
    count = len(cycle)
    far = count // 2
    cut = own.shape[2] // 256 * 128
    split = NEAR + far - 1
    far_part = lax.ppermute(other[split:], "tensor", swap)
    near_part = lax.ppermute(other[:split], "tensor", swap)

    def part(offset, lo=0, hi=None, *more):
        slot = (offset + NEAR) % count
        given = far_part[slot - split] if slot >= split else near_part[slot]
        terms = (own[slot][:, lo:hi], given[:, lo:hi]) + more
        return sum(v.astype(F32) for v in terms).astype(BF)

    low, high = both_ways(part(far, 0, cut), part(far, cut), cycle)
    step = far - 1
    ahead = jnp.concatenate([part(step, 0, cut, low), part(step, cut)], axis=1)
    behind = jnp.concatenate([part(-step, 0, cut), part(-step, cut, None, high)], axis=1)
    left, right = both_ways(ahead, behind, cycle)
    for step in range(far - 2, 0, -1):
        ahead, behind = part(step, 0, None, left), part(-step, 0, None, right)
        left, right = both_ways(ahead, behind, cycle)
    return own[NEAR], near_part[NEAR], left, right


def per_device(tokens, out_grad, image_count, w_qkv, w_out, w_up, w_down, head_bias, up_bias, gains, shifts):
    seq, width = tokens.shape[2:]
    shards = lax.axis_size("fsdp")
    ring = shards == len(GRID_RING)
    hidden = w_up.shape[2] * 2
    dm = Dims(seq, width, hidden, len(GRID_RING))
    block = width // dm.shards
    swap = [(0, 1), (1, 0)]
    vectors = (head_bias, up_bias, gains, shifts)
    small = jnp.concatenate([gains[0], shifts[0], head_bias[0]], axis=0)
    if ring:
        ext = jnp.concatenate(
            [
                jnp.pad(small, ((0, 0), (0, EXT - small.shape[1]))),
                jnp.pad(up_bias, ((0, block - 9), (0, EXT - up_bias.shape[1]))),
            ],
            axis=0,
        )
        packed = jnp.concatenate(
            [w_qkv[0, :, 0], w_qkv[0, :, 1], w_qkv[0, :, 2], w_out[0].T, w_up[0], w_down[0].T, ext], axis=1
        )
        found, layout = gather_ring(packed, GRID_RING)
    else:
        rows = jnp.concatenate([w_qkv[0].reshape(w_qkv.shape[1], -1), w_out[0].T, w_up[0], w_down[0].T], axis=1)
        rows = lax.all_gather(rows, "fsdp", axis=0, tiled=True)
        small = lax.all_gather(small, "fsdp", axis=1, tiled=True)
        up = lax.all_gather(up_bias, "fsdp", axis=1, tiled=True)
        small = jnp.moveaxis(small.reshape(8, dm.shards, -1), 1, 0)
        ext = jnp.concatenate(
            [
                jnp.pad(small, ((0, 0), (0, 0), (0, EXT - small.shape[2]))),
                jnp.pad(
                    up.reshape(dm.shards, 1, -1), ((0, 0), (0, block - 9), (0, EXT - up.shape[1] // dm.shards))
                ),
            ],
            axis=1,
        )
        rows = jnp.concatenate([rows, ext.reshape(width, EXT)], axis=1)
        found = [rows[i * block : (i + 1) * block] for i in range(dm.shards)]
        layout = [(i, 0) for i in range(dm.shards)]
    others = [lax.ppermute(b, "tensor", swap) for b in found]
    states = dm.state_shapes()
    cotangents = dm.cotangent_shapes()
    shape = tokens.shape
    buffers = lambda shapes: [pltpu.VMEM(*v) for v in shapes]
    work = buffers(dm.work_shapes().values())
    w, vecs, low0 = call(
        functools.partial(kernel_first, dm, layout, ring),
        [VM] + [AN] * (2 * len(found)),
        [((2, width, dm.cols), BF), ((16, width), F32), (shape, BF)],
        (tokens,) + tuple(found) + tuple(others),
        scratch=buffers([states["proj"], states["probs"], states["mixed"], ((dm.rows, width), F32)])
        + [pltpu.VMEM((2, dm.shards, block, EXT), BF), pltpu.SemaphoreType.DMA((3, 2 * len(found)))],
    )
    h1 = lax.ppermute(low0, "section", [(0, 1)])
    kept = list(states.values()) + list(cotangents.values())
    acts, grad1, *kept = call(
        functools.partial(kernel_second, dm),
        [SM] + [VM] * 5,
        [(shape, BF), (shape, BF)] + kept,
        (image_count, tokens, h1, out_grad, w, vecs),
        scratch=work,
    )
    incoming = lax.ppermute(grad1, "section", [(1, 0)])
    in_grads, own, other = call(
        functools.partial(kernel_third, dm, ring),
        [VM] * (4 + len(kept)),
        [(shape, BF)] + [((dm.shards, block, dm.packed), BF)] * 2,
        (incoming, w, vecs, grad1) + tuple(kept),
        scratch=buffers(cotangents.values()) + work,
    )
    if ring:
        terms = reduce_ring(own, other, GRID_RING, swap)
        shapes = [(3, block, dm.half), (block, dm.half), (block, dm.fh), (block, dm.fh)] + [v.shape for v in vectors]
        g_qkv, g_out, g_up, g_down, *small = call(
            functools.partial(kernel_unpack, dm), [VM] * len(terms), [(v, F32) for v in shapes], terms
        )
        grads = [jnp.transpose(g_qkv, (1, 0, 2))[None], g_out.T[None], g_up[None], g_down.T[None], *small]
    else:
        half = dm.half
        mine = own.astype(F32) + lax.ppermute(other, "tensor", swap).astype(F32)
        mine = mine.reshape(width, dm.packed)
        body = lax.psum_scatter(mine[:, : dm.cols], "fsdp", scatter_dimension=0, tiled=True)
        share, up_share = half // dm.shards, dm.fh // dm.shards
        ext = mine[:, dm.cols :].reshape(dm.shards, block, EXT)
        small = jnp.moveaxis(ext[:, 0:8, 0:share], 0, 1).reshape(8, half)
        small = lax.psum_scatter(small, "fsdp", scatter_dimension=1, tiled=True)
        up = lax.psum_scatter(ext[:, 8, 0:up_share].reshape(-1), "fsdp", scatter_dimension=0, tiled=True)
        grads = [
            body[:, : 3 * half].reshape(w_qkv.shape),
            body[:, dm.o_out : dm.o_up].T[None],
            body[:, dm.o_up : dm.o_down][None],
            body[:, dm.o_down :].T[None],
            small[6:8][None],
            up[None],
            small[0:2][None],
            small[2:6][None],
        ]
    return (acts[None], in_grads[None], *grads)


def solution(mesh):
    both = ("tensor", "fsdp")
    params = (
        P("section", "fsdp", None, "tensor"),
        P("section", "tensor", "fsdp"),
        P("section", "fsdp", "tensor"),
        P("section", "tensor", "fsdp"),
        P("section", None, both),
        P("section", both),
        P("section", None, both),
        P("section", None, both),
    )
    images = P(None, ("fsdp", "tensor"), None, None)
    layered = P("section", None, ("fsdp", "tensor"), None, None)
    return jax.shard_map(
        per_device,
        mesh=mesh,
        in_specs=(images, images, P(None, "fsdp")) + params,
        out_specs=(layered, layered) + params,
        check_vma=False,
    )
```

time: 162 us -> 101 us (0.62)
  between operations: 24.4 us -> 0.89 us
  local copies, waits for them, and re-layouts: 27.7 us -> 8.74 us
  Pallas kernels: 24.1 us -> 13.6 us
  waiting for transfers between devices: 55.9 us -> 51.4 us
  starting transfers between devices: 25.9 us -> 24.1 us
    unnamed x74 -> x19, local copies, waits for them, and re-layouts: 25 us -> 6.63 us
    pallas_call x5 -> x4, Pallas kernels: 24.1 us -> 13.6 us  [call(): pl.pallas_call(kernel, in_specs=ins, out_specs=[VM] * len(outs), out_shap...]
    ppermute x1, waiting for transfers between devices: 17.6 us -> 8.33 us  [per_device(): incoming = lax.ppermute(grad1, 'section', [(1, 0)])]
    ppermute x16, waiting for transfers between devices: 35.9 us -> 38.8 us  [shifted(): lax.ppermute(value, 'fsdp', [(cycle[i], cycle[(i + step) % count]) for i...]
    convert_element_type x6, other arithmetic: 2.81 us -> 0.62 us  [part(): return sum((v.astype(F32) for v in terms)).astype(BF)]
    ppermute x1 -> x2, waiting for transfers between devices: 0.01 us -> 2.08 us  [the longest x1 2.07 us: reduce_ring(): far_part = lax.ppermute(other[split:], 'tensor', swap)]
    dynamic_slice x2 -> x0, local copies, waits for them, and re-layouts: 1.88 us -> none  [the longest x1 1.24 us: per_device(): place = jnp.array(inverse, jnp.int32)[lax.axis_index('fsdp')]]
  transfers between devices with their start and end apart: 27 -> 29, of which waited for: 12 -> 17; matrix products, arithmetic and copies ran while one was open for 4% -> 4% of each run, Pallas kernels for 0% -> 0%
where the time goes in v2:
time: 101 us
  waiting for transfers between devices  51.4 us (51%)
  starting transfers between devices  24.1 us (24%)
  Pallas kernels  13.6 us (13%)
  local copies, waits for them, and re-layouts  8.74 us (9%)
  other arithmetic  2.02 us (2%)
    ppermute x16, waiting for transfers between devices, shifted(): lax.ppermute(value, 'fsdp', [(cycle[i], cycle[(i + step) % count]) for i...  38.8 us
    ppermute x16, starting transfers between devices, shifted(): lax.ppermute(value, 'fsdp', [(cycle[i], cycle[(i + step) % count]) for i...  17.6 us
    pallas_call x4, Pallas kernels, call(): pl.pallas_call(kernel, in_specs=ins, out_specs=[VM] * len(outs), out_shap...  13.6 us
    ppermute x1, waiting for transfers between devices, per_device(): incoming = lax.ppermute(grad1, 'section', [(1, 0)])  8.33 us
    unnamed x19, local copies, waits for them, and re-layouts  6.63 us
    ppermute x1, starting transfers between devices, per_device(): h1 = lax.ppermute(low0, 'section', [(0, 1)])  4.05 us
    ppermute x1, waiting for transfers between devices, reduce_ring(): far_part = lax.ppermute(other[split:], 'tensor', swap)  2.07 us
  transfers between devices with their start and end apart: 29, of which 17 were waited for; matrix products, arithmetic and copies ran while one was open for 4% of the time, Pallas kernels for 0%

profile of v2, /device:TPU:0, one launch (start us, length us, event | category | flops | bytes accessed | tf_op | source)
XLA Modules:
  0.0 100.7 jit_solution(8245084316659567296)
XLA Ops:
  0.6 0.8 slice_bitcast_fusion.8
  1.4 0.7 fusion.10
  2.1 0.7 fusion.5
  2.8 1.0 %concatenate.17.refs_0_ = bf16[48,2432]{1,0:T(8,128)(2,1)S(1)} concatenate(bf16[48,192]{1,0:T(8,128)(2,1)S(1)} %get-tuple-element.126, bf16[48,192]{1,0:T(8,128)(2,1)S(1)} %get-tuple-element.127, bf16[48,192]{1,0:T(8,128)(2,1)S(1)} %get-tuple-element.125, bf16[48,192]{1,0:T(8,128)(2,1)} %bitcast.64, bf16[48,768]{1,0:T(8,128)(2,1)} %bitcast.62, bf16[48,768]{1,0:T(8,128)(2,1)} %bitcast.63, ...), dimensions={1} | concatenate | bytes 466944 | tf_op jit(solution)/shard_map/concatenate | solution.py:492
  3.8 3.1 %collective-permute-start.1 = (bf16[48,2432]{1,0:T(8,128)(2,1)S(1)}, bf16[48,2432]{1,0:T(8,128)(2,1)S(1)}, u32[]{:S(2)}, u32[]{:S(2)}) collective-permute-start(bf16[48,2432]{1,0:T(8,128)(2,1)S(1)} %concatenate.17.refs_0_), channel_id=1, source_target_pairs={{0,2},{1,0},{3,1},{5,3},{7,5},{6,7},{4,6},{2,4},{8,10},{9,8},{11,9... | collective-permute-start | bytes 700424 | tf_op jit(solution)/shard_map/ppermute | solution.py:427
  6.9 5.6 %collective-permute-done.1.refs_2_ = bf16[48,2432]{1,0:T(8,128)(2,1)S(1)} collective-permute-done((bf16[48,2432]{1,0:T(8,128)(2,1)S(1)}, bf16[48,2432]{1,0:T(8,128)(2,1)S(1)}, u32[]{:S(2)}, u32[]{:S(2)}) %collective-permute-start.1) | collective-permute-done | bytes 233504 | tf_op jit(solution)/shard_map/ppermute | solution.py:427
  12.5 1.8 %collective-permute-start.3 = (bf16[48,2432]{1,0:T(8,128)(2,1)S(1)}, bf16[48,2432]{1,0:T(8,128)(2,1)S(1)}, u32[]{:S(2)}, u32[]{:S(2)}) collective-permute-start(bf16[48,2432]{1,0:T(8,128)(2,1)S(1)} %collective-permute-done.1.refs_2_), channel_id=1, source_target_pairs={{0,2},{1,0},{3,1},{5,3},{7,5},{6,7},{4,6},{2,4},{8,10},{9,8},{11,9... | collective-permute-start | bytes 700424 | tf_op jit(solution)/shard_map/ppermute | solution.py:427
  14.6 4.8 %collective-permute-done.3.refs_4_ = bf16[48,2432]{1,0:T(8,128)(2,1)S(1)} collective-permute-done((bf16[48,2432]{1,0:T(8,128)(2,1)S(1)}, bf16[48,2432]{1,0:T(8,128)(2,1)S(1)}, u32[]{:S(2)}, u32[]{:S(2)}) %collective-permute-start.3) | collective-permute-done | bytes 233504 | tf_op jit(solution)/shard_map/ppermute | solution.py:427
  19.4 1.5 %collective-permute-start.5 = (bf16[48,2432]{1,0:T(8,128)(2,1)S(1)}, bf16[48,2432]{1,0:T(8,128)(2,1)S(1)}, u32[]{:S(2)}, u32[]{:S(2)}) collective-permute-start(bf16[48,2432]{1,0:T(8,128)(2,1)S(1)} %collective-permute-done.3.refs_4_), channel_id=1, source_target_pairs={{0,2},{1,0},{3,1},{5,3},{7,5},{6,7},{4,6},{2,4},{8,10},{9,8},{11,9... | collective-permute-start | bytes 700424 | tf_op jit(solution)/shard_map/ppermute | solution.py:427
  20.9 0.5 collective-permute-start.10
  21.4 0.5 collective-permute-start.4
  22.0 3.5 %collective-permute-done.5.refs_6_ = bf16[48,2432]{1,0:T(8,128)(2,1)S(1)} collective-permute-done((bf16[48,2432]{1,0:T(8,128)(2,1)S(1)}, bf16[48,2432]{1,0:T(8,128)(2,1)S(1)}, u32[]{:S(2)}, u32[]{:S(2)}) %collective-permute-start.5) | collective-permute-done | bytes 233504 | tf_op jit(solution)/shard_map/ppermute | solution.py:427
  25.5 1.5 %collective-permute-start.7 = (bf16[48,1280]{1,0:T(8,128)(2,1)S(1)}, bf16[48,1280]{1,0:T(8,128)(2,1)S(1)}, u32[]{:S(2)}, u32[]{:S(2)}) collective-permute-start(bf16[48,1280]{1,0:T(8,128)(2,1)S(1)} %slice.147), channel_id=1, source_target_pairs={{0,2},{1,0},{3,1},{5,3},{7,5},{6,7},{4,6},{2,4},{8,10},{9,8},{11,9... | collective-permute-start | bytes 368648 | tf_op jit(solution)/shard_map/ppermute | solution.py:427
  27.6 2.0 %collective-permute-done.4.refs_5_ = bf16[48,2432]{1,0:T(8,128)(2,1)S(1)} collective-permute-done((bf16[48,2432]{1,0:T(8,128)(2,1)S(1)}, bf16[48,2432]{1,0:T(8,128)(2,1)S(1)}, u32[]{:S(2)}, u32[]{:S(2)}) %collective-permute-start.4) | collective-permute-done | bytes 233504 | tf_op jit(solution)/shard_map/ppermute | solution.py:427
  29.6 0.6 collective-permute-start.6
  30.2 1.1 %collective-permute-done.7.refs_8_ = bf16[48,1280]{1,0:T(8,128)(2,1)S(1)} collective-permute-done((bf16[48,1280]{1,0:T(8,128)(2,1)S(1)}, bf16[48,1280]{1,0:T(8,128)(2,1)S(1)}, u32[]{:S(2)}, u32[]{:S(2)}) %collective-permute-start.7) | collective-permute-done | bytes 122912 | tf_op jit(solution)/shard_map/ppermute | solution.py:427
  31.3 3.8 %collective-permute-done.6.refs_7_ = bf16[48,1152]{1,0:T(8,128)(2,1)S(1)} collective-permute-done((bf16[48,1152]{1,0:T(8,128)(2,1)S(1)}, bf16[48,1152]{1,0:T(8,128)(2,1)S(1)}, u32[]{:S(2)}, u32[]{:S(2)}) %collective-permute-start.6) | collective-permute-done | bytes 110624 | tf_op jit(solution)/shard_map/ppermute | solution.py:427
  35.1 0.9 copy.23.tokens
  36.4 0.9 copy-done.3
  37.4 4.8 %shard_map.186 = (bf16[2,384,2304]{2,1,0:T(8,128)(2,1)S(1)}, f32[16,384]{1,0:T(8,128)S(1)}, bf16[2,1,82,384]{3,2,1,0:T(8,128)(2,1)}) custom-call(bf16[2,1,82,384]{3,2,1,0:T(8,128)(2,1)S(1)} %copy.23.tokens, bf16[48,2432]{1,0:T(8,128)(2,1)S(1)} %copy-done.3, bf16[48,2432]{1,0:T(8,128)(2,1)S(1)} %collective-permute-done.refs_1_, ...), custom_call_target="tpu_custom_call" | custom-call | tf_op jit(solution)/shard_map/pallas_call | solution.py:415
  42.2 0.6 copy-done.4
  42.8 4.0 %collective-permute-start.17 = (bf16[2,1,82,384]{3,2,1,0:T(8,128)(2,1)}, bf16[2,1,82,384]{3,2,1,0:T(8,128)(2,1)}, u32[]{:S(2)}, u32[]{:S(2)}) collective-permute-start(bf16[2,1,82,384]{3,2,1,0:T(8,128)(2,1)} %get-tuple-element.57), channel_id=1, source_target_pairs={{0,16},{1,17},{2,18},{3,19},{4,20},{5,21},{6,22},{7,23},{8,24},{9,... | collective-permute-start | bytes 377864 | tf_op jit(solution)/shard_map/ppermute | solution.py:528
  47.0 0.9 copy.24.out_grad
  47.9 1.8 %collective-permute-done.17.h1 = bf16[2,1,82,384]{3,2,1,0:T(8,128)(2,1)} collective-permute-done((bf16[2,1,82,384]{3,2,1,0:T(8,128)(2,1)}, bf16[2,1,82,384]{3,2,1,0:T(8,128)(2,1)}, u32[]{:S(2)}, u32[]{:S(2)}) %collective-permute-start.17) | collective-permute-done | bytes 125984 | tf_op jit(solution)/shard_map/ppermute | solution.py:528
  49.7 0.9 copy-done.1
  50.6 0.7 copy-done.5
  51.3 3.6 %shard_map.187 = (bf16[2,1,82,384]{3,2,1,0:T(8,128)(2,1)S(1)}, bf16[2,1,82,384]{3,2,1,0:T(8,128)(2,1)S(1)}, f32[2,176,576]{2,1,0:T(8,128)S(1)}, f32[12,88,88]{2,...) custom-call(s32[2,1]{1,0:T(2,128)S(1)} %copy.22.count_ref, ...), custom_call_target="tpu_custom_call" | custom-call | tf_op jit(solution)/shard_map/pallas_call | solution.py:415
  54.9 1.3 %collective-permute-start.18 = (bf16[2,1,82,384]{3,2,1,0:T(8,128)(2,1)S(1)}, bf16[2,1,82,384]{3,2,1,0:T(8,128)(2,1)S(1)}, u32[]{:S(2)}, u32[]{:S(2)}) collective-permute-start(bf16[2,1,82,384]{3,2,1,0:T(8,128)(2,1)S(1)} %get-tuple-element.61.own), channel_id=1, source_target_pairs={{16,0},{17,1},{18,2},{19,3},{20,4},{21,5},{22,6},{23,7},{24,8},{25... | collective-permute-start | bytes 377864 | tf_op jit(solution)/shard_map/ppermute | solution.py:537
  56.2 8.3 %collective-permute-done.18.incoming = bf16[2,1,82,384]{3,2,1,0:T(8,128)(2,1)S(1)} collective-permute-done((bf16[2,1,82,384]{3,2,1,0:T(8,128)(2,1)S(1)}, bf16[2,1,82,384]{3,2,1,0:T(8,128)(2,1)S(1)}, u32[]{:S(2)}, u32[]{:S(2)}) %collective-permute-start.18) | collective-permute-done | bytes 125984 | tf_op jit(solution)/shard_map/ppermute | solution.py:537
  64.6 4.3 %shard_map.188 = (bf16[2,1,82,384]{3,2,1,0:T(8,128)(2,1)S(1)}, bf16[8,48,2432]{2,1,0:T(8,128)(2,1)S(1)}, bf16[8,48,2432]{2,1,0:T(8,128)(2,1)S(1)}) custom-call(bf16[2,1,82,384]{3,2,1,0:T(8,128)(2,1)S(1)} %collective-permute-done.18.incoming, bf16[2,384,2304]{2,1,0:T(8,128)(2,1)S(1)} %get-tuple-element.58.w, f32[16,384]{1,0:T(8,128)S(1)} %copy-done.5, ...), custom_call_target="tpu_custom_call" | custom-call | tf_op jit(solution)/shard_map/pallas_call | solution.py:415
  69.1 2.1 %collective-permute-done.20 = bf16[3,48,2432]{2,1,0:T(8,128)(2,1)S(1)} collective-permute-done((bf16[3,48,2432]{2,1,0:T(8,128)(2,1)S(1)}, bf16[3,48,2432]{2,1,0:T(8,128)(2,1)S(1)}, u32[]{:S(2)}, u32[]{:S(2)}) %collective-permute-start.20) | collective-permute-done | bytes 700448 | tf_op jit(solution)/shard_map/ppermute | solution.py:454
  71.3 1.7 %collective-permute-start.22 = (bf16[48,1280]{1,0:T(8,128)(2,1)S(1)}, bf16[48,1280]{1,0:T(8,128)(2,1)S(1)}, u32[]{:S(2)}, u32[]{:S(2)}) collective-permute-start(bf16[48,1280]{1,0:T(8,128)(2,1)S(1)} %add_convert_fusion.2), channel_id=1, source_target_pairs={{0,2},{1,0},{3,1},{5,3},{7,5},{6,7},{4,6},{2,4},{8,10},{9,8},{11,9... | collective-permute-start | bytes 368648 | tf_op jit(solution)/shard_map/ppermute | solution.py:427
  73.0 0.4 collective-permute-start.21
  73.6 4.2 %collective-permute-done.21 = bf16[48,1152]{1,0:T(8,128)(2,1)S(1)} collective-permute-done((bf16[48,1152]{1,0:T(8,128)(2,1)S(1)}, bf16[48,1152]{1,0:T(8,128)(2,1)S(1)}, u32[]{:S(2)}, u32[]{:S(2)}) %collective-permute-start.21) | collective-permute-done | bytes 110624 | tf_op jit(solution)/shard_map/ppermute | solution.py:427
  78.1 0.5 collective-permute-start.23
  78.5 1.6 %collective-permute-start.24 = (bf16[48,2432]{1,0:T(8,128)(2,1)S(1)}, bf16[48,2432]{1,0:T(8,128)(2,1)S(1)}, u32[]{:S(2)}, u32[]{:S(2)}) collective-permute-start(bf16[48,2432]{1,0:T(8,128)(2,1)S(1)} %pad_maximum_fusion.1), channel_id=1, source_target_pairs={{0,2},{1,0},{3,1},{5,3},{7,5},{6,7},{4,6},{2,4},{8,10},{9,8},{11,9... | collective-permute-start | bytes 700424 | tf_op jit(solution)/shard_map/ppermute | solution.py:427
  80.1 4.6 %collective-permute-done.23 = bf16[48,2432]{1,0:T(8,128)(2,1)S(1)} collective-permute-done((bf16[48,2432]{1,0:T(8,128)(2,1)S(1)}, bf16[48,2432]{1,0:T(8,128)(2,1)S(1)}, u32[]{:S(2)}, u32[]{:S(2)}) %collective-permute-start.23) | collective-permute-done | bytes 233504 | tf_op jit(solution)/shard_map/ppermute | solution.py:427
  85.0 0.9 collective-permute-start.25
  85.9 1.2 %collective-permute-start.26 = (bf16[48,2432]{1,0:T(8,128)(2,1)S(1)}, bf16[48,2432]{1,0:T(8,128)(2,1)S(1)}, u32[]{:S(2)}, u32[]{:S(2)}) collective-permute-start(bf16[48,2432]{1,0:T(8,128)(2,1)S(1)} %get-tuple-element.89), channel_id=1, source_target_pairs={{0,2},{1,0},{3,1},{5,3},{7,5},{6,7},{4,6},{2,4},{8,10},{9,8},{11,9... | collective-permute-start | bytes 700424 | tf_op jit(solution)/shard_map/ppermute | solution.py:427
  87.1 0.7 copy.25
  87.9 0.7 copy.26
  88.6 2.5 %collective-permute-done.25 = bf16[48,2432]{1,0:T(8,128)(2,1)S(1)} collective-permute-done((bf16[48,2432]{1,0:T(8,128)(2,1)S(1)}, bf16[48,2432]{1,0:T(8,128)(2,1)S(1)}, u32[]{:S(2)}, u32[]{:S(2)}) %collective-permute-start.25) | collective-permute-done | bytes 233504 | tf_op jit(solution)/shard_map/ppermute | solution.py:427
  91.1 0.8 collective-permute-done.26
  92.2 1.6 %collective-permute-start.27 = (bf16[48,2432]{1,0:T(8,128)(2,1)S(1)}, bf16[48,2432]{1,0:T(8,128)(2,1)S(1)}, u32[]{:S(2)}, u32[]{:S(2)}) collective-permute-start(bf16[48,2432]{1,0:T(8,128)(2,1)S(1)} %get-tuple-element.92), channel_id=1, source_target_pairs={{0,1},{1,3},{3,5},{5,7},{7,6},{6,4},{4,2},{2,0},{8,9},{9,11},{11,1... | collective-permute-start | bytes 700424 | tf_op jit(solution)/shard_map/ppermute | solution.py:427
  93.8 0.4 collective-permute-start.28
  94.3 4.0 %collective-permute-done.27.refs_2_ = bf16[48,2432]{1,0:T(8,128)(2,1)S(1)} collective-permute-done((bf16[48,2432]{1,0:T(8,128)(2,1)S(1)}, bf16[48,2432]{1,0:T(8,128)(2,1)S(1)}, u32[]{:S(2)}, u32[]{:S(2)}) %collective-permute-start.27) | collective-permute-done | bytes 233504 | tf_op jit(solution)/shard_map/ppermute | solution.py:427
  98.3 1.6 %collective-permute-done.28.refs_3_ = bf16[48,2432]{1,0:T(8,128)(2,1)S(1)} collective-permute-done((bf16[48,2432]{1,0:T(8,128)(2,1)S(1)}, bf16[48,2432]{1,0:T(8,128)(2,1)S(1)}, u32[]{:S(2)}, u32[]{:S(2)}) %collective-permute-start.28) | collective-permute-done | bytes 233504 | tf_op jit(solution)/shard_map/ppermute | solution.py:427
  99.9 0.9 shard_map.189
  (52 shorter events, 2.5 us)
Async XLA Ops:
  3.8 32.6 %copy-start.2 = (bf16[48,2432]{1,0:T(8,128)(2,1)}, bf16[48,2432]{1,0:T(8,128)(2,1)S(1)}, u32[]{:S(2)}) copy-start(bf16[48,2432]{1,0:T(8,128)(2,1)S(1)} %concatenate.17.refs_0_) | copy-start | bytes 700420
  3.8 8.7 %collective-permute-start.1 = (bf16[48,2432]{1,0:T(8,128)(2,1)S(1)}, bf16[48,2432]{1,0:T(8,128)(2,1)S(1)}, u32[]{:S(2)}, u32[]{:S(2)}) collective-permute-start(bf16[48,2432]{1,0:T(8,128)(2,1)S(1)} %concatenate.17.refs_0_), channel_id=1, source_target_pairs={{0,2},{1,0},{3,1},{5,3},{7,5},{6,7},{4,6},{2,4},{8,10},{9,8},{11,9... | collective-permute-start | bytes 700424 | tf_op jit(solution)/shard_map/ppermute | solution.py:427
  6.9 7.4 %collective-permute-start = (bf16[48,2432]{1,0:T(8,128)(2,1)S(1)}, bf16[48,2432]{1,0:T(8,128)(2,1)S(1)}, u32[]{:S(2)}, u32[]{:S(2)}) collective-permute-start(bf16[48,2432]{1,0:T(8,128)(2,1)S(1)} %concatenate.17.refs_0_), channel_id=1, source_target_pairs={{0,1},{1,3},{3,5},{5,7},{7,6},{6,4},{4,2},{2,0},{8,9},{9,11},{11,1... | collective-permute-start | bytes 700424 | tf_op jit(solution)/shard_map/ppermute | solution.py:427
  12.5 6.9 %collective-permute-start.3 = (bf16[48,2432]{1,0:T(8,128)(2,1)S(1)}, bf16[48,2432]{1,0:T(8,128)(2,1)S(1)}, u32[]{:S(2)}, u32[]{:S(2)}) collective-permute-start(bf16[48,2432]{1,0:T(8,128)(2,1)S(1)} %collective-permute-done.1.refs_2_), channel_id=1, source_target_pairs={{0,2},{1,0},{3,1},{5,3},{7,5},{6,7},{4,6},{2,4},{8,10},{9,8},{11,9... | collective-permute-start | bytes 700424 | tf_op jit(solution)/shard_map/ppermute | solution.py:427
  14.3 7.1 %collective-permute-start.2 = (bf16[48,2432]{1,0:T(8,128)(2,1)S(1)}, bf16[48,2432]{1,0:T(8,128)(2,1)S(1)}, u32[]{:S(2)}, u32[]{:S(2)}) collective-permute-start(bf16[48,2432]{1,0:T(8,128)(2,1)S(1)} %collective-permute-done.refs_1_), channel_id=1, source_target_pairs={{0,1},{1,3},{3,5},{5,7},{7,6},{6,4},{4,2},{2,0},{8,9},{9,11},{11,1... | collective-permute-start | bytes 700424 | tf_op jit(solution)/shard_map/ppermute | solution.py:427
  19.4 6.1 %collective-permute-start.5 = (bf16[48,2432]{1,0:T(8,128)(2,1)S(1)}, bf16[48,2432]{1,0:T(8,128)(2,1)S(1)}, u32[]{:S(2)}, u32[]{:S(2)}) collective-permute-start(bf16[48,2432]{1,0:T(8,128)(2,1)S(1)} %collective-permute-done.3.refs_4_), channel_id=1, source_target_pairs={{0,2},{1,0},{3,1},{5,3},{7,5},{6,7},{4,6},{2,4},{8,10},{9,8},{11,9... | collective-permute-start | bytes 700424 | tf_op jit(solution)/shard_map/ppermute | solution.py:427
  20.9 4.6 %collective-permute-start.8 = (bf16[48,2432]{1,0:T(8,128)(2,1)S(1)}, bf16[48,2432]{1,0:T(8,128)(2,1)S(1)}, u32[]{:S(2)}, u32[]{:S(2)}) collective-permute-start(bf16[48,2432]{1,0:T(8,128)(2,1)S(1)} %concatenate.17.refs_0_), channel_id=1, source_target_pairs={{0,8},{8,0},{1,9},{9,1},{2,10},{10,2},{3,11},{11,3},{4,12},{12,4},... | collective-permute-start | bytes 700424 | tf_op jit(solution)/shard_map/ppermute | solution.py:514
  20.9 6.1 %collective-permute-start.10 = (bf16[48,2432]{1,0:T(8,128)(2,1)S(1)}, bf16[48,2432]{1,0:T(8,128)(2,1)S(1)}, u32[]{:S(2)}, u32[]{:S(2)}) collective-permute-start(bf16[48,2432]{1,0:T(8,128)(2,1)S(1)} %collective-permute-done.1.refs_2_), channel_id=1, source_target_pairs={{0,8},{8,0},{1,9},{9,1},{2,10},{10,2},{3,11},{11,3},{4,12},{12,4},... | collective-permute-start | bytes 700424 | tf_op jit(solution)/shard_map/ppermute | solution.py:514
  21.4 5.9 %collective-permute-start.9 = (bf16[48,2432]{1,0:T(8,128)(2,1)S(1)}, bf16[48,2432]{1,0:T(8,128)(2,1)S(1)}, u32[]{:S(2)}, u32[]{:S(2)}) collective-permute-start(bf16[48,2432]{1,0:T(8,128)(2,1)S(1)} %collective-permute-done.refs_1_), channel_id=1, source_target_pairs={{0,8},{8,0},{1,9},{9,1},{2,10},{10,2},{3,11},{11,3},{4,12},{12,4},... | collective-permute-start | bytes 700424 | tf_op jit(solution)/shard_map/ppermute | solution.py:514
  21.4 8.1 %collective-permute-start.4 = (bf16[48,2432]{1,0:T(8,128)(2,1)S(1)}, bf16[48,2432]{1,0:T(8,128)(2,1)S(1)}, u32[]{:S(2)}, u32[]{:S(2)}) collective-permute-start(bf16[48,2432]{1,0:T(8,128)(2,1)S(1)} %collective-permute-done.2.refs_3_), channel_id=1, source_target_pairs={{0,1},{1,3},{3,5},{5,7},{7,6},{6,4},{4,2},{2,0},{8,9},{9,11},{11,1... | collective-permute-start | bytes 700424 | tf_op jit(solution)/shard_map/ppermute | solution.py:427
  25.5 4.1 %collective-permute-start.12 = (bf16[48,2432]{1,0:T(8,128)(2,1)S(1)}, bf16[48,2432]{1,0:T(8,128)(2,1)S(1)}, u32[]{:S(2)}, u32[]{:S(2)}) collective-permute-start(bf16[48,2432]{1,0:T(8,128)(2,1)S(1)} %collective-permute-done.3.refs_4_), channel_id=1, source_target_pairs={{0,8},{8,0},{1,9},{9,1},{2,10},{10,2},{3,11},{11,3},{4,12},{12,4},... | collective-permute-start | bytes 700424 | tf_op jit(solution)/shard_map/ppermute | solution.py:514
  25.5 5.8 %collective-permute-start.7 = (bf16[48,1280]{1,0:T(8,128)(2,1)S(1)}, bf16[48,1280]{1,0:T(8,128)(2,1)S(1)}, u32[]{:S(2)}, u32[]{:S(2)}) collective-permute-start(bf16[48,1280]{1,0:T(8,128)(2,1)S(1)} %slice.147), channel_id=1, source_target_pairs={{0,2},{1,0},{3,1},{5,3},{7,5},{6,7},{4,6},{2,4},{8,10},{9,8},{11,9... | collective-permute-start | bytes 368648 | tf_op jit(solution)/shard_map/ppermute | solution.py:427
  27.1 9.0 %collective-permute-start.11 = (bf16[48,2432]{1,0:T(8,128)(2,1)S(1)}, bf16[48,2432]{1,0:T(8,128)(2,1)S(1)}, u32[]{:S(2)}, u32[]{:S(2)}) collective-permute-start(bf16[48,2432]{1,0:T(8,128)(2,1)S(1)} %collective-permute-done.2.refs_3_), channel_id=1, source_target_pairs={{0,8},{8,0},{1,9},{9,1},{2,10},{10,2},{3,11},{11,3},{4,12},{12,4},... | collective-permute-start | bytes 700424 | tf_op jit(solution)/shard_map/ppermute | solution.py:514
  27.3 9.1 %collective-permute-start.14 = (bf16[48,2432]{1,0:T(8,128)(2,1)S(1)}, bf16[48,2432]{1,0:T(8,128)(2,1)S(1)}, u32[]{:S(2)}, u32[]{:S(2)}) collective-permute-start(bf16[48,2432]{1,0:T(8,128)(2,1)S(1)} %collective-permute-done.5.refs_6_), channel_id=1, source_target_pairs={{0,8},{8,0},{1,9},{9,1},{2,10},{10,2},{3,11},{11,3},{4,12},{12,4},... | collective-permute-start | bytes 700424 | tf_op jit(solution)/shard_map/ppermute | solution.py:514
  29.5 6.9 %collective-permute-start.13 = (bf16[48,2432]{1,0:T(8,128)(2,1)S(1)}, bf16[48,2432]{1,0:T(8,128)(2,1)S(1)}, u32[]{:S(2)}, u32[]{:S(2)}) collective-permute-start(bf16[48,2432]{1,0:T(8,128)(2,1)S(1)} %collective-permute-done.4.refs_5_), channel_id=1, source_target_pairs={{0,8},{8,0},{1,9},{9,1},{2,10},{10,2},{3,11},{11,3},{4,12},{12,4},... | collective-permute-start | bytes 700424 | tf_op jit(solution)/shard_map/ppermute | solution.py:514
  29.6 5.5 %collective-permute-start.6 = (bf16[48,1152]{1,0:T(8,128)(2,1)S(1)}, bf16[48,1152]{1,0:T(8,128)(2,1)S(1)}, u32[]{:S(2)}, u32[]{:S(2)}) collective-permute-start(bf16[48,1152]{1,0:T(8,128)(2,1)S(1)} %slice.146), channel_id=1, source_target_pairs={{0,1},{1,3},{3,5},{5,7},{7,6},{6,4},{4,2},{2,0},{8,9},{9,11},{11,1... | collective-permute-start | bytes 331784 | tf_op jit(solution)/shard_map/ppermute | solution.py:427
  31.3 5.1 %collective-permute-start.16 = (bf16[48,1280]{1,0:T(8,128)(2,1)S(1)}, bf16[48,1280]{1,0:T(8,128)(2,1)S(1)}, u32[]{:S(2)}, u32[]{:S(2)}) collective-permute-start(bf16[48,1280]{1,0:T(8,128)(2,1)S(1)} %collective-permute-done.7.refs_8_), channel_id=1, source_target_pairs={{0,8},{8,0},{1,9},{9,1},{2,10},{10,2},{3,11},{11,3},{4,12},{12,4},... | collective-permute-start | bytes 368648 | tf_op jit(solution)/shard_map/ppermute | solution.py:514
  35.1 1.3 %collective-permute-start.15 = (bf16[48,1152]{1,0:T(8,128)(2,1)S(1)}, bf16[48,1152]{1,0:T(8,128)(2,1)S(1)}, u32[]{:S(2)}, u32[]{:S(2)}) collective-permute-start(bf16[48,1152]{1,0:T(8,128)(2,1)S(1)} %collective-permute-done.6.refs_7_), channel_id=1, source_target_pairs={{0,8},{8,0},{1,9},{9,1},{2,10},{10,2},{3,11},{11,3},{4,12},{12,4},... | collective-permute-start | bytes 331784 | tf_op jit(solution)/shard_map/ppermute | solution.py:514
  35.1 11.8 %copy-start.6 = (s32[2,1]{0,1:T(1,128)S(1)}, s32[2,1]{0,1:T(1,128)}, u32[]{:S(2)}) copy-start(s32[2,1]{0,1:T(1,128)} %param.13) | copy-start | bytes 28
  36.0 6.2 %copy-start = (bf16[2,1,82,384]{3,2,1,0:T(8,128)(2,1)}, bf16[2,1,82,384]{3,2,1,0:T(8,128)(2,1)S(1)}, u32[]{:S(2)}) copy-start(bf16[2,1,82,384]{3,2,1,0:T(8,128)(2,1)S(1)} %copy.23.tokens) | copy-start | bytes 377860
  36.4 0.9 copy-start.3
  42.2 0.6 copy-start.4
  42.8 6.9 %collective-permute-start.17 = (bf16[2,1,82,384]{3,2,1,0:T(8,128)(2,1)}, bf16[2,1,82,384]{3,2,1,0:T(8,128)(2,1)}, u32[]{:S(2)}, u32[]{:S(2)}) collective-permute-start(bf16[2,1,82,384]{3,2,1,0:T(8,128)(2,1)} %get-tuple-element.57), channel_id=1, source_target_pairs={{0,16},{1,17},{2,18},{3,19},{4,20},{5,21},{6,22},{7,23},{8,24},{9,... | collective-permute-start | bytes 377864 | tf_op jit(solution)/shard_map/ppermute | solution.py:528
  49.7 0.9 copy-start.1
  50.6 0.7 copy-start.5
  54.9 9.6 %collective-permute-start.18 = (bf16[2,1,82,384]{3,2,1,0:T(8,128)(2,1)S(1)}, bf16[2,1,82,384]{3,2,1,0:T(8,128)(2,1)S(1)}, u32[]{:S(2)}, u32[]{:S(2)}) collective-permute-start(bf16[2,1,82,384]{3,2,1,0:T(8,128)(2,1)S(1)} %get-tuple-element.61.own), channel_id=1, source_target_pairs={{16,0},{17,1},{18,2},{19,3},{20,4},{21,5},{22,6},{23,7},{24,8},{25... | collective-permute-start | bytes 377864 | tf_op jit(solution)/shard_map/ppermute | solution.py:537
  69.0 2.2 %collective-permute-start.20 = (bf16[3,48,2432]{2,1,0:T(8,128)(2,1)S(1)}, bf16[3,48,2432]{2,1,0:T(8,128)(2,1)S(1)}, u32[]{:S(2)}, u32[]{:S(2)}) collective-permute-start(bf16[3,48,2432]{2,1,0:T(8,128)(2,1)S(1)} %slice.125), channel_id=1, source_target_pairs={{0,8},{8,0},{1,9},{9,1},{2,10},{10,2},{3,11},{11,3},{4,12},{12,4},... | collective-permute-start | bytes 2101256 | tf_op jit(solution)/shard_map/ppermute | solution.py:454
  71.3 6.5 %collective-permute-start.22 = (bf16[48,1280]{1,0:T(8,128)(2,1)S(1)}, bf16[48,1280]{1,0:T(8,128)(2,1)S(1)}, u32[]{:S(2)}, u32[]{:S(2)}) collective-permute-start(bf16[48,1280]{1,0:T(8,128)(2,1)S(1)} %add_convert_fusion.2), channel_id=1, source_target_pairs={{0,2},{1,0},{3,1},{5,3},{7,5},{6,7},{4,6},{2,4},{8,10},{9,8},{11,9... | collective-permute-start | bytes 368648 | tf_op jit(solution)/shard_map/ppermute | solution.py:427
  73.0 4.8 %collective-permute-start.21 = (bf16[48,1152]{1,0:T(8,128)(2,1)S(1)}, bf16[48,1152]{1,0:T(8,128)(2,1)S(1)}, u32[]{:S(2)}, u32[]{:S(2)}) collective-permute-start(bf16[48,1152]{1,0:T(8,128)(2,1)S(1)} %add_convert_fusion.5), channel_id=1, source_target_pairs={{0,1},{1,3},{3,5},{5,7},{7,6},{6,4},{4,2},{2,0},{8,9},{9,11},{11,1... | collective-permute-start | bytes 331784 | tf_op jit(solution)/shard_map/ppermute | solution.py:427
  73.5 11.3 %collective-permute-start.19 = (bf16[5,48,2432]{2,1,0:T(8,128)(2,1)S(1)}, bf16[5,48,2432]{2,1,0:T(8,128)(2,1)S(1)}, u32[]{:S(2)}, u32[]{:S(2)}) collective-permute-start(bf16[5,48,2432]{2,1,0:T(8,128)(2,1)S(1)} %slice.117), channel_id=1, source_target_pairs={{0,8},{8,0},{1,9},{9,1},{2,10},{10,2},{3,11},{11,3},{4,12},{12,4},... | collective-permute-start | bytes 3502088 | tf_op jit(solution)/shard_map/ppermute | solution.py:455
  78.1 6.6 %collective-permute-start.23 = (bf16[48,2432]{1,0:T(8,128)(2,1)S(1)}, bf16[48,2432]{1,0:T(8,128)(2,1)S(1)}, u32[]{:S(2)}, u32[]{:S(2)}) collective-permute-start(bf16[48,2432]{1,0:T(8,128)(2,1)S(1)} %pad_maximum_fusion), channel_id=1, source_target_pairs={{0,1},{1,3},{3,5},{5,7},{7,6},{6,4},{4,2},{2,0},{8,9},{9,11},{11,1... | collective-permute-start | bytes 700424 | tf_op jit(solution)/shard_map/ppermute | solution.py:427
  78.5 6.3 %collective-permute-start.24 = (bf16[48,2432]{1,0:T(8,128)(2,1)S(1)}, bf16[48,2432]{1,0:T(8,128)(2,1)S(1)}, u32[]{:S(2)}, u32[]{:S(2)}) collective-permute-start(bf16[48,2432]{1,0:T(8,128)(2,1)S(1)} %pad_maximum_fusion.1), channel_id=1, source_target_pairs={{0,2},{1,0},{3,1},{5,3},{7,5},{6,7},{4,6},{2,4},{8,10},{9,8},{11,9... | collective-permute-start | bytes 700424 | tf_op jit(solution)/shard_map/ppermute | solution.py:427
  85.0 6.1 %collective-permute-start.25 = (bf16[48,2432]{1,0:T(8,128)(2,1)S(1)}, bf16[48,2432]{1,0:T(8,128)(2,1)S(1)}, u32[]{:S(2)}, u32[]{:S(2)}) collective-permute-start(bf16[48,2432]{1,0:T(8,128)(2,1)S(1)} %get-tuple-element.88), channel_id=1, source_target_pairs={{0,1},{1,3},{3,5},{5,7},{7,6},{6,4},{4,2},{2,0},{8,9},{9,11},{11,1... | collective-permute-start | bytes 700424 | tf_op jit(solution)/shard_map/ppermute | solution.py:427
  85.9 6.1 %collective-permute-start.26 = (bf16[48,2432]{1,0:T(8,128)(2,1)S(1)}, bf16[48,2432]{1,0:T(8,128)(2,1)S(1)}, u32[]{:S(2)}, u32[]{:S(2)}) collective-permute-start(bf16[48,2432]{1,0:T(8,128)(2,1)S(1)} %get-tuple-element.89), channel_id=1, source_target_pairs={{0,2},{1,0},{3,1},{5,3},{7,5},{6,7},{4,6},{2,4},{8,10},{9,8},{11,9... | collective-permute-start | bytes 700424 | tf_op jit(solution)/shard_map/ppermute | solution.py:427
  92.2 6.1 %collective-permute-start.27 = (bf16[48,2432]{1,0:T(8,128)(2,1)S(1)}, bf16[48,2432]{1,0:T(8,128)(2,1)S(1)}, u32[]{:S(2)}, u32[]{:S(2)}) collective-permute-start(bf16[48,2432]{1,0:T(8,128)(2,1)S(1)} %get-tuple-element.92), channel_id=1, source_target_pairs={{0,1},{1,3},{3,5},{5,7},{7,6},{6,4},{4,2},{2,0},{8,9},{9,11},{11,1... | collective-permute-start | bytes 700424 | tf_op jit(solution)/shard_map/ppermute | solution.py:427
  93.8 6.1 %collective-permute-start.28 = (bf16[48,2432]{1,0:T(8,128)(2,1)S(1)}, bf16[48,2432]{1,0:T(8,128)(2,1)S(1)}, u32[]{:S(2)}, u32[]{:S(2)}) collective-permute-start(bf16[48,2432]{1,0:T(8,128)(2,1)S(1)} %get-tuple-element.93), channel_id=1, source_target_pairs={{0,2},{1,0},{3,1},{5,3},{7,5},{6,7},{4,6},{2,4},{8,10},{9,8},{11,9... | collective-permute-start | bytes 700424 | tf_op jit(solution)/shard_map/ppermute | solution.py:427

commit v3 on v2

--- a/solution.py
+++ b/solution.py
@@ -17,7 +17,8 @@
 F32 = jnp.float32
 GRID_RING = (0, 1, 3, 5, 7, 6, 4, 2)
 RING_PLACE = tuple(GRID_RING.index(i) for i in range(len(GRID_RING)))
-NEAR = 2
+KEPT_OWN = (7, 6, 4, 2, 0, 9, 11, 13)
+KEPT_OTHER = (15, 5, 3, 1, 8, 10, 12, 14)
 ROW_STEP = 88
 EXT = 128
 
@@ -72,7 +73,10 @@
         self.cols = self.o_down + self.fh
         self.packed = self.cols + EXT
         self.rows = 2 * ROW_STEP
-        self.groups = width // 128
+        self.o_vecs = width
+        self.o_image = width + 16
+        self.o_grad = self.o_image + 96
+        self.w_rows = self.o_grad + 96
 
     def state_shapes(self):
         r, w = self.rows, self.width
@@ -114,8 +118,8 @@
                     yield (t * 2 + m) * self.heads + h, t, rows, h * HD
 
 
-def layer_forward(dm, state, w, vecs, st, keep, weights_ready=None):
-    half, fh = dm.half, dm.fh
+def forward_attention(dm, state, w, vecs, st, keep):
+    half = dm.half
     unit, factor = norm(state)
     first = (unit * vecs[0:1, :] + vecs[2:3, :]).astype(BF)
     if keep:
@@ -124,7 +128,7 @@
         st["first"][...] = first
     proj, mixed = st["proj"], st["mixed"]
     for t in range(2):
-        value = nn(first, w[t, :, 0 : 3 * half])
+        value = nn(first, w[t, 0 : dm.width, 0 : 3 * half])
         proj[t, :, 0:half] = value[:, 0:half] + vecs[6:7, t * half : (t + 1) * half]
         proj[t, :, half : 2 * half] = value[:, half : 2 * half]
         proj[t, :, 2 * half :] = value[:, 2 * half :] + vecs[7:8, t * half : (t + 1) * half]
@@ -141,7 +145,12 @@
         mixed[t, rows, c : c + HD] = nn(st["probs"][i].astype(BF), values.astype(BF))
     resid = state + vecs[3:4, :]
     for t in range(2):
-        resid += nt(mixed[t].astype(BF), w[t, :, dm.o_out : dm.o_out + half])
+        resid += nt(mixed[t].astype(BF), w[t, 0 : dm.width, dm.o_out : dm.o_out + half])
+    return resid
+
+
+def forward_mlp(dm, resid, w, vecs, st, keep):
+    fh = dm.fh
     unit, factor = norm(resid)
     second = (unit * vecs[1:2, :] + vecs[4:5, :]).astype(BF)
     if keep:
@@ -150,17 +159,15 @@
         st["second"][...] = second
     output = resid + vecs[5:6, :]
     per = fh // dm.width
-    if weights_ready is not None:
-        weights_ready()
     for t in range(2):
         bias = jnp.concatenate([vecs[8 + t * per + j : 9 + t * per + j, :] for j in range(per)], axis=1)
-        hidden = nn(second, w[t, :, dm.o_up : dm.o_up + fh]) + bias
+        hidden = nn(second, w[t, 0 : dm.width, dm.o_up : dm.o_up + fh]) + bias
         curve = 0.5 * (1.0 + lax.erf(hidden * INV_ROOT_TWO))
         active = (hidden * curve).astype(BF)
         if keep:
             st["slope"][t] = curve + hidden * jnp.exp(-0.5 * hidden * hidden) * INV_ROOT_TWO_PI
             st["active"][t] = active
-        output += nt(active, w[t, :, dm.o_down : dm.o_down + fh])
+        output += nt(active, w[t, 0 : dm.width, dm.o_down : dm.o_down + fh])
     return output
 
 
@@ -176,13 +183,13 @@
     per = fh // dm.width
     grad_second = None
     for t in range(2):
-        raw = nn(low, w[t, :, dm.o_down : dm.o_down + fh]) * st["slope"][t]
+        raw = nn(low, w[t, 0 : dm.width, dm.o_down : dm.o_down + fh]) * st["slope"][t]
         up_bias = total_rows(raw)
         for j in range(per):
             ct["vecs"][8 + t * per + j : 9 + t * per + j, :] = up_bias[:, j * dm.width : (j + 1) * dm.width]
         grad_hidden = raw.astype(BF)
         ct["hidden"][t] = grad_hidden
-        part = nt(grad_hidden, w[t, :, dm.o_up : dm.o_up + fh])
+        part = nt(grad_hidden, w[t, 0 : dm.width, dm.o_up : dm.o_up + fh])
         grad_second = part if grad_second is None else grad_second + part
     unit = st["unit_two"][...]
     gain_two, shift_two = total_rows(grad_second * unit), total_rows(grad_second)
@@ -192,7 +199,7 @@
     shift_attn = total_rows(low.astype(F32))
     proj, gproj, gmix, scores = st["proj"], ct["proj"], work["mixed"], work["scores"]
     for t in range(2):
-        gmix[t] = nn(low, w[t, :, dm.o_out : dm.o_out + half])
+        gmix[t] = nn(low, w[t, 0 : dm.width, dm.o_out : dm.o_out + half])
     for i, t, rows, c in dm.cells():
         values = proj[t, rows, 2 * half + c : 2 * half + c + HD].astype(BF)
         gm = gmix[t, rows, c : c + HD].astype(BF)
@@ -210,7 +217,7 @@
     for t in range(2):
         ct["vecs"][6:7, t * half : (t + 1) * half] = total_rows(gproj[t, :, 0:half])
         ct["vecs"][7:8, t * half : (t + 1) * half] = total_rows(gproj[t, :, 2 * half :])
-        part = nt(gproj[t].astype(BF), w[t, :, 0 : 3 * half])
+        part = nt(gproj[t].astype(BF), w[t, 0 : dm.width, 0 : 3 * half])
         grad_first = part if grad_first is None else grad_first + part
     unit = st["unit_one"][...]
     gain_one, shift_one = total_rows(grad_first * unit), total_rows(grad_first)
@@ -226,7 +233,7 @@
     def keep(t, column, value):
         for f in range(dm.shards):
             rows = value[f * block : (f + 1) * block].astype(BF)
-            grads[t][slots[f], :, column : column + value.shape[1]] = rows
+            grads[slots[t][f], :, column : column + value.shape[1]] = rows
 
     for t in range(2):
         keep(t, dm.o_down, tn(ct["branch"][...], st["active"][t]))
@@ -247,7 +254,7 @@
             up_piece = up[:, f * up_share : (f + 1) * up_share]
             up_piece = jnp.concatenate([up_piece, jnp.zeros((1, EXT - up_share), F32)], axis=1)
             piece = jnp.concatenate([piece, up_piece, jnp.zeros((block - 9, EXT), F32)], axis=0)
-            grads[t][slots[f], :, dm.cols :] = piece.astype(BF)
+            grads[slots[t][f], :, dm.cols :] = piece.astype(BF)
 
 
 def spread(dm, ref, get):
@@ -265,37 +272,48 @@
     return dict(zip(shapes, refs)), refs[len(shapes) :]
 
 
-def kernel_first(dm, layout, ring, tokens, *refs):
-    count = len(layout)
-    pieces, refs = refs[: 2 * count], refs[2 * count :]
-    w, vecs, out, proj, probs, mixed, rows, extra, sems = refs
+def kernel_first(dm, layout, ring, count_ref, tokens, out_grad, *refs):
+    pieces, refs = refs[:-8], refs[-8:]
+    w, out, proj, probs, mixed, rows, extra, sems = refs
     st = dict(proj=proj, probs=probs, mixed=mixed)
     block = dm.width // dm.shards
     early, late = [], []
     if ring:
         place = picked(RING_PLACE, lax.axis_index("fsdp"))
-    for t in range(2):
-        for i, (offset, start) in enumerate(layout):
-            piece = pieces[t * count + i]
-            if ring:
-                owner = picked([GRID_RING[(p + offset) % dm.shards] for p in range(dm.shards)], place)
-                where = pl.ds(pl.multiple_of(owner * block, 16), block)
-            else:
-                owner = offset
-                where = pl.ds(offset * block, block)
-            stop = start + piece.shape[1]
-            bounds = (0, dm.o_up, dm.cols, dm.packed)
-            for j in range(3):
-                lo, hi = max(start, bounds[j]), min(stop, bounds[j + 1])
-                if lo < hi:
-                    target = extra.at[t, owner] if j == 2 else w.at[t, where, pl.ds(lo, hi - lo)]
-                    copy = pltpu.make_async_copy(
-                        piece.at[:, pl.ds(lo - start, hi - lo)], target, sems.at[j, t * count + i]
-                    )
-                    (late if j == 1 else early).append(copy)
+    for n, (t, array, row, offset, start, stop) in enumerate(layout):
+        if ring:
+            owner = jnp.where(
+                lax.axis_index("tensor") == 0,
+                picked([GRID_RING[(p + offset) % dm.shards] for p in range(dm.shards)], place),
+                picked([GRID_RING[(p - offset) % dm.shards] for p in range(dm.shards)], place),
+            )
+            where = pl.ds(pl.multiple_of(owner * block, 16), block)
+        else:
+            owner = offset
+            where = pl.ds(offset * block, block)
+        bounds = (0, dm.o_up, dm.cols, dm.packed)
+        for j in range(3):
+            lo, hi = max(start, bounds[j]), min(stop, bounds[j + 1])
+            if lo < hi:
+                target = extra.at[t, owner] if j == 2 else w.at[t, where, pl.ds(lo, hi - lo)]
+                source = pieces[array].at[pl.ds(row, block), pl.ds(lo - start, hi - lo)]
+                copy = pltpu.make_async_copy(source, target, sems.at[j, n])
+                (late if j == 1 else early).append(copy)
     for copy in early + late:
         copy.start()
-    spread(dm, rows, lambda m: tokens[m, 0].astype(F32))
+    live = [live_of(count_ref, m) for m in range(2)]
+
+    def put(start):
+        for m in range(2):
+            value = jnp.concatenate([rows[m * ROW_STEP : (m + 1) * ROW_STEP, :], jnp.zeros((8, dm.width), F32)], axis=0)
+            w[m, start : start + 96, 0 : dm.width] = value.astype(BF)
+
+    value = out_grad[...].astype(F32)
+    spread(dm, rows, lambda m: value[:, m, :] * live[m])
+    put(dm.o_grad)
+    value = tokens[...].astype(F32)
+    spread(dm, rows, lambda m: value[:, m, :])
+    put(dm.o_image)
     for copy in early:
         copy.wait()
     share, up_share = dm.half // dm.shards, dm.fh // dm.shards
@@ -305,21 +323,33 @@
     own_first = lax.axis_index("tensor") == 0
     straight = jnp.concatenate(small, axis=1)
     turned = jnp.concatenate(small[::-1], axis=1)
-    vecs[0:6, :] = jnp.where(own_first, straight, turned)[0:6]
-    vecs[6:8, :] = straight[6:8]
+    vecs = [jnp.where(own_first, straight, turned)[0:6], straight[6:8]]
     per = dm.fh // dm.width
     for t in range(2):
         up = jnp.concatenate([extra[t, f].astype(F32)[8:9, 0:up_share] for f in range(dm.shards)], axis=1)
-        for j in range(per):
-            vecs[8 + t * per + j : 9 + t * per + j, :] = up[:, j * dm.width : (j + 1) * dm.width]
-
-    def weights_ready():
-        for copy in late:
-            copy.wait()
-
-    output = layer_forward(dm, rows[...], w, vecs, st, False, weights_ready)
-    for m in range(2):
-        out[m, 0] = image(dm, output, m).astype(BF)
+        vecs += [up[:, j * dm.width : (j + 1) * dm.width] for j in range(per)]
+    vecs += [jnp.full((1, dm.width), v, F32) for v in live]
+    vecs.append(jnp.zeros((6 - 2 * per, dm.width), F32))
+    vecs = jnp.concatenate(vecs, axis=0)
+    w[0, dm.o_vecs : dm.o_image, 0 : dm.width] = vecs.astype(BF)
+    used = lax.axis_index("section") == 0
+
+    @pl.when(used)
+    def _():
+        rows[...] = forward_attention(dm, rows[...], w, vecs, st, False)
+
+    for copy in late:
+        copy.wait()
+
+    @pl.when(used)
+    def _():
+        output = forward_mlp(dm, rows[...], w, vecs, st, False)
+        for m in range(2):
+            out[m, 0] = image(dm, output, m).astype(BF)
+
+
+def vectors_of(dm, w):
+    return w[0, dm.o_vecs : dm.o_image, 0 : dm.width].astype(F32)
 
 
 def live_of(count_ref, m):
@@ -328,42 +358,54 @@
 
 def ring_slots(dm, ring):
     if not ring:
-        return range(dm.shards)
+        return [range(t * dm.shards, (t + 1) * dm.shards) for t in range(2)]
     place = picked(RING_PLACE, lax.axis_index("fsdp"))
-    return [lax.rem(RING_PLACE[f] + NEAR + dm.shards - place, dm.shards) for f in range(dm.shards)]
-
-
-def kernel_second(dm, count_ref, tokens, h1, out_grad, w, vecs, acts, grad_in, *refs):
+    found = [[], []]
+    for p in RING_PLACE:
+        ahead = jnp.where(lax.axis_index("tensor") == 0, p - place, place - p)
+        ahead = lax.rem(ahead + dm.shards, dm.shards)
+        found[0].append(picked(KEPT_OWN, ahead))
+        found[1].append(picked(KEPT_OTHER, ahead))
+    return found
+
+
+def kernel_second(dm, h1, w, acts, grad_in, *refs):
     st, refs = named(dm.state_shapes(), refs)
     ct, refs = named(dm.cotangent_shapes(), refs)
     work, _ = named(dm.work_shapes(), refs)
     rows = work["rows"]
     last = lax.axis_index("section") != 0
 
+    def take(start):
+        for m in range(2):
+            value = w[m, start : start + 96, 0 : dm.width].astype(F32)
+            rows[m * ROW_STEP : (m + 1) * ROW_STEP, :] = value[0:ROW_STEP]
+
     @pl.when(jnp.logical_not(last))
     def _():
-        spread(dm, rows, lambda m: tokens[m, 0].astype(F32))
+        take(dm.o_image)
 
     @pl.when(last)
     def _():
         spread(dm, rows, lambda m: h1[m, 0].astype(F32))
 
-    output = layer_forward(dm, rows[...], w, vecs, st, True)
+    vecs = vectors_of(dm, w)
+    output = forward_mlp(dm, forward_attention(dm, rows[...], w, vecs, st, True), w, vecs, st, True)
     for m in range(2):
-        acts[m, 0] = (image(dm, output, m) * live_of(count_ref, m)).astype(BF)
+        acts[m, 0] = (image(dm, output, m) * vecs[12 + m : 13 + m]).astype(BF)
 
     @pl.when(last)
     def _():
-        spread(dm, rows, lambda m: out_grad[m, 0].astype(F32) * live_of(count_ref, m))
+        take(dm.o_grad)
         grad = layer_backward(dm, rows[...], w, vecs, st, ct, work)
         for m in range(2):
             grad_in[m, 0] = image(dm, grad, m).astype(BF)
 
 
-def kernel_third(dm, ring, incoming, w, vecs, own, *refs):
+def kernel_third(dm, ring, incoming, w, own, *refs):
     st, refs = named(dm.state_shapes(), refs)
     given, refs = named(dm.cotangent_shapes(), refs)
-    grad_in, grad_own, grad_other, *refs = refs
+    grad_in, grads, *refs = refs
     ct, refs = named(dm.cotangent_shapes(), refs)
     work, _ = named(dm.work_shapes(), refs)
     rows = work["rows"]
@@ -372,7 +414,7 @@
     @pl.when(jnp.logical_not(last))
     def _():
         spread(dm, rows, lambda m: incoming[m, 0].astype(F32))
-        grad = layer_backward(dm, rows[...], w, vecs, st, ct, work)
+        grad = layer_backward(dm, rows[...], w, vectors_of(dm, w), st, ct, work)
         for m in range(2):
             grad_in[m, 0] = image(dm, grad, m).astype(BF)
 
@@ -382,7 +424,7 @@
         for name in ct:
             ct[name][...] = given[name][...]
 
-    parameter_grads(dm, st, ct, (grad_own, grad_other), ring_slots(dm, ring))
+    parameter_grads(dm, st, ct, grads, ring_slots(dm, ring))
 
 
 def kernel_unpack(dm, *refs):
@@ -422,53 +464,55 @@
     )(*args)
 
 
-def shifted(value, cycle, step):
+def onward(value, cycle):
     count = len(cycle)
-    return lax.ppermute(value, "fsdp", [(cycle[i], cycle[(i + step) % count]) for i in range(count)])
-
-
-def gather_ring(block, cycle):
+    route = []
+    for i in range(count):
+        route.append((cycle[i], cycle[(i + 1) % count]))
+        route.append((count + cycle[i], count + cycle[(i - 1) % count]))
+    return lax.ppermute(value, ("tensor", "fsdp"), route)
+
+
+def gather_ring(block, cycle, swap):
+    far = len(cycle) // 2
+    own, other = [block], [lax.ppermute(block, "tensor", swap)]
+    for step in range(far):
+        own.append(onward(own[-1], cycle))
+        if step + 1 < far:
+            other.append(onward(other[-1], cycle))
+    found, places = own + other, [(0, -s) for s in range(far + 1)] + [(1, -s) for s in range(far)]
+    for t, values in ((1, own), (0, other)):
+        for step in range(1, len(values)):
+            found.append(lax.ppermute(values[step], "tensor", swap))
+            places.append((t, step))
+    layout = [(t, i, 0, offset, 0, block.shape[1]) for i, (t, offset) in enumerate(places)]
+    return found, layout
+
+
+def reduce_ring(blocks, cycle, swap):
     count = len(cycle)
-    ahead = behind = block
-    found, layout = [block], [(0, 0)]
-    for step in range(1, count // 2):
-        ahead, behind = shifted(ahead, cycle, 1), shifted(behind, cycle, -1)
-        found += [ahead, behind]
-        layout += [(-step, 0), (step, 0)]
-    cut = block.shape[1] // 256 * 128
-    found += [shifted(ahead[:, :cut], cycle, 1), shifted(behind[:, cut:], cycle, -1)]
-    layout += [(-(count // 2), 0), (count // 2, cut)]
-    return found, layout
-
-
-def both_ways(ahead, behind, cycle):
-    ahead, behind = lax.optimization_barrier((ahead, behind))
-    return lax.optimization_barrier((shifted(ahead, cycle, 1), shifted(behind, cycle, -1)))
-
-
-def reduce_ring(own, other, cycle, swap):
-    count = len(cycle)
-    far = count // 2
-    cut = own.shape[2] // 256 * 128
-    split = NEAR + far - 1
-    far_part = lax.ppermute(other[split:], "tensor", swap)
-    near_part = lax.ppermute(other[:split], "tensor", swap)
-
-    def part(offset, lo=0, hi=None, *more):
-        slot = (offset + NEAR) % count
-        given = far_part[slot - split] if slot >= split else near_part[slot]
-        terms = (own[slot][:, lo:hi], given[:, lo:hi]) + more
-        return sum(v.astype(F32) for v in terms).astype(BF)
-
-    low, high = both_ways(part(far, 0, cut), part(far, cut), cycle)
-    step = far - 1
-    ahead = jnp.concatenate([part(step, 0, cut, low), part(step, cut)], axis=1)
-    behind = jnp.concatenate([part(-step, 0, cut), part(-step, cut, None, high)], axis=1)
-    left, right = both_ways(ahead, behind, cycle)
-    for step in range(far - 2, 0, -1):
-        ahead, behind = part(step, 0, None, left), part(-step, 0, None, right)
-        left, right = both_ways(ahead, behind, cycle)
-    return own[NEAR], near_part[NEAR], left, right
+    early = 3
+    first = lax.ppermute(blocks[count : count + early], "tensor", swap)
+    later = lax.ppermute(blocks[count + early :], "tensor", swap)
+
+    def part(i, *more):
+        given = first[i] if i < early else later[i - early]
+        return sum(v.astype(F32) for v in (blocks[i], given) + more).astype(BF)
+
+    def after(value, sent):
+        return lax.optimization_barrier((value, sent))[0]
+
+    own = onward(part(0), cycle)
+    sent = part(1)
+    other = onward(sent, cycle)
+    for i in range(2, count, 2):
+        sent = part(i, after(own, sent))
+        own = onward(sent, cycle)
+        if i + 1 < count - 1:
+            sent = part(i + 1, after(other, sent))
+            other = onward(sent, cycle)
+    other = lax.ppermute(other, "tensor", swap)
+    return blocks[count - 1], later[count - 1 - early], own, other
 
 
 def per_device(tokens, out_grad, image_count, w_qkv, w_out, w_up, w_down, head_bias, up_bias, gains, shifts):
@@ -480,22 +524,18 @@
     block = width // dm.shards
     swap = [(0, 1), (1, 0)]
     vectors = (head_bias, up_bias, gains, shifts)
-    small = jnp.concatenate([gains[0], shifts[0], head_bias[0]], axis=0)
     if ring:
-        ext = jnp.concatenate(
-            [
-                jnp.pad(small, ((0, 0), (0, EXT - small.shape[1]))),
-                jnp.pad(up_bias, ((0, block - 9), (0, EXT - up_bias.shape[1]))),
-            ],
-            axis=0,
+        places = [(w_qkv[0, :, k], 0, k * dm.half) for k in range(3)]
+        places += [(w_out[0].T, 0, dm.o_out), (w_up[0], 0, dm.o_up), (w_down[0].T, 0, dm.o_down)]
+        places += [(v, r, dm.cols) for v, r in ((gains[0], 0), (shifts[0], 2), (head_bias[0], 6), (up_bias, 8))]
+        packed = sum(
+            jnp.pad(v, ((r, block - r - v.shape[0]), (c, dm.packed - c - v.shape[1]))) for v, r, c in places
         )
-        packed = jnp.concatenate(
-            [w_qkv[0, :, 0], w_qkv[0, :, 1], w_qkv[0, :, 2], w_out[0].T, w_up[0], w_down[0].T, ext], axis=1
-        )
-        found, layout = gather_ring(packed, GRID_RING)
+        found, layout = gather_ring(packed, GRID_RING, swap)
     else:
         rows = jnp.concatenate([w_qkv[0].reshape(w_qkv.shape[1], -1), w_out[0].T, w_up[0], w_down[0].T], axis=1)
         rows = lax.all_gather(rows, "fsdp", axis=0, tiled=True)
+        small = jnp.concatenate([gains[0], shifts[0], head_bias[0]], axis=0)
         small = lax.all_gather(small, "fsdp", axis=1, tiled=True)
         up = lax.all_gather(up_bias, "fsdp", axis=1, tiled=True)
         small = jnp.moveaxis(small.reshape(8, dm.shards, -1), 1, 0)
@@ -509,41 +549,40 @@
             axis=1,
         )
         rows = jnp.concatenate([rows, ext.reshape(width, EXT)], axis=1)
-        found = [rows[i * block : (i + 1) * block] for i in range(dm.shards)]
-        layout = [(i, 0) for i in range(dm.shards)]
-    others = [lax.ppermute(b, "tensor", swap) for b in found]
+        found = [rows, lax.ppermute(rows, "tensor", swap)]
+        layout = [(t, t, i * block, i, 0, dm.packed) for t in range(2) for i in range(dm.shards)]
     states = dm.state_shapes()
     cotangents = dm.cotangent_shapes()
     shape = tokens.shape
     buffers = lambda shapes: [pltpu.VMEM(*v) for v in shapes]
     work = buffers(dm.work_shapes().values())
-    w, vecs, low0 = call(
+    w, low0 = call(
         functools.partial(kernel_first, dm, layout, ring),
-        [VM] + [AN] * (2 * len(found)),
-        [((2, width, dm.cols), BF), ((16, width), F32), (shape, BF)],
-        (tokens,) + tuple(found) + tuple(others),
+        [SM, VM, VM] + [AN] * len(found),
+        [((2, dm.w_rows, dm.cols), BF), (shape, BF)],
+        (image_count,) + tuple(jnp.transpose(v[:, 0], (1, 0, 2)) for v in (tokens, out_grad)) + tuple(found),
         scratch=buffers([states["proj"], states["probs"], states["mixed"], ((dm.rows, width), F32)])
-        + [pltpu.VMEM((2, dm.shards, block, EXT), BF), pltpu.SemaphoreType.DMA((3, 2 * len(found)))],
+        + [pltpu.VMEM((2, dm.shards, block, EXT), BF), pltpu.SemaphoreType.DMA((3, len(layout)))],
     )
     h1 = lax.ppermute(low0, "section", [(0, 1)])
     kept = list(states.values()) + list(cotangents.values())
     acts, grad1, *kept = call(
         functools.partial(kernel_second, dm),
-        [SM] + [VM] * 5,
+        [VM] * 2,
         [(shape, BF), (shape, BF)] + kept,
-        (image_count, tokens, h1, out_grad, w, vecs),
+        (h1, w),
         scratch=work,
     )
     incoming = lax.ppermute(grad1, "section", [(1, 0)])
-    in_grads, own, other = call(
+    in_grads, blocks = call(
         functools.partial(kernel_third, dm, ring),
-        [VM] * (4 + len(kept)),
-        [(shape, BF)] + [((dm.shards, block, dm.packed), BF)] * 2,
-        (incoming, w, vecs, grad1) + tuple(kept),
+        [VM] * (3 + len(kept)),
+        [(shape, BF), ((2 * dm.shards, block, dm.packed), BF)],
+        (incoming, w, grad1) + tuple(kept),
         scratch=buffers(cotangents.values()) + work,
     )
     if ring:
-        terms = reduce_ring(own, other, GRID_RING, swap)
+        terms = reduce_ring(blocks, GRID_RING, swap)
         shapes = [(3, block, dm.half), (block, dm.half), (block, dm.fh), (block, dm.fh)] + [v.shape for v in vectors]
         g_qkv, g_out, g_up, g_down, *small = call(
             functools.partial(kernel_unpack, dm), [VM] * len(terms), [(v, F32) for v in shapes], terms
@@ -551,7 +590,8 @@
         grads = [jnp.transpose(g_qkv, (1, 0, 2))[None], g_out.T[None], g_up[None], g_down.T[None], *small]
     else:
         half = dm.half
-        mine = own.astype(F32) + lax.ppermute(other, "tensor", swap).astype(F32)
+        mine = blocks[: dm.shards].astype(F32)
+        mine += lax.ppermute(blocks[dm.shards :], "tensor", swap).astype(F32)
         mine = mine.reshape(width, dm.packed)
         body = lax.psum_scatter(mine[:, : dm.cols], "fsdp", scatter_dimension=0, tiled=True)
         share, up_share = half // dm.shards, dm.fh // dm.shards

time: 101 us -> 86.5 us (0.86)
  waiting for transfers between devices: 51.4 us -> 32.9 us
  starting transfers between devices: 24.1 us -> 32.8 us
  local copies, waits for them, and re-layouts: 8.74 us -> 4.99 us
    ppermute x27 -> x25, waiting for transfers between devices: 41.2 us -> 21.2 us  [the longest x14 19.6 us: onward(): return lax.ppermute(value, ('tensor', 'fsdp'), route)]
    ppermute x27 -> x25, starting transfers between devices: 18.8 us -> 30.1 us  [the longest x14 27.4 us: onward(): return lax.ppermute(value, ('tensor', 'fsdp'), route)]
    ppermute x1, starting transfers between devices: 4.05 us -> 1.44 us  [per_device(): h1 = lax.ppermute(low0, 'section', [(0, 1)])]
    unnamed x19 -> x7, local copies, waits for them, and re-layouts: 6.63 us -> 4.04 us
    ppermute x1, waiting for transfers between devices: 1.81 us -> 3.25 us  [per_device(): h1 = lax.ppermute(low0, 'section', [(0, 1)])]
    concatenate x4 -> x0, other arithmetic: 1.4 us -> none  [the longest x1 0.7 us: per_device(): small = jnp.concatenate([gains[0], shifts[0], head_bias[0]], axis=0)]
    add x0 -> x1, other arithmetic: none -> 1.08 us  [per_device(): sum((jnp.pad(v, ((r, block - r - v.shape[0]), (c, dm.packed - c - v.shape...]
    concatenate x1 -> x0, local copies, waits for them, and re-layouts: 1.04 us -> none  [per_device(): jnp.concatenate([w_qkv[0, :, 0], w_qkv[0, :, 1], w_qkv[0, :, 2], w_out[0]...]
  transfers between devices with their start and end apart: 29 -> 27, of which waited for: 17 -> 16; matrix products, arithmetic and copies ran while one was open for 4% -> 3% of each run, Pallas kernels for 0% -> 0%
where the time goes in v3:
time: 86.5 us; the launch traced here: 86.2 us
  waiting for transfers between devices  32.9 us (38%)
  starting transfers between devices  32.8 us (38%)
  Pallas kernels  13 us (15%)
  local copies, waits for them, and re-layouts  4.99 us (6%)
  other arithmetic  1.69 us (2%)
    ppermute x14, starting transfers between devices, onward(): return lax.ppermute(value, ('tensor', 'fsdp'), route)  27.4 us
    ppermute x14, waiting for transfers between devices, onward(): return lax.ppermute(value, ('tensor', 'fsdp'), route)  19.6 us
    pallas_call x4, Pallas kernels, call(): pl.pallas_call(kernel, in_specs=ins, out_specs=[VM] * len(outs), out_shap...  13 us
    ppermute x1, waiting for transfers between devices, per_device(): incoming = lax.ppermute(grad1, 'section', [(1, 0)])  8.45 us
    unnamed x7, local copies, waits for them, and re-layouts  4.04 us
    ppermute x1, waiting for transfers between devices, per_device(): h1 = lax.ppermute(low0, 'section', [(0, 1)])  3.25 us
  transfers between devices with their start and end apart: 27, of which 16 were waited for; matrix products, arithmetic and copies ran while one was open for 3% of the time, Pallas kernels for 0%

profile of v3, /device:TPU:0, one launch (start us, length us, event | category | flops | bytes accessed | tf_op | source)
XLA Modules:
  0.0 86.2 jit_solution(12858301348681357812)
XLA Ops:
  0.6 0.8 slice_bitcast_fusion.4
  1.4 1.1 %pad_add_fusion.refs_0_ = bf16[48,2432]{1,0:T(8,128)(2,1)S(1)} fusion(bf16[1,96]{1,0:T(2,128)(2,1)} %param.19, bf16[2,24]{1,0:T(2,128)(2,1)} %bitcast.70, bf16[4,24]{1,0:T(4,128)(2,1)} %bitcast.69, bf16[2,24]{1,0:T(2,128)(2,1)} %bitcast.71, bf16[48,768]{1,0:T(8,128)(2,1)} %bitcast.66, bf16[48,768]{1,0:T(8,128)(2,1)} %bitcast.67, ...), kind=kLoop, calls=%fused_computation.16 | loop fusion | flops 2334720 | bytes 455232 | tf_op jit(solution)/shard_map/add | solution.py:531
  2.5 0.5 collective-permute-start.4
  3.0 2.6 %collective-permute-start = (bf16[48,2432]{1,0:T(8,128)(2,1)S(1)}, bf16[48,2432]{1,0:T(8,128)(2,1)S(1)}, u32[]{:S(2)}, u32[]{:S(2)}) collective-permute-start(bf16[48,2432]{1,0:T(8,128)(2,1)S(1)} %pad_add_fusion.refs_0_), channel_id=1, source_target_pairs={{0,1},{8,10},{1,3},{9,8},{3,5},{11,9},{5,7},{13,11},{7,6},{15,13},... | collective-permute-start | bytes 700424 | tf_op jit(solution)/shard_map/ppermute | solution.py:473
  5.6 1.6 %collective-permute-start.5 = (bf16[48,2432]{1,0:T(8,128)(2,1)S(1)}, bf16[48,2432]{1,0:T(8,128)(2,1)S(1)}, u32[]{:S(2)}, u32[]{:S(2)}) collective-permute-start(bf16[48,2432]{1,0:T(8,128)(2,1)S(1)} %collective-permute-done.4.refs_5_), channel_id=1, source_target_pairs={{0,1},{8,10},{1,3},{9,8},{3,5},{11,9},{5,7},{13,11},{7,6},{15,13},... | collective-permute-start | bytes 700424 | tf_op jit(solution)/shard_map/ppermute | solution.py:473
  7.2 2.5 %collective-permute-done.refs_1_ = bf16[48,2432]{1,0:T(8,128)(2,1)S(1)} collective-permute-done((bf16[48,2432]{1,0:T(8,128)(2,1)S(1)}, bf16[48,2432]{1,0:T(8,128)(2,1)S(1)}, u32[]{:S(2)}, u32[]{:S(2)}) %collective-permute-start) | collective-permute-done | bytes 233504 | tf_op jit(solution)/shard_map/ppermute | solution.py:473
  9.7 2.0 %collective-permute-start.1 = (bf16[48,2432]{1,0:T(8,128)(2,1)S(1)}, bf16[48,2432]{1,0:T(8,128)(2,1)S(1)}, u32[]{:S(2)}, u32[]{:S(2)}) collective-permute-start(bf16[48,2432]{1,0:T(8,128)(2,1)S(1)} %collective-permute-done.refs_1_), channel_id=1, source_target_pairs={{0,1},{8,10},{1,3},{9,8},{3,5},{11,9},{5,7},{13,11},{7,6},{15,13},... | collective-permute-start | bytes 700424 | tf_op jit(solution)/shard_map/ppermute | solution.py:473
  11.7 0.5 collective-permute-done.5.refs_6_
  12.2 2.0 %collective-permute-start.6 = (bf16[48,2432]{1,0:T(8,128)(2,1)S(1)}, bf16[48,2432]{1,0:T(8,128)(2,1)S(1)}, u32[]{:S(2)}, u32[]{:S(2)}) collective-permute-start(bf16[48,2432]{1,0:T(8,128)(2,1)S(1)} %collective-permute-done.5.refs_6_), channel_id=1, source_target_pairs={{0,1},{8,10},{1,3},{9,8},{3,5},{11,9},{5,7},{13,11},{7,6},{15,13},... | collective-permute-start | bytes 700424 | tf_op jit(solution)/shard_map/ppermute | solution.py:473
  14.2 1.6 %collective-permute-done.1.refs_2_ = bf16[48,2432]{1,0:T(8,128)(2,1)S(1)} collective-permute-done((bf16[48,2432]{1,0:T(8,128)(2,1)S(1)}, bf16[48,2432]{1,0:T(8,128)(2,1)S(1)}, u32[]{:S(2)}, u32[]{:S(2)}) %collective-permute-start.1) | collective-permute-done | bytes 233504 | tf_op jit(solution)/shard_map/ppermute | solution.py:473
  15.8 2.0 %collective-permute-start.2 = (bf16[48,2432]{1,0:T(8,128)(2,1)S(1)}, bf16[48,2432]{1,0:T(8,128)(2,1)S(1)}, u32[]{:S(2)}, u32[]{:S(2)}) collective-permute-start(bf16[48,2432]{1,0:T(8,128)(2,1)S(1)} %collective-permute-done.1.refs_2_), channel_id=1, source_target_pairs={{0,1},{8,10},{1,3},{9,8},{3,5},{11,9},{5,7},{13,11},{7,6},{15,13},... | collective-permute-start | bytes 700424 | tf_op jit(solution)/shard_map/ppermute | solution.py:473
  17.7 0.5 collective-permute-start.12
  18.3 2.0 %collective-permute-start.7 = (bf16[48,2432]{1,0:T(8,128)(2,1)S(1)}, bf16[48,2432]{1,0:T(8,128)(2,1)S(1)}, u32[]{:S(2)}, u32[]{:S(2)}) collective-permute-start(bf16[48,2432]{1,0:T(8,128)(2,1)S(1)} %collective-permute-done.6.refs_7_), channel_id=1, source_target_pairs={{0,1},{8,10},{1,3},{9,8},{3,5},{11,9},{5,7},{13,11},{7,6},{15,13},... | collective-permute-start | bytes 700424 | tf_op jit(solution)/shard_map/ppermute | solution.py:473
  20.2 1.6 %collective-permute-done.2.refs_3_ = bf16[48,2432]{1,0:T(8,128)(2,1)S(1)} collective-permute-done((bf16[48,2432]{1,0:T(8,128)(2,1)S(1)}, bf16[48,2432]{1,0:T(8,128)(2,1)S(1)}, u32[]{:S(2)}, u32[]{:S(2)}) %collective-permute-start.2) | collective-permute-done | bytes 233504 | tf_op jit(solution)/shard_map/ppermute | solution.py:473
  21.8 2.0 %collective-permute-start.3 = (bf16[48,2432]{1,0:T(8,128)(2,1)S(1)}, bf16[48,2432]{1,0:T(8,128)(2,1)S(1)}, u32[]{:S(2)}, u32[]{:S(2)}) collective-permute-start(bf16[48,2432]{1,0:T(8,128)(2,1)S(1)} %collective-permute-done.2.refs_3_), channel_id=1, source_target_pairs={{0,1},{8,10},{1,3},{9,8},{3,5},{11,9},{5,7},{13,11},{7,6},{15,13},... | collective-permute-start | bytes 700424 | tf_op jit(solution)/shard_map/ppermute | solution.py:473
  23.8 0.5 collective-permute-start.13
  24.4 0.4 collective-permute-start.14
  24.8 3.1 %collective-permute-done.3.refs_4_ = bf16[48,2432]{1,0:T(8,128)(2,1)S(1)} collective-permute-done((bf16[48,2432]{1,0:T(8,128)(2,1)S(1)}, bf16[48,2432]{1,0:T(8,128)(2,1)S(1)}, u32[]{:S(2)}, u32[]{:S(2)}) %collective-permute-start.3) | collective-permute-done | bytes 233504 | tf_op jit(solution)/shard_map/ppermute | solution.py:473
  27.9 0.7 copy.21.count_ref
  28.7 0.9 collective-permute-done.11.refs_12_
  29.5 0.9 %copy-done = bf16[2,1,82,384]{3,0,2,1:T(2,128)(2,1)S(1)} copy-done((bf16[2,1,82,384]{3,0,2,1:T(2,128)(2,1)S(1)}, bf16[2,1,82,384]{3,0,2,1:T(2,128)(2,1)}, u32[]{:S(2)}) %copy-start) | copy-done | bytes 125976
  30.4 0.9 %copy-done.1 = bf16[2,1,82,384]{3,0,2,1:T(2,128)(2,1)S(1)} copy-done((bf16[2,1,82,384]{3,0,2,1:T(2,128)(2,1)S(1)}, bf16[2,1,82,384]{3,0,2,1:T(2,128)(2,1)}, u32[]{:S(2)}) %copy-start.1) | copy-done | bytes 125976
  31.3 5.2 %shard_map.186 = (bf16[2,592,2304]{2,1,0:T(8,128)(2,1)S(1)}, bf16[2,1,82,384]{3,2,1,0:T(8,128)(2,1)S(1)}) custom-call(s32[2,1]{1,0:T(2,128)S(1)} %copy.21.count_ref, bf16[82,2,384]{2,1,0:T(2,128)(2,1)S(1)} %bitcast.64, bf16[82,2,384]{2,1,0:T(2,128)(2,1)S(1)} %bitcast.65, bf16[48,2432]{1,0:T(8,128)(2,1)S(1)} %pad_add_fusion.refs_0_, ...), custom_call_target="tpu_custom_call" | custom-call | tf_op jit(solution)/shard_map/pallas_call | solution.py:457
  36.5 1.4 %collective-permute-start.15 = (bf16[2,1,82,384]{3,2,1,0:T(8,128)(2,1)S(1)}, bf16[2,1,82,384]{3,2,1,0:T(8,128)(2,1)S(1)}, u32[]{:S(2)}, u32[]{:S(2)}) collective-permute-start(bf16[2,1,82,384]{3,2,1,0:T(8,128)(2,1)S(1)} %get-tuple-element.44), channel_id=1, source_target_pairs={{0,16},{1,17},{2,18},{3,19},{4,20},{5,21},{6,22},{7,23},{8,24},{9,... | collective-permute-start | bytes 377864 | tf_op jit(solution)/shard_map/ppermute | solution.py:567
  37.9 3.2 %collective-permute-done.15.h1 = bf16[2,1,82,384]{3,2,1,0:T(8,128)(2,1)S(1)} collective-permute-done((bf16[2,1,82,384]{3,2,1,0:T(8,128)(2,1)S(1)}, bf16[2,1,82,384]{3,2,1,0:T(8,128)(2,1)S(1)}, u32[]{:S(2)}, u32[]{:S(2)}) %collective-permute-start.15) | collective-permute-done | bytes 125984 | tf_op jit(solution)/shard_map/ppermute | solution.py:567
  41.2 2.7 %shard_map.187 = (bf16[2,1,82,384]{3,2,1,0:T(8,128)(2,1)S(1)}, bf16[2,1,82,384]{3,2,1,0:T(8,128)(2,1)S(1)}, f32[2,176,576]{2,1,0:T(8,128)S(1)}, f32[12,88,88]{2,...) custom-call(bf16[2,1,82,384]{3,2,1,0:T(8,128)(2,1)S(1)} %collective-, ...), custom_call_target="tpu_custom_call" | custom-call | tf_op jit(solution)/shard_map/pallas_call | solution.py:457
  43.9 1.3 %collective-permute-start.16 = (bf16[2,1,82,384]{3,2,1,0:T(8,128)(2,1)S(1)}, bf16[2,1,82,384]{3,2,1,0:T(8,128)(2,1)S(1)}, u32[]{:S(2)}, u32[]{:S(2)}) collective-permute-start(bf16[2,1,82,384]{3,2,1,0:T(8,128)(2,1)S(1)} %get-tuple-element.47.own), channel_id=1, source_target_pairs={{16,0},{17,1},{18,2},{19,3},{20,4},{21,5},{22,6},{23,7},{24,8},{25... | collective-permute-start | bytes 377864 | tf_op jit(solution)/shard_map/ppermute | solution.py:576
  45.2 8.5 %collective-permute-done.16.incoming = bf16[2,1,82,384]{3,2,1,0:T(8,128)(2,1)S(1)} collective-permute-done((bf16[2,1,82,384]{3,2,1,0:T(8,128)(2,1)S(1)}, bf16[2,1,82,384]{3,2,1,0:T(8,128)(2,1)S(1)}, u32[]{:S(2)}, u32[]{:S(2)}) %collective-permute-start.16) | collective-permute-done | bytes 125984 | tf_op jit(solution)/shard_map/ppermute | solution.py:576
  53.7 4.2 %shard_map.188 = (bf16[2,1,82,384]{3,2,1,0:T(8,128)(2,1)S(1)}, bf16[16,48,2432]{2,1,0:T(8,128)(2,1)S(1)}) custom-call(bf16[2,1,82,384]{3,2,1,0:T(8,128)(2,1)S(1)} %collective-permute-done.16.incoming, bf16[2,592,2304]{2,1,0:T(8,128)(2,1)S(1)} %get-tuple-element.45.w, bf16[2,1,82,384]{3,2,1,0:T(8,128)(2,1)S(1)} %get-tuple-element.47.own, ...), custom_call_target="tpu_custom_call" | custom-call | tf_op jit(solution)/shard_map/pallas_call | solution.py:457
  58.0 0.7 copy.22
  58.9 0.6 collective-permute-start.17
  59.4 0.8 collective-permute-done.18
  60.3 2.2 %collective-permute-start.19 = (bf16[48,2432]{1,0:T(8,128)(2,1)S(1)}, bf16[48,2432]{1,0:T(8,128)(2,1)S(1)}, u32[]{:S(2)}, u32[]{:S(2)}) collective-permute-start(bf16[48,2432]{1,0:T(8,128)(2,1)S(1)} %get-tuple-element.89), channel_id=1, source_target_pairs={{0,1},{8,10},{1,3},{9,8},{3,5},{11,9},{5,7},{13,11},{7,6},{15,13},... | collective-permute-start | bytes 700424 | tf_op jit(solution)/shard_map/ppermute | solution.py:473
  62.6 0.7 copy.23
  63.3 1.6 %collective-permute-start.21 = (bf16[48,2432]{1,0:T(8,128)(2,1)S(1)}, bf16[48,2432]{1,0:T(8,128)(2,1)S(1)}, u32[]{:S(2)}, u32[]{:S(2)}) collective-permute-start(bf16[48,2432]{1,0:T(8,128)(2,1)S(1)} %get-tuple-element.88), channel_id=1, source_target_pairs={{0,1},{8,10},{1,3},{9,8},{3,5},{11,9},{5,7},{13,11},{7,6},{15,13},... | collective-permute-start | bytes 700424 | tf_op jit(solution)/shard_map/ppermute | solution.py:473
  64.9 1.8 %collective-permute-done.19 = bf16[48,2432]{1,0:T(8,128)(2,1)S(1)} collective-permute-done((bf16[48,2432]{1,0:T(8,128)(2,1)S(1)}, bf16[48,2432]{1,0:T(8,128)(2,1)S(1)}, u32[]{:S(2)}, u32[]{:S(2)}) %collective-permute-start.19) | collective-permute-done | bytes 233504 | tf_op jit(solution)/shard_map/ppermute | solution.py:473
  66.7 2.0 %collective-permute-start.20 = (bf16[48,2432]{1,0:T(8,128)(2,1)S(1)}, bf16[48,2432]{1,0:T(8,128)(2,1)S(1)}, u32[]{:S(2)}, u32[]{:S(2)}) collective-permute-start(bf16[48,2432]{1,0:T(8,128)(2,1)S(1)} %fusion.2), channel_id=1, source_target_pairs={{0,1},{8,10},{1,3},{9,8},{3,5},{11,9},{5,7},{13,11},{7,6},{15,13},... | collective-permute-start | bytes 700424 | tf_op jit(solution)/shard_map/ppermute | solution.py:473
  68.8 0.6 collective-permute-done.21
  69.5 1.8 %collective-permute-start.23 = (bf16[48,2432]{1,0:T(8,128)(2,1)S(1)}, bf16[48,2432]{1,0:T(8,128)(2,1)S(1)}, u32[]{:S(2)}, u32[]{:S(2)}) collective-permute-start(bf16[48,2432]{1,0:T(8,128)(2,1)S(1)} %fusion.1), channel_id=1, source_target_pairs={{0,1},{8,10},{1,3},{9,8},{3,5},{11,9},{5,7},{13,11},{7,6},{15,13},... | collective-permute-start | bytes 700424 | tf_op jit(solution)/shard_map/ppermute | solution.py:473
  71.3 1.6 %collective-permute-done.20 = bf16[48,2432]{1,0:T(8,128)(2,1)S(1)} collective-permute-done((bf16[48,2432]{1,0:T(8,128)(2,1)S(1)}, bf16[48,2432]{1,0:T(8,128)(2,1)S(1)}, u32[]{:S(2)}, u32[]{:S(2)}) %collective-permute-start.20) | collective-permute-done | bytes 233504 | tf_op jit(solution)/shard_map/ppermute | solution.py:473
  73.0 2.0 %collective-permute-start.22 = (bf16[48,2432]{1,0:T(8,128)(2,1)S(1)}, bf16[48,2432]{1,0:T(8,128)(2,1)S(1)}, u32[]{:S(2)}, u32[]{:S(2)}) collective-permute-start(bf16[48,2432]{1,0:T(8,128)(2,1)S(1)} %fusion.3), channel_id=1, source_target_pairs={{0,1},{8,10},{1,3},{9,8},{3,5},{11,9},{5,7},{13,11},{7,6},{15,13},... | collective-permute-start | bytes 700424 | tf_op jit(solution)/shard_map/ppermute | solution.py:473
  75.0 0.6 collective-permute-done.23
  75.7 1.8 %collective-permute-start.25 = (bf16[48,2432]{1,0:T(8,128)(2,1)S(1)}, bf16[48,2432]{1,0:T(8,128)(2,1)S(1)}, u32[]{:S(2)}, u32[]{:S(2)}) collective-permute-start(bf16[48,2432]{1,0:T(8,128)(2,1)S(1)} %fusion), channel_id=1, source_target_pairs={{0,1},{8,10},{1,3},{9,8},{3,5},{11,9},{5,7},{13,11},{7,6},{15,13},... | collective-permute-start | bytes 700424 | tf_op jit(solution)/shard_map/ppermute | solution.py:473
  77.5 1.6 %collective-permute-done.22 = bf16[48,2432]{1,0:T(8,128)(2,1)S(1)} collective-permute-done((bf16[48,2432]{1,0:T(8,128)(2,1)S(1)}, bf16[48,2432]{1,0:T(8,128)(2,1)S(1)}, u32[]{:S(2)}, u32[]{:S(2)}) %collective-permute-start.22) | collective-permute-done | bytes 233504 | tf_op jit(solution)/shard_map/ppermute | solution.py:473
  79.2 2.0 %collective-permute-start.24 = (bf16[48,2432]{1,0:T(8,128)(2,1)S(1)}, bf16[48,2432]{1,0:T(8,128)(2,1)S(1)}, u32[]{:S(2)}, u32[]{:S(2)}) collective-permute-start(bf16[48,2432]{1,0:T(8,128)(2,1)S(1)} %fusion.4), channel_id=1, source_target_pairs={{0,1},{8,10},{1,3},{9,8},{3,5},{11,9},{5,7},{13,11},{7,6},{15,13},... | collective-permute-start | bytes 700424 | tf_op jit(solution)/shard_map/ppermute | solution.py:473
  81.2 0.6 collective-permute-done.25
  81.8 3.4 %collective-permute-done.24.refs_2_ = bf16[48,2432]{1,0:T(8,128)(2,1)S(1)} collective-permute-done((bf16[48,2432]{1,0:T(8,128)(2,1)S(1)}, bf16[48,2432]{1,0:T(8,128)(2,1)S(1)}, u32[]{:S(2)}, u32[]{:S(2)}) %collective-permute-start.24) | collective-permute-done | bytes 233504 | tf_op jit(solution)/shard_map/ppermute | solution.py:473
  85.3 0.9 shard_map.189
  (29 shorter events, 1.0 us)
Async XLA Ops:
  2.5 3.1 %collective-permute-start.4 = (bf16[48,2432]{1,0:T(8,128)(2,1)S(1)}, bf16[48,2432]{1,0:T(8,128)(2,1)S(1)}, u32[]{:S(2)}, u32[]{:S(2)}) collective-permute-start(bf16[48,2432]{1,0:T(8,128)(2,1)S(1)} %pad_add_fusion.refs_0_), channel_id=1, source_target_pairs={{0,8},{8,0},{1,9},{9,1},{2,10},{10,2},{3,11},{11,3},{4,12},{12,4},... | collective-permute-start | bytes 700424 | tf_op jit(solution)/shard_map/ppermute | solution.py:478
  3.0 6.7 %collective-permute-start = (bf16[48,2432]{1,0:T(8,128)(2,1)S(1)}, bf16[48,2432]{1,0:T(8,128)(2,1)S(1)}, u32[]{:S(2)}, u32[]{:S(2)}) collective-permute-start(bf16[48,2432]{1,0:T(8,128)(2,1)S(1)} %pad_add_fusion.refs_0_), channel_id=1, source_target_pairs={{0,1},{8,10},{1,3},{9,8},{3,5},{11,9},{5,7},{13,11},{7,6},{15,13},... | collective-permute-start | bytes 700424 | tf_op jit(solution)/shard_map/ppermute | solution.py:473
  5.6 6.6 %collective-permute-start.5 = (bf16[48,2432]{1,0:T(8,128)(2,1)S(1)}, bf16[48,2432]{1,0:T(8,128)(2,1)S(1)}, u32[]{:S(2)}, u32[]{:S(2)}) collective-permute-start(bf16[48,2432]{1,0:T(8,128)(2,1)S(1)} %collective-permute-done.4.refs_5_), channel_id=1, source_target_pairs={{0,1},{8,10},{1,3},{9,8},{3,5},{11,9},{5,7},{13,11},{7,6},{15,13},... | collective-permute-start | bytes 700424 | tf_op jit(solution)/shard_map/ppermute | solution.py:473
  9.7 6.1 %collective-permute-start.1 = (bf16[48,2432]{1,0:T(8,128)(2,1)S(1)}, bf16[48,2432]{1,0:T(8,128)(2,1)S(1)}, u32[]{:S(2)}, u32[]{:S(2)}) collective-permute-start(bf16[48,2432]{1,0:T(8,128)(2,1)S(1)} %collective-permute-done.refs_1_), channel_id=1, source_target_pairs={{0,1},{8,10},{1,3},{9,8},{3,5},{11,9},{5,7},{13,11},{7,6},{15,13},... | collective-permute-start | bytes 700424 | tf_op jit(solution)/shard_map/ppermute | solution.py:473
  12.2 6.1 %collective-permute-start.6 = (bf16[48,2432]{1,0:T(8,128)(2,1)S(1)}, bf16[48,2432]{1,0:T(8,128)(2,1)S(1)}, u32[]{:S(2)}, u32[]{:S(2)}) collective-permute-start(bf16[48,2432]{1,0:T(8,128)(2,1)S(1)} %collective-permute-done.5.refs_6_), channel_id=1, source_target_pairs={{0,1},{8,10},{1,3},{9,8},{3,5},{11,9},{5,7},{13,11},{7,6},{15,13},... | collective-permute-start | bytes 700424 | tf_op jit(solution)/shard_map/ppermute | solution.py:473
  15.8 6.1 %collective-permute-start.2 = (bf16[48,2432]{1,0:T(8,128)(2,1)S(1)}, bf16[48,2432]{1,0:T(8,128)(2,1)S(1)}, u32[]{:S(2)}, u32[]{:S(2)}) collective-permute-start(bf16[48,2432]{1,0:T(8,128)(2,1)S(1)} %collective-permute-done.1.refs_2_), channel_id=1, source_target_pairs={{0,1},{8,10},{1,3},{9,8},{3,5},{11,9},{5,7},{13,11},{7,6},{15,13},... | collective-permute-start | bytes 700424 | tf_op jit(solution)/shard_map/ppermute | solution.py:473
  17.7 6.1 %collective-permute-start.8 = (bf16[48,2432]{1,0:T(8,128)(2,1)S(1)}, bf16[48,2432]{1,0:T(8,128)(2,1)S(1)}, u32[]{:S(2)}, u32[]{:S(2)}) collective-permute-start(bf16[48,2432]{1,0:T(8,128)(2,1)S(1)} %collective-permute-done.refs_1_), channel_id=1, source_target_pairs={{0,8},{8,0},{1,9},{9,1},{2,10},{10,2},{3,11},{11,3},{4,12},{12,4},... | collective-permute-start | bytes 700424 | tf_op jit(solution)/shard_map/ppermute | solution.py:486
  17.7 6.6 %collective-permute-start.12 = (bf16[48,2432]{1,0:T(8,128)(2,1)S(1)}, bf16[48,2432]{1,0:T(8,128)(2,1)S(1)}, u32[]{:S(2)}, u32[]{:S(2)}) collective-permute-start(bf16[48,2432]{1,0:T(8,128)(2,1)S(1)} %collective-permute-done.5.refs_6_), channel_id=1, source_target_pairs={{0,8},{8,0},{1,9},{9,1},{2,10},{10,2},{3,11},{11,3},{4,12},{12,4},... | collective-permute-start | bytes 700424 | tf_op jit(solution)/shard_map/ppermute | solution.py:486
  18.3 6.1 %collective-permute-start.7 = (bf16[48,2432]{1,0:T(8,128)(2,1)S(1)}, bf16[48,2432]{1,0:T(8,128)(2,1)S(1)}, u32[]{:S(2)}, u32[]{:S(2)}) collective-permute-start(bf16[48,2432]{1,0:T(8,128)(2,1)S(1)} %collective-permute-done.6.refs_7_), channel_id=1, source_target_pairs={{0,1},{8,10},{1,3},{9,8},{3,5},{11,9},{5,7},{13,11},{7,6},{15,13},... | collective-permute-start | bytes 700424 | tf_op jit(solution)/shard_map/ppermute | solution.py:473
  21.8 6.1 %collective-permute-start.3 = (bf16[48,2432]{1,0:T(8,128)(2,1)S(1)}, bf16[48,2432]{1,0:T(8,128)(2,1)S(1)}, u32[]{:S(2)}, u32[]{:S(2)}) collective-permute-start(bf16[48,2432]{1,0:T(8,128)(2,1)S(1)} %collective-permute-done.2.refs_3_), channel_id=1, source_target_pairs={{0,1},{8,10},{1,3},{9,8},{3,5},{11,9},{5,7},{13,11},{7,6},{15,13},... | collective-permute-start | bytes 700424 | tf_op jit(solution)/shard_map/ppermute | solution.py:473
  23.8 4.8 %collective-permute-start.9 = (bf16[48,2432]{1,0:T(8,128)(2,1)S(1)}, bf16[48,2432]{1,0:T(8,128)(2,1)S(1)}, u32[]{:S(2)}, u32[]{:S(2)}) collective-permute-start(bf16[48,2432]{1,0:T(8,128)(2,1)S(1)} %collective-permute-done.1.refs_2_), channel_id=1, source_target_pairs={{0,8},{8,0},{1,9},{9,1},{2,10},{10,2},{3,11},{11,3},{4,12},{12,4},... | collective-permute-start | bytes 700424 | tf_op jit(solution)/shard_map/ppermute | solution.py:486
  23.8 4.8 %collective-permute-start.13 = (bf16[48,2432]{1,0:T(8,128)(2,1)S(1)}, bf16[48,2432]{1,0:T(8,128)(2,1)S(1)}, u32[]{:S(2)}, u32[]{:S(2)}) collective-permute-start(bf16[48,2432]{1,0:T(8,128)(2,1)S(1)} %collective-permute-done.6.refs_7_), channel_id=1, source_target_pairs={{0,8},{8,0},{1,9},{9,1},{2,10},{10,2},{3,11},{11,3},{4,12},{12,4},... | collective-permute-start | bytes 700424 | tf_op jit(solution)/shard_map/ppermute | solution.py:486
  24.3 4.3 %collective-permute-start.10 = (bf16[48,2432]{1,0:T(8,128)(2,1)S(1)}, bf16[48,2432]{1,0:T(8,128)(2,1)S(1)}, u32[]{:S(2)}, u32[]{:S(2)}) collective-permute-start(bf16[48,2432]{1,0:T(8,128)(2,1)S(1)} %collective-permute-done.2.refs_3_), channel_id=1, source_target_pairs={{0,8},{8,0},{1,9},{9,1},{2,10},{10,2},{3,11},{11,3},{4,12},{12,4},... | collective-permute-start | bytes 700424 | tf_op jit(solution)/shard_map/ppermute | solution.py:486
  24.4 4.3 %collective-permute-start.14 = (bf16[48,2432]{1,0:T(8,128)(2,1)S(1)}, bf16[48,2432]{1,0:T(8,128)(2,1)S(1)}, u32[]{:S(2)}, u32[]{:S(2)}) collective-permute-start(bf16[48,2432]{1,0:T(8,128)(2,1)S(1)} %collective-permute-done.7.refs_8_), channel_id=1, source_target_pairs={{0,8},{8,0},{1,9},{9,1},{2,10},{10,2},{3,11},{11,3},{4,12},{12,4},... | collective-permute-start | bytes 700424 | tf_op jit(solution)/shard_map/ppermute | solution.py:486
  27.9 1.6 %collective-permute-start.11 = (bf16[48,2432]{1,0:T(8,128)(2,1)S(1)}, bf16[48,2432]{1,0:T(8,128)(2,1)}, u32[]{:S(2)}, u32[]{:S(2)}) collective-permute-start(bf16[48,2432]{1,0:T(8,128)(2,1)S(1)} %collective-permute-done.3.refs_4_), channel_id=1, source_target_pairs={{0,8},{8,0},{1,9},{9,1},{2,10},{10,2},{3,11},{11,3},{4,12},{12,4},... | collective-permute-start | bytes 700424 | tf_op jit(solution)/shard_map/ppermute | solution.py:486
  29.5 0.9 %copy-start = (bf16[2,1,82,384]{3,0,2,1:T(2,128)(2,1)S(1)}, bf16[2,1,82,384]{3,0,2,1:T(2,128)(2,1)}, u32[]{:S(2)}) copy-start(bf16[2,1,82,384]{3,0,2,1:T(2,128)(2,1)} %param.11) | copy-start | bytes 377860
  30.4 0.9 %copy-start.1 = (bf16[2,1,82,384]{3,0,2,1:T(2,128)(2,1)S(1)}, bf16[2,1,82,384]{3,0,2,1:T(2,128)(2,1)}, u32[]{:S(2)}) copy-start(bf16[2,1,82,384]{3,0,2,1:T(2,128)(2,1)} %param.12) | copy-start | bytes 377860
  36.5 4.7 %collective-permute-start.15 = (bf16[2,1,82,384]{3,2,1,0:T(8,128)(2,1)S(1)}, bf16[2,1,82,384]{3,2,1,0:T(8,128)(2,1)S(1)}, u32[]{:S(2)}, u32[]{:S(2)}) collective-permute-start(bf16[2,1,82,384]{3,2,1,0:T(8,128)(2,1)S(1)} %get-tuple-element.44), channel_id=1, source_target_pairs={{0,16},{1,17},{2,18},{3,19},{4,20},{5,21},{6,22},{7,23},{8,24},{9,... | collective-permute-start | bytes 377864 | tf_op jit(solution)/shard_map/ppermute | solution.py:567
  43.9 9.8 %collective-permute-start.16 = (bf16[2,1,82,384]{3,2,1,0:T(8,128)(2,1)S(1)}, bf16[2,1,82,384]{3,2,1,0:T(8,128)(2,1)S(1)}, u32[]{:S(2)}, u32[]{:S(2)}) collective-permute-start(bf16[2,1,82,384]{3,2,1,0:T(8,128)(2,1)S(1)} %get-tuple-element.47.own), channel_id=1, source_target_pairs={{16,0},{17,1},{18,2},{19,3},{20,4},{21,5},{22,6},{23,7},{24,8},{25... | collective-permute-start | bytes 377864 | tf_op jit(solution)/shard_map/ppermute | solution.py:576
  58.0 2.2 %collective-permute-start.18 = (bf16[3,48,2432]{2,1,0:T(8,128)(2,1)S(1)}, bf16[3,48,2432]{2,1,0:T(8,128)(2,1)S(1)}, u32[]{:S(2)}, u32[]{:S(2)}) collective-permute-start(bf16[3,48,2432]{2,1,0:T(8,128)(2,1)S(1)} %slice.74), channel_id=1, source_target_pairs={{0,8},{8,0},{1,9},{9,1},{2,10},{10,2},{3,11},{11,3},{4,12},{12,4},... | collective-permute-start | bytes 2101256 | tf_op jit(solution)/shard_map/ppermute | solution.py:495
  58.9 10.5 %collective-permute-start.17 = (bf16[5,48,2432]{2,1,0:T(8,128)(2,1)S(1)}, bf16[5,48,2432]{2,1,0:T(8,128)(2,1)S(1)}, u32[]{:S(2)}, u32[]{:S(2)}) collective-permute-start(bf16[5,48,2432]{2,1,0:T(8,128)(2,1)S(1)} %slice.67), channel_id=1, source_target_pairs={{0,8},{8,0},{1,9},{9,1},{2,10},{10,2},{3,11},{11,3},{4,12},{12,4},... | collective-permute-start | bytes 3502088 | tf_op jit(solution)/shard_map/ppermute | solution.py:496
  60.3 6.3 %collective-permute-start.19 = (bf16[48,2432]{1,0:T(8,128)(2,1)S(1)}, bf16[48,2432]{1,0:T(8,128)(2,1)S(1)}, u32[]{:S(2)}, u32[]{:S(2)}) collective-permute-start(bf16[48,2432]{1,0:T(8,128)(2,1)S(1)} %get-tuple-element.89), channel_id=1, source_target_pairs={{0,1},{8,10},{1,3},{9,8},{3,5},{11,9},{5,7},{13,11},{7,6},{15,13},... | collective-permute-start | bytes 700424 | tf_op jit(solution)/shard_map/ppermute | solution.py:473
  63.3 6.1 %collective-permute-start.21 = (bf16[48,2432]{1,0:T(8,128)(2,1)S(1)}, bf16[48,2432]{1,0:T(8,128)(2,1)S(1)}, u32[]{:S(2)}, u32[]{:S(2)}) collective-permute-start(bf16[48,2432]{1,0:T(8,128)(2,1)S(1)} %get-tuple-element.88), channel_id=1, source_target_pairs={{0,1},{8,10},{1,3},{9,8},{3,5},{11,9},{5,7},{13,11},{7,6},{15,13},... | collective-permute-start | bytes 700424 | tf_op jit(solution)/shard_map/ppermute | solution.py:473
  66.7 6.1 %collective-permute-start.20 = (bf16[48,2432]{1,0:T(8,128)(2,1)S(1)}, bf16[48,2432]{1,0:T(8,128)(2,1)S(1)}, u32[]{:S(2)}, u32[]{:S(2)}) collective-permute-start(bf16[48,2432]{1,0:T(8,128)(2,1)S(1)} %fusion.2), channel_id=1, source_target_pairs={{0,1},{8,10},{1,3},{9,8},{3,5},{11,9},{5,7},{13,11},{7,6},{15,13},... | collective-permute-start | bytes 700424 | tf_op jit(solution)/shard_map/ppermute | solution.py:473
  69.5 6.1 %collective-permute-start.23 = (bf16[48,2432]{1,0:T(8,128)(2,1)S(1)}, bf16[48,2432]{1,0:T(8,128)(2,1)S(1)}, u32[]{:S(2)}, u32[]{:S(2)}) collective-permute-start(bf16[48,2432]{1,0:T(8,128)(2,1)S(1)} %fusion.1), channel_id=1, source_target_pairs={{0,1},{8,10},{1,3},{9,8},{3,5},{11,9},{5,7},{13,11},{7,6},{15,13},... | collective-permute-start | bytes 700424 | tf_op jit(solution)/shard_map/ppermute | solution.py:473
  73.0 6.1 %collective-permute-start.22 = (bf16[48,2432]{1,0:T(8,128)(2,1)S(1)}, bf16[48,2432]{1,0:T(8,128)(2,1)S(1)}, u32[]{:S(2)}, u32[]{:S(2)}) collective-permute-start(bf16[48,2432]{1,0:T(8,128)(2,1)S(1)} %fusion.3), channel_id=1, source_target_pairs={{0,1},{8,10},{1,3},{9,8},{3,5},{11,9},{5,7},{13,11},{7,6},{15,13},... | collective-permute-start | bytes 700424 | tf_op jit(solution)/shard_map/ppermute | solution.py:473
  75.7 6.1 %collective-permute-start.25 = (bf16[48,2432]{1,0:T(8,128)(2,1)S(1)}, bf16[48,2432]{1,0:T(8,128)(2,1)S(1)}, u32[]{:S(2)}, u32[]{:S(2)}) collective-permute-start(bf16[48,2432]{1,0:T(8,128)(2,1)S(1)} %fusion), channel_id=1, source_target_pairs={{0,1},{8,10},{1,3},{9,8},{3,5},{11,9},{5,7},{13,11},{7,6},{15,13},... | collective-permute-start | bytes 700424 | tf_op jit(solution)/shard_map/ppermute | solution.py:473
  79.2 6.1 %collective-permute-start.24 = (bf16[48,2432]{1,0:T(8,128)(2,1)S(1)}, bf16[48,2432]{1,0:T(8,128)(2,1)S(1)}, u32[]{:S(2)}, u32[]{:S(2)}) collective-permute-start(bf16[48,2432]{1,0:T(8,128)(2,1)S(1)} %fusion.4), channel_id=1, source_target_pairs={{0,1},{8,10},{1,3},{9,8},{3,5},{11,9},{5,7},{13,11},{7,6},{15,13},... | collective-permute-start | bytes 700424 | tf_op jit(solution)/shard_map/ppermute | solution.py:473
  81.8 3.5 %collective-permute-start.26 = (bf16[48,2432]{1,0:T(8,128)(2,1)S(1)}, bf16[48,2432]{1,0:T(8,128)(2,1)S(1)}, u32[]{:S(2)}, u32[]{:S(2)}) collective-permute-start(bf16[48,2432]{1,0:T(8,128)(2,1)S(1)} %collective-permute-done.25), channel_id=1, source_target_pairs={{0,8},{8,0},{1,9},{9,1},{2,10},{10,2},{3,11},{11,3},{4,12},{12,4},... | collective-permute-start | bytes 700424 | tf_op jit(solution)/shard_map/ppermute | solution.py:514

commit v4 on v3

--- a/solution.py
+++ b/solution.py
@@ -68,10 +68,10 @@
         self.fh = hidden // 2
         self.heads = self.half // HD
         self.o_out = 3 * self.half
-        self.o_up = self.o_out + self.half
+        self.o_ext = self.o_out + self.half
+        self.o_up = self.o_ext + EXT
         self.o_down = self.o_up + self.fh
-        self.cols = self.o_down + self.fh
-        self.packed = self.cols + EXT
+        self.packed = self.o_down + self.fh
         self.rows = 2 * ROW_STEP
         self.o_vecs = width
         self.o_image = width + 16
@@ -254,7 +254,7 @@
             up_piece = up[:, f * up_share : (f + 1) * up_share]
             up_piece = jnp.concatenate([up_piece, jnp.zeros((1, EXT - up_share), F32)], axis=1)
             piece = jnp.concatenate([piece, up_piece, jnp.zeros((block - 9, EXT), F32)], axis=0)
-            grads[slots[t][f], :, dm.cols :] = piece.astype(BF)
+            grads[slots[t][f], :, dm.o_ext : dm.o_up] = piece.astype(BF)
 
 
 def spread(dm, ref, get):
@@ -272,53 +272,65 @@
     return dict(zip(shapes, refs)), refs[len(shapes) :]
 
 
-def kernel_first(dm, layout, ring, count_ref, tokens, out_grad, *refs):
-    pieces, refs = refs[:-8], refs[-8:]
-    w, out, proj, probs, mixed, rows, extra, sems = refs
+def padded_images(dm, ref, out, rows, raw, sem):
+    copy = pltpu.make_async_copy(ref, raw, sem.at[0])
+    copy.start()
+    rows[dm.seq : 96, :] = jnp.zeros((96 - dm.seq, dm.width), F32)
+    copy.wait()
+    value = raw[...].astype(F32)
+    for m in range(2):
+        rows[0 : dm.seq, :] = value[:, m, :]
+        out[m] = rows[...].astype(BF)
+
+
+def kernel_tokens(dm, tokens, out, rows, raw, sem):
+    padded_images(dm, tokens, out, rows, raw, sem)
+
+
+def kernel_cotangents(dm, count_ref, out_grad, out, rows, raw, sem):
+    live = [live_of(count_ref, m) for m in range(2)]
+    out[2, 0:16, :] = jnp.concatenate(
+        [jnp.full((1, dm.width), v, F32) for v in live] + [jnp.zeros((14, dm.width), F32)], axis=0
+    ).astype(BF)
+    padded_images(dm, out_grad, out, rows, raw, sem)
+
+
+def kernel_first(dm, layout, ring, images, cotangents, *refs):
+    pieces, refs = refs[:-7], refs[-7:]
+    w, out, proj, probs, mixed, rows, sems = refs
     st = dict(proj=proj, probs=probs, mixed=mixed)
     block = dm.width // dm.shards
-    early, late = [], []
+    early, late, owners = [], [], {}
     if ring:
         place = picked(RING_PLACE, lax.axis_index("fsdp"))
-    for n, (t, array, row, offset, start, stop) in enumerate(layout):
+        sign = 1 - 2 * lax.axis_index("tensor")
+    for n, (t, array, row, offset) in enumerate(layout):
         if ring:
-            owner = jnp.where(
-                lax.axis_index("tensor") == 0,
-                picked([GRID_RING[(p + offset) % dm.shards] for p in range(dm.shards)], place),
-                picked([GRID_RING[(p - offset) % dm.shards] for p in range(dm.shards)], place),
-            )
-            where = pl.ds(pl.multiple_of(owner * block, 16), block)
+            key = offset % dm.shards
+            if key not in owners:
+                there = lax.rem(place + sign * key + 2 * dm.shards, dm.shards)
+                owners[key] = pl.multiple_of(picked(GRID_RING, there) * block, 16)
+            where = pl.ds(owners[key], block)
         else:
-            owner = offset
             where = pl.ds(offset * block, block)
-        bounds = (0, dm.o_up, dm.cols, dm.packed)
-        for j in range(3):
-            lo, hi = max(start, bounds[j]), min(stop, bounds[j + 1])
-            if lo < hi:
-                target = extra.at[t, owner] if j == 2 else w.at[t, where, pl.ds(lo, hi - lo)]
-                source = pieces[array].at[pl.ds(row, block), pl.ds(lo - start, hi - lo)]
-                copy = pltpu.make_async_copy(source, target, sems.at[j, n])
-                (late if j == 1 else early).append(copy)
+        for j, (lo, hi) in enumerate(((0, dm.o_up), (dm.o_up, dm.packed))):
+            source = pieces[array].at[pl.ds(row, block), pl.ds(lo, hi - lo)]
+            copy = pltpu.make_async_copy(source, w.at[t, where, pl.ds(lo, hi - lo)], sems.at[j, n])
+            (early, late)[j].append(copy)
     for copy in early + late:
         copy.start()
-    live = [live_of(count_ref, m) for m in range(2)]
-
-    def put(start):
-        for m in range(2):
-            value = jnp.concatenate([rows[m * ROW_STEP : (m + 1) * ROW_STEP, :], jnp.zeros((8, dm.width), F32)], axis=0)
-            w[m, start : start + 96, 0 : dm.width] = value.astype(BF)
-
-    value = out_grad[...].astype(F32)
-    spread(dm, rows, lambda m: value[:, m, :] * live[m])
-    put(dm.o_grad)
-    value = tokens[...].astype(F32)
-    spread(dm, rows, lambda m: value[:, m, :])
-    put(dm.o_image)
+    for m in range(2):
+        w[m, dm.o_image : dm.o_grad, 0 : dm.width] = images[m]
+        w[m, dm.o_grad : dm.w_rows, 0 : dm.width] = cotangents[m]
+        rows[m * ROW_STEP : (m + 1) * ROW_STEP, :] = images[m].astype(F32)[0:ROW_STEP]
     for copy in early:
         copy.wait()
+    extra = [
+        [w[t, f * block : f * block + 16, dm.o_ext : dm.o_up].astype(F32) for f in range(dm.shards)] for t in range(2)
+    ]
     share, up_share = dm.half // dm.shards, dm.fh // dm.shards
     small = [
-        jnp.concatenate([extra[t, f].astype(F32)[0:8, 0:share] for f in range(dm.shards)], axis=1) for t in range(2)
+        jnp.concatenate([v[0:8, 0:share] for v in extra[t]], axis=1) for t in range(2)
     ]
     own_first = lax.axis_index("tensor") == 0
     straight = jnp.concatenate(small, axis=1)
@@ -326,9 +338,9 @@
     vecs = [jnp.where(own_first, straight, turned)[0:6], straight[6:8]]
     per = dm.fh // dm.width
     for t in range(2):
-        up = jnp.concatenate([extra[t, f].astype(F32)[8:9, 0:up_share] for f in range(dm.shards)], axis=1)
+        up = jnp.concatenate([v[8:9, 0:up_share] for v in extra[t]], axis=1)
         vecs += [up[:, j * dm.width : (j + 1) * dm.width] for j in range(per)]
-    vecs += [jnp.full((1, dm.width), v, F32) for v in live]
+    vecs.append(cotangents[2, 0:16, :].astype(F32)[0:2])
     vecs.append(jnp.zeros((6 - 2 * per, dm.width), F32))
     vecs = jnp.concatenate(vecs, axis=0)
     w[0, dm.o_vecs : dm.o_image, 0 : dm.width] = vecs.astype(BF)
@@ -353,7 +365,7 @@
 
 
 def live_of(count_ref, m):
-    return (lax.axis_index("tensor") < count_ref[m, 0]).astype(F32)
+    return (lax.axis_index("tensor") < count_ref[0, m]).astype(F32)
 
 
 def ring_slots(dm, ring):
@@ -397,6 +409,10 @@
     @pl.when(last)
     def _():
         take(dm.o_grad)
+        for m in range(2):
+            rows[m * ROW_STEP : (m + 1) * ROW_STEP, :] = (
+                rows[m * ROW_STEP : (m + 1) * ROW_STEP, :] * vecs[12 + m : 13 + m]
+            )
         grad = layer_backward(dm, rows[...], w, vecs, st, ct, work)
         for m in range(2):
             grad_in[m, 0] = image(dm, grad, m).astype(BF)
@@ -440,7 +456,7 @@
     g_out[...] = total(every, dm.o_out, half)
     g_up[...] = total(every, dm.o_up, fh)
     g_down[...] = total(every, dm.o_down, fh)
-    ext = total(slice(0, 16), dm.cols, EXT)
+    ext = total(slice(0, 16), dm.o_ext, EXT)
     share, up_share = half // dm.shards, fh // dm.shards
     g_gain[0] = ext[0:2, 0:share]
     g_shift[0] = ext[2:6, 0:share]
@@ -473,7 +489,7 @@
     return lax.ppermute(value, ("tensor", "fsdp"), route)
 
 
-def gather_ring(block, cycle, swap):
+def gather_ring(block, images, cycle, swap):
     far = len(cycle) // 2
     own, other = [block], [lax.ppermute(block, "tensor", swap)]
     for step in range(far):
@@ -483,13 +499,18 @@
     found, places = own + other, [(0, -s) for s in range(far + 1)] + [(1, -s) for s in range(far)]
     for t, values in ((1, own), (0, other)):
         for step in range(1, len(values)):
-            found.append(lax.ppermute(values[step], "tensor", swap))
+            value = values[step]
+            if t == 1 and step < far and step % 2 == 1:
+                n = step // 2
+                value, ready = lax.optimization_barrier((value, images[n]))
+                images = images[:n] + [ready] + images[n + 1 :]
+            found.append(lax.ppermute(value, "tensor", swap))
             places.append((t, step))
-    layout = [(t, i, 0, offset, 0, block.shape[1]) for i, (t, offset) in enumerate(places)]
-    return found, layout
-
-
-def reduce_ring(blocks, cycle, swap):
+    layout = [(t, i, 0, offset) for i, (t, offset) in enumerate(places)]
+    return found, layout, images
+
+
+def reduce_ring(blocks, outputs, cycle, swap):
     count = len(cycle)
     early = 3
     first = lax.ppermute(blocks[count : count + early], "tensor", swap)
@@ -512,7 +533,8 @@
             sent = part(i + 1, after(other, sent))
             other = onward(sent, cycle)
     other = lax.ppermute(other, "tensor", swap)
-    return blocks[count - 1], later[count - 1 - early], own, other
+    outputs = after(outputs, sent)
+    return (blocks[count - 1], later[count - 1 - early], own, other), outputs
 
 
 def per_device(tokens, out_grad, image_count, w_qkv, w_out, w_up, w_down, head_bias, up_bias, gains, shifts):
@@ -524,17 +546,30 @@
     block = width // dm.shards
     swap = [(0, 1), (1, 0)]
     vectors = (head_bias, up_bias, gains, shifts)
+    raw = [jnp.transpose(v[:, 0], (1, 0, 2)) for v in (tokens, out_grad)]
+    space = [pltpu.VMEM((96, width), F32), pltpu.VMEM((seq, 2, width), BF), pltpu.SemaphoreType.DMA((1,))]
+    images = [
+        call(functools.partial(kernel_tokens, dm), [AN], [((2, 96, width), BF)], raw[:1], space)[0],
+        call(
+            functools.partial(kernel_cotangents, dm),
+            [SM, AN],
+            [((3, 96, width), BF)],
+            (image_count.T, raw[1]),
+            space,
+        )[0],
+    ]
     if ring:
         places = [(w_qkv[0, :, k], 0, k * dm.half) for k in range(3)]
         places += [(w_out[0].T, 0, dm.o_out), (w_up[0], 0, dm.o_up), (w_down[0].T, 0, dm.o_down)]
-        places += [(v, r, dm.cols) for v, r in ((gains[0], 0), (shifts[0], 2), (head_bias[0], 6), (up_bias, 8))]
+        places += [(v, r, dm.o_ext) for v, r in ((gains[0], 0), (shifts[0], 2), (head_bias[0], 6), (up_bias, 8))]
         packed = sum(
             jnp.pad(v, ((r, block - r - v.shape[0]), (c, dm.packed - c - v.shape[1]))) for v, r, c in places
         )
-        found, layout = gather_ring(packed, GRID_RING, swap)
+        found, layout, images = gather_ring(packed, images, GRID_RING, swap)
     else:
         rows = jnp.concatenate([w_qkv[0].reshape(w_qkv.shape[1], -1), w_out[0].T, w_up[0], w_down[0].T], axis=1)
         rows = lax.all_gather(rows, "fsdp", axis=0, tiled=True)
+        front = dm.o_ext
         small = jnp.concatenate([gains[0], shifts[0], head_bias[0]], axis=0)
         small = lax.all_gather(small, "fsdp", axis=1, tiled=True)
         up = lax.all_gather(up_bias, "fsdp", axis=1, tiled=True)
@@ -548,9 +583,9 @@
             ],
             axis=1,
         )
-        rows = jnp.concatenate([rows, ext.reshape(width, EXT)], axis=1)
+        rows = jnp.concatenate([rows[:, :front], ext.reshape(width, EXT), rows[:, front:]], axis=1)
         found = [rows, lax.ppermute(rows, "tensor", swap)]
-        layout = [(t, t, i * block, i, 0, dm.packed) for t in range(2) for i in range(dm.shards)]
+        layout = [(t, t, i * block, i) for t in range(2) for i in range(dm.shards)]
     states = dm.state_shapes()
     cotangents = dm.cotangent_shapes()
     shape = tokens.shape
@@ -558,11 +593,11 @@
     work = buffers(dm.work_shapes().values())
     w, low0 = call(
         functools.partial(kernel_first, dm, layout, ring),
-        [SM, VM, VM] + [AN] * len(found),
-        [((2, dm.w_rows, dm.cols), BF), (shape, BF)],
-        (image_count,) + tuple(jnp.transpose(v[:, 0], (1, 0, 2)) for v in (tokens, out_grad)) + tuple(found),
+        [VM, VM] + [AN] * len(found),
+        [((2, dm.w_rows, dm.packed), BF), (shape, BF)],
+        (*images, *found),
         scratch=buffers([states["proj"], states["probs"], states["mixed"], ((dm.rows, width), F32)])
-        + [pltpu.VMEM((2, dm.shards, block, EXT), BF), pltpu.SemaphoreType.DMA((3, len(layout)))],
+        + [pltpu.SemaphoreType.DMA((2, len(layout)))],
     )
     h1 = lax.ppermute(low0, "section", [(0, 1)])
     kept = list(states.values()) + list(cotangents.values())
@@ -582,7 +617,7 @@
         scratch=buffers(cotangents.values()) + work,
     )
     if ring:
-        terms = reduce_ring(blocks, GRID_RING, swap)
+        terms, (acts, in_grads) = reduce_ring(blocks, (acts, in_grads), GRID_RING, swap)
         shapes = [(3, block, dm.half), (block, dm.half), (block, dm.fh), (block, dm.fh)] + [v.shape for v in vectors]
         g_qkv, g_out, g_up, g_down, *small = call(
             functools.partial(kernel_unpack, dm), [VM] * len(terms), [(v, F32) for v in shapes], terms
@@ -593,17 +628,19 @@
         mine = blocks[: dm.shards].astype(F32)
         mine += lax.ppermute(blocks[dm.shards :], "tensor", swap).astype(F32)
         mine = mine.reshape(width, dm.packed)
-        body = lax.psum_scatter(mine[:, : dm.cols], "fsdp", scatter_dimension=0, tiled=True)
+        body = jnp.concatenate([mine[:, : dm.o_ext], mine[:, dm.o_up :]], axis=1)
+        body = lax.psum_scatter(body, "fsdp", scatter_dimension=0, tiled=True)
+        up_at, down_at = dm.o_ext, dm.o_ext + dm.fh
         share, up_share = half // dm.shards, dm.fh // dm.shards
-        ext = mine[:, dm.cols :].reshape(dm.shards, block, EXT)
+        ext = mine[:, dm.o_ext : dm.o_up].reshape(dm.shards, block, EXT)
         small = jnp.moveaxis(ext[:, 0:8, 0:share], 0, 1).reshape(8, half)
         small = lax.psum_scatter(small, "fsdp", scatter_dimension=1, tiled=True)
         up = lax.psum_scatter(ext[:, 8, 0:up_share].reshape(-1), "fsdp", scatter_dimension=0, tiled=True)
         grads = [
             body[:, : 3 * half].reshape(w_qkv.shape),
-            body[:, dm.o_out : dm.o_up].T[None],
-            body[:, dm.o_up : dm.o_down][None],
-            body[:, dm.o_down :].T[None],
+            body[:, dm.o_out : up_at].T[None],
+            body[:, up_at : down_at][None],
+            body[:, down_at:].T[None],
             small[6:8][None],
             up[None],
             small[0:2][None],

time: 86.5 us -> 83.5 us (0.965)
  waiting for transfers between devices: 32.9 us -> 30.8 us
    ppermute x14, waiting for transfers between devices: 19.6 us -> 15.8 us  [onward(): return lax.ppermute(value, ('tensor', 'fsdp'), route)]
    unnamed x7 -> x8, local copies, waits for them, and re-layouts: 4.04 us -> 3.95 us
    pallas_call x4 -> x6, Pallas kernels: 13 us -> 13 us  [call(): pl.pallas_call(kernel, in_specs=ins, out_specs=[VM] * len(outs), out_shap...]
  transfers between devices with their start and end apart: 27 -> 27, of which waited for: 16 -> 18; matrix products, arithmetic and copies ran while one was open for 3% -> 3% of each run, Pallas kernels for 0% -> 1%
where the time goes in v4:
time: 83.5 us; the launch traced here: 83.2 us
  starting transfers between devices  32.1 us (38%)
  waiting for transfers between devices  30.8 us (37%)
  Pallas kernels  13 us (16%)
  local copies, waits for them, and re-layouts  4.9 us (6%)
  other arithmetic  1.69 us (2%)
    ppermute x14, starting transfers between devices, onward(): return lax.ppermute(value, ('tensor', 'fsdp'), route)  26.7 us
    ppermute x14, waiting for transfers between devices, onward(): return lax.ppermute(value, ('tensor', 'fsdp'), route)  15.8 us
    pallas_call x6, Pallas kernels, call(): pl.pallas_call(kernel, in_specs=ins, out_specs=[VM] * len(outs), out_shap...  13 us
    ppermute x1, waiting for transfers between devices, per_device(): incoming = lax.ppermute(grad1, 'section', [(1, 0)])  8.6 us
    unnamed x8, local copies, waits for them, and re-layouts  3.95 us
    ppermute x1, waiting for transfers between devices, per_device(): h1 = lax.ppermute(low0, 'section', [(0, 1)])  3.38 us
  transfers between devices with their start and end apart: 27, of which 18 were waited for; matrix products, arithmetic and copies ran while one was open for 3% of the time, Pallas kernels for 1%

profile of v4, /device:TPU:0, one launch (start us, length us, event | category | flops | bytes accessed | tf_op | source)
XLA Modules:
  0.0 83.2 jit_solution(15379331244625222418)
XLA Ops:
  0.6 0.8 slice_bitcast_fusion.4
  1.4 1.1 %pad_add_fusion.refs_0_ = bf16[48,2432]{1,0:T(8,128)(2,1)S(1)} fusion(bf16[1,96]{1,0:T(2,128)(2,1)} %param.19, bf16[2,24]{1,0:T(2,128)(2,1)} %bitcast.72, bf16[4,24]{1,0:T(4,128)(2,1)} %bitcast.71, bf16[2,24]{1,0:T(2,128)(2,1)} %bitcast.73, bf16[48,768]{1,0:T(8,128)(2,1)} %bitcast.68, bf16[48,768]{1,0:T(8,128)(2,1)} %bitcast.69, ...), kind=kLoop, calls=%fused_computation.16 | loop fusion | flops 2334720 | bytes 455232 | tf_op jit(solution)/shard_map/add | solution.py:565
  2.5 0.5 collective-permute-start.4
  3.0 2.6 %collective-permute-start = (bf16[48,2432]{1,0:T(8,128)(2,1)S(1)}, bf16[48,2432]{1,0:T(8,128)(2,1)S(1)}, u32[]{:S(2)}, u32[]{:S(2)}) collective-permute-start(bf16[48,2432]{1,0:T(8,128)(2,1)S(1)} %pad_add_fusion.refs_0_), channel_id=1, source_target_pairs={{0,1},{8,10},{1,3},{9,8},{3,5},{11,9},{5,7},{13,11},{7,6},{15,13},... | collective-permute-start | bytes 700424 | tf_op jit(solution)/shard_map/ppermute | solution.py:489
  5.6 1.6 %collective-permute-start.5 = (bf16[48,2432]{1,0:T(8,128)(2,1)S(1)}, bf16[48,2432]{1,0:T(8,128)(2,1)S(1)}, u32[]{:S(2)}, u32[]{:S(2)}) collective-permute-start(bf16[48,2432]{1,0:T(8,128)(2,1)S(1)} %collective-permute-done.4.refs_5_), channel_id=1, source_target_pairs={{0,1},{8,10},{1,3},{9,8},{3,5},{11,9},{5,7},{13,11},{7,6},{15,13},... | collective-permute-start | bytes 700424 | tf_op jit(solution)/shard_map/ppermute | solution.py:489
  7.2 2.5 %collective-permute-done.refs_1_ = bf16[48,2432]{1,0:T(8,128)(2,1)S(1)} collective-permute-done((bf16[48,2432]{1,0:T(8,128)(2,1)S(1)}, bf16[48,2432]{1,0:T(8,128)(2,1)S(1)}, u32[]{:S(2)}, u32[]{:S(2)}) %collective-permute-start) | collective-permute-done | bytes 233504 | tf_op jit(solution)/shard_map/ppermute | solution.py:489
  9.7 2.0 %collective-permute-start.1 = (bf16[48,2432]{1,0:T(8,128)(2,1)S(1)}, bf16[48,2432]{1,0:T(8,128)(2,1)S(1)}, u32[]{:S(2)}, u32[]{:S(2)}) collective-permute-start(bf16[48,2432]{1,0:T(8,128)(2,1)S(1)} %collective-permute-done.refs_1_), channel_id=1, source_target_pairs={{0,1},{8,10},{1,3},{9,8},{3,5},{11,9},{5,7},{13,11},{7,6},{15,13},... | collective-permute-start | bytes 700424 | tf_op jit(solution)/shard_map/ppermute | solution.py:489
  11.7 0.5 collective-permute-done.5.refs_6_
  12.2 2.0 %collective-permute-start.6 = (bf16[48,2432]{1,0:T(8,128)(2,1)S(1)}, bf16[48,2432]{1,0:T(8,128)(2,1)S(1)}, u32[]{:S(2)}, u32[]{:S(2)}) collective-permute-start(bf16[48,2432]{1,0:T(8,128)(2,1)S(1)} %collective-permute-done.5.refs_6_), channel_id=1, source_target_pairs={{0,1},{8,10},{1,3},{9,8},{3,5},{11,9},{5,7},{13,11},{7,6},{15,13},... | collective-permute-start | bytes 700424 | tf_op jit(solution)/shard_map/ppermute | solution.py:489
  14.2 1.6 %collective-permute-done.1.refs_2_ = bf16[48,2432]{1,0:T(8,128)(2,1)S(1)} collective-permute-done((bf16[48,2432]{1,0:T(8,128)(2,1)S(1)}, bf16[48,2432]{1,0:T(8,128)(2,1)S(1)}, u32[]{:S(2)}, u32[]{:S(2)}) %collective-permute-start.1) | collective-permute-done | bytes 233504 | tf_op jit(solution)/shard_map/ppermute | solution.py:489
  15.8 2.0 %collective-permute-start.2 = (bf16[48,2432]{1,0:T(8,128)(2,1)S(1)}, bf16[48,2432]{1,0:T(8,128)(2,1)S(1)}, u32[]{:S(2)}, u32[]{:S(2)}) collective-permute-start(bf16[48,2432]{1,0:T(8,128)(2,1)S(1)} %collective-permute-done.1.refs_2_), channel_id=1, source_target_pairs={{0,1},{8,10},{1,3},{9,8},{3,5},{11,9},{5,7},{13,11},{7,6},{15,13},... | collective-permute-start | bytes 700424 | tf_op jit(solution)/shard_map/ppermute | solution.py:489
  17.7 0.9 %copy-done = bf16[2,1,82,384]{3,0,2,1:T(2,128)(2,1)S(1)} copy-done((bf16[2,1,82,384]{3,0,2,1:T(2,128)(2,1)S(1)}, bf16[2,1,82,384]{3,0,2,1:T(2,128)(2,1)}, u32[]{:S(2)}) %copy-start) | copy-done | bytes 125976
  19.0 0.5 collective-permute-start.12
  19.5 1.6 %collective-permute-start.7 = (bf16[48,2432]{1,0:T(8,128)(2,1)S(1)}, bf16[48,2432]{1,0:T(8,128)(2,1)S(1)}, u32[]{:S(2)}, u32[]{:S(2)}) collective-permute-start(bf16[48,2432]{1,0:T(8,128)(2,1)S(1)} %collective-permute-done.6.refs_7_), channel_id=1, source_target_pairs={{0,1},{8,10},{1,3},{9,8},{3,5},{11,9},{5,7},{13,11},{7,6},{15,13},... | collective-permute-start | bytes 700424 | tf_op jit(solution)/shard_map/ppermute | solution.py:489
  21.1 0.8 collective-permute-done.2.refs_3_
  21.8 2.0 %collective-permute-start.3 = (bf16[48,2432]{1,0:T(8,128)(2,1)S(1)}, bf16[48,2432]{1,0:T(8,128)(2,1)S(1)}, u32[]{:S(2)}, u32[]{:S(2)}) collective-permute-start(bf16[48,2432]{1,0:T(8,128)(2,1)S(1)} %collective-permute-done.2.refs_3_), channel_id=1, source_target_pairs={{0,1},{8,10},{1,3},{9,8},{3,5},{11,9},{5,7},{13,11},{7,6},{15,13},... | collective-permute-start | bytes 700424 | tf_op jit(solution)/shard_map/ppermute | solution.py:489
  23.8 0.9 %copy-done.1 = bf16[2,1,82,384]{3,0,2,1:T(2,128)(2,1)S(1)} copy-done((bf16[2,1,82,384]{3,0,2,1:T(2,128)(2,1)S(1)}, bf16[2,1,82,384]{3,0,2,1:T(2,128)(2,1)}, u32[]{:S(2)}) %copy-start.1) | copy-done | bytes 125976
  24.7 0.7 copy-done.2
  25.4 0.8 %shard_map.187.cotangents = bf16[3,96,384]{2,1,0:T(8,128)(2,1)S(1)} custom-call(s32[1,2]{1,0:T(1,128)S(1)} %bitcast.67, bf16[82,2,384]{2,1,0:T(2,128)(2,1)S(1)} %bitcast.66), custom_call_target="tpu_custom_call" | custom-call | tf_op jit(solution)/shard_map/pallas_call | solution.py:473
  26.3 0.5 collective-permute-start.10
  27.3 0.7 collective-permute-done.3.refs_4_
  28.8 0.8 collective-permute-done.11.refs_12_
  29.5 4.1 %shard_map.188 = (bf16[2,592,2432]{2,1,0:T(8,128)(2,1)S(1)}, bf16[2,1,82,384]{3,2,1,0:T(8,128)(2,1)S(1)}) custom-call(bf16[2,96,384]{2,1,0:T(8,128)(2,1)S(1)} %shard_map.186.images, bf16[3,96,384]{2,1,0:T(8,128)(2,1)S(1)} %shard_map.187.cotangents, bf16[48,2432]{1,0:T(8,128)(2,1)S(1)} %pad_add_fusion.refs_0_, ...), custom_call_target="tpu_custom_call" | custom-call | tf_op jit(solution)/shard_map/pallas_call | solution.py:473
  33.6 1.3 %collective-permute-start.15 = (bf16[2,1,82,384]{3,2,1,0:T(8,128)(2,1)S(1)}, bf16[2,1,82,384]{3,2,1,0:T(8,128)(2,1)S(1)}, u32[]{:S(2)}, u32[]{:S(2)}) collective-permute-start(bf16[2,1,82,384]{3,2,1,0:T(8,128)(2,1)S(1)} %get-tuple-element.54), channel_id=1, source_target_pairs={{0,16},{1,17},{2,18},{3,19},{4,20},{5,21},{6,22},{7,23},{8,24},{9,... | collective-permute-start | bytes 377864 | tf_op jit(solution)/shard_map/ppermute | solution.py:602
  34.9 3.4 %collective-permute-done.15.h1 = bf16[2,1,82,384]{3,2,1,0:T(8,128)(2,1)S(1)} collective-permute-done((bf16[2,1,82,384]{3,2,1,0:T(8,128)(2,1)S(1)}, bf16[2,1,82,384]{3,2,1,0:T(8,128)(2,1)S(1)}, u32[]{:S(2)}, u32[]{:S(2)}) %collective-permute-start.15) | collective-permute-done | bytes 125984 | tf_op jit(solution)/shard_map/ppermute | solution.py:602
  38.3 2.7 %shard_map.189 = (bf16[2,1,82,384]{3,2,1,0:T(8,128)(2,1)S(1)}, bf16[2,1,82,384]{3,2,1,0:T(8,128)(2,1)S(1)}, f32[2,176,576]{2,1,0:T(8,128)S(1)}, f32[12,88,88]{2,...) custom-call(bf16[2,1,82,384]{3,2,1,0:T(8,128)(2,1)S(1)} %collective-, ...), custom_call_target="tpu_custom_call" | custom-call | tf_op jit(solution)/shard_map/pallas_call | solution.py:473
  41.0 1.3 %collective-permute-start.16 = (bf16[2,1,82,384]{3,2,1,0:T(8,128)(2,1)S(1)}, bf16[2,1,82,384]{3,2,1,0:T(8,128)(2,1)S(1)}, u32[]{:S(2)}, u32[]{:S(2)}) collective-permute-start(bf16[2,1,82,384]{3,2,1,0:T(8,128)(2,1)S(1)} %get-tuple-element.57.own), channel_id=1, source_target_pairs={{16,0},{17,1},{18,2},{19,3},{20,4},{21,5},{22,6},{23,7},{24,8},{25... | collective-permute-start | bytes 377864 | tf_op jit(solution)/shard_map/ppermute | solution.py:611
  42.3 8.6 %collective-permute-done.16.incoming = bf16[2,1,82,384]{3,2,1,0:T(8,128)(2,1)S(1)} collective-permute-done((bf16[2,1,82,384]{3,2,1,0:T(8,128)(2,1)S(1)}, bf16[2,1,82,384]{3,2,1,0:T(8,128)(2,1)S(1)}, u32[]{:S(2)}, u32[]{:S(2)}) %collective-permute-start.16) | collective-permute-done | bytes 125984 | tf_op jit(solution)/shard_map/ppermute | solution.py:611
  50.9 4.3 %shard_map.190 = (bf16[2,1,82,384]{3,2,1,0:T(8,128)(2,1)S(1)}, bf16[16,48,2432]{2,1,0:T(8,128)(2,1)S(1)}) custom-call(bf16[2,1,82,384]{3,2,1,0:T(8,128)(2,1)S(1)} %collective-permute-done.16.incoming, bf16[2,592,2432]{2,1,0:T(8,128)(2,1)S(1)} %get-tuple-element.55.w, bf16[2,1,82,384]{3,2,1,0:T(8,128)(2,1)S(1)} %get-tuple-element.57.own, ...), custom_call_target="tpu_custom_call" | custom-call | tf_op jit(solution)/shard_map/pallas_call | solution.py:473
  55.4 0.6 collective-permute-start.17
  56.0 1.5 %collective-permute-done.18 = bf16[3,48,2432]{2,1,0:T(8,128)(2,1)S(1)} collective-permute-done((bf16[3,48,2432]{2,1,0:T(8,128)(2,1)S(1)}, bf16[3,48,2432]{2,1,0:T(8,128)(2,1)S(1)}, u32[]{:S(2)}, u32[]{:S(2)}) %collective-permute-start.18) | collective-permute-done | bytes 700448 | tf_op jit(solution)/shard_map/ppermute | solution.py:516
  57.6 1.9 %collective-permute-start.19 = (bf16[48,2432]{1,0:T(8,128)(2,1)S(1)}, bf16[48,2432]{1,0:T(8,128)(2,1)S(1)}, u32[]{:S(2)}, u32[]{:S(2)}) collective-permute-start(bf16[48,2432]{1,0:T(8,128)(2,1)S(1)} %get-tuple-element.101), channel_id=1, source_target_pairs={{0,1},{8,10},{1,3},{9,8},{3,5},{11,9},{5,7},{13,11},{7,6},{15,13},... | collective-permute-start | bytes 700424 | tf_op jit(solution)/shard_map/ppermute | solution.py:489
  59.5 1.6 %collective-permute-start.21 = (bf16[48,2432]{1,0:T(8,128)(2,1)S(1)}, bf16[48,2432]{1,0:T(8,128)(2,1)S(1)}, u32[]{:S(2)}, u32[]{:S(2)}) collective-permute-start(bf16[48,2432]{1,0:T(8,128)(2,1)S(1)} %get-tuple-element.100), channel_id=1, source_target_pairs={{0,1},{8,10},{1,3},{9,8},{3,5},{11,9},{5,7},{13,11},{7,6},{15,13},... | collective-permute-start | bytes 700424 | tf_op jit(solution)/shard_map/ppermute | solution.py:489
  61.2 2.6 %collective-permute-done.19 = bf16[48,2432]{1,0:T(8,128)(2,1)S(1)} collective-permute-done((bf16[48,2432]{1,0:T(8,128)(2,1)S(1)}, bf16[48,2432]{1,0:T(8,128)(2,1)S(1)}, u32[]{:S(2)}, u32[]{:S(2)}) %collective-permute-start.19) | collective-permute-done | bytes 233504 | tf_op jit(solution)/shard_map/ppermute | solution.py:489
  63.8 1.9 %collective-permute-start.20 = (bf16[48,2432]{1,0:T(8,128)(2,1)S(1)}, bf16[48,2432]{1,0:T(8,128)(2,1)S(1)}, u32[]{:S(2)}, u32[]{:S(2)}) collective-permute-start(bf16[48,2432]{1,0:T(8,128)(2,1)S(1)} %fusion.2), channel_id=1, source_target_pairs={{0,1},{8,10},{1,3},{9,8},{3,5},{11,9},{5,7},{13,11},{7,6},{15,13},... | collective-permute-start | bytes 700424 | tf_op jit(solution)/shard_map/ppermute | solution.py:489
  65.7 0.5 collective-permute-done.21
  66.3 1.9 %collective-permute-start.23 = (bf16[48,2432]{1,0:T(8,128)(2,1)S(1)}, bf16[48,2432]{1,0:T(8,128)(2,1)S(1)}, u32[]{:S(2)}, u32[]{:S(2)}) collective-permute-start(bf16[48,2432]{1,0:T(8,128)(2,1)S(1)} %fusion.1), channel_id=1, source_target_pairs={{0,1},{8,10},{1,3},{9,8},{3,5},{11,9},{5,7},{13,11},{7,6},{15,13},... | collective-permute-start | bytes 700424 | tf_op jit(solution)/shard_map/ppermute | solution.py:489
  68.2 1.7 %collective-permute-done.20 = bf16[48,2432]{1,0:T(8,128)(2,1)S(1)} collective-permute-done((bf16[48,2432]{1,0:T(8,128)(2,1)S(1)}, bf16[48,2432]{1,0:T(8,128)(2,1)S(1)}, u32[]{:S(2)}, u32[]{:S(2)}) %collective-permute-start.20) | collective-permute-done | bytes 233504 | tf_op jit(solution)/shard_map/ppermute | solution.py:489
  70.0 1.9 %collective-permute-start.22 = (bf16[48,2432]{1,0:T(8,128)(2,1)S(1)}, bf16[48,2432]{1,0:T(8,128)(2,1)S(1)}, u32[]{:S(2)}, u32[]{:S(2)}) collective-permute-start(bf16[48,2432]{1,0:T(8,128)(2,1)S(1)} %fusion.3), channel_id=1, source_target_pairs={{0,1},{8,10},{1,3},{9,8},{3,5},{11,9},{5,7},{13,11},{7,6},{15,13},... | collective-permute-start | bytes 700424 | tf_op jit(solution)/shard_map/ppermute | solution.py:489
  71.9 0.5 collective-permute-done.23
  72.5 1.9 %collective-permute-start.25 = (bf16[48,2432]{1,0:T(8,128)(2,1)S(1)}, bf16[48,2432]{1,0:T(8,128)(2,1)S(1)}, u32[]{:S(2)}, u32[]{:S(2)}) collective-permute-start(bf16[48,2432]{1,0:T(8,128)(2,1)S(1)} %fusion), channel_id=1, source_target_pairs={{0,1},{8,10},{1,3},{9,8},{3,5},{11,9},{5,7},{13,11},{7,6},{15,13},... | collective-permute-start | bytes 700424 | tf_op jit(solution)/shard_map/ppermute | solution.py:489
  74.5 1.7 %collective-permute-done.22 = bf16[48,2432]{1,0:T(8,128)(2,1)S(1)} collective-permute-done((bf16[48,2432]{1,0:T(8,128)(2,1)S(1)}, bf16[48,2432]{1,0:T(8,128)(2,1)S(1)}, u32[]{:S(2)}, u32[]{:S(2)}) %collective-permute-start.22) | collective-permute-done | bytes 233504 | tf_op jit(solution)/shard_map/ppermute | solution.py:489
  76.3 1.9 %collective-permute-start.24 = (bf16[48,2432]{1,0:T(8,128)(2,1)S(1)}, bf16[48,2432]{1,0:T(8,128)(2,1)S(1)}, u32[]{:S(2)}, u32[]{:S(2)}) collective-permute-start(bf16[48,2432]{1,0:T(8,128)(2,1)S(1)} %fusion.4), channel_id=1, source_target_pairs={{0,1},{8,10},{1,3},{9,8},{3,5},{11,9},{5,7},{13,11},{7,6},{15,13},... | collective-permute-start | bytes 700424 | tf_op jit(solution)/shard_map/ppermute | solution.py:489
  78.2 0.5 collective-permute-done.25
  78.7 0.7 copy.21
  79.4 0.7 copy.22
  80.2 2.2 %collective-permute-done.24.refs_2_ = bf16[48,2432]{1,0:T(8,128)(2,1)S(1)} collective-permute-done((bf16[48,2432]{1,0:T(8,128)(2,1)S(1)}, bf16[48,2432]{1,0:T(8,128)(2,1)S(1)}, u32[]{:S(2)}, u32[]{:S(2)}) %collective-permute-start.24) | collective-permute-done | bytes 233504 | tf_op jit(solution)/shard_map/ppermute | solution.py:489
  82.4 0.9 %shard_map.191 = (f32[3,48,192]{2,1,0:T(8,128)}, f32[48,192]{1,0:T(8,128)}, f32[48,768]{1,0:T(8,128)}, f32[48,768]{1,0:T(8,128)}, f32[1,2,24]{2,1,0:T(2,128)}, /...) custom-call(bf16[48,2432]{1,0:T(8,128)(2,1)S(1)} %slice_bitcast_fusion.1.refs_0_, ...), custom_call_target="tpu_custom_call" | custom-call | tf_op jit(solution)/shard_map/pallas_call | solution.py:473
  (32 shorter events, 2.5 us)
Async XLA Ops:
  2.5 3.1 %collective-permute-start.4 = (bf16[48,2432]{1,0:T(8,128)(2,1)S(1)}, bf16[48,2432]{1,0:T(8,128)(2,1)S(1)}, u32[]{:S(2)}, u32[]{:S(2)}) collective-permute-start(bf16[48,2432]{1,0:T(8,128)(2,1)S(1)} %pad_add_fusion.refs_0_), channel_id=1, source_target_pairs={{0,8},{8,0},{1,9},{9,1},{2,10},{10,2},{3,11},{11,3},{4,12},{12,4},... | collective-permute-start | bytes 700424 | tf_op jit(solution)/shard_map/ppermute | solution.py:494
  3.0 6.7 %collective-permute-start = (bf16[48,2432]{1,0:T(8,128)(2,1)S(1)}, bf16[48,2432]{1,0:T(8,128)(2,1)S(1)}, u32[]{:S(2)}, u32[]{:S(2)}) collective-permute-start(bf16[48,2432]{1,0:T(8,128)(2,1)S(1)} %pad_add_fusion.refs_0_), channel_id=1, source_target_pairs={{0,1},{8,10},{1,3},{9,8},{3,5},{11,9},{5,7},{13,11},{7,6},{15,13},... | collective-permute-start | bytes 700424 | tf_op jit(solution)/shard_map/ppermute | solution.py:489
  5.6 6.6 %collective-permute-start.5 = (bf16[48,2432]{1,0:T(8,128)(2,1)S(1)}, bf16[48,2432]{1,0:T(8,128)(2,1)S(1)}, u32[]{:S(2)}, u32[]{:S(2)}) collective-permute-start(bf16[48,2432]{1,0:T(8,128)(2,1)S(1)} %collective-permute-done.4.refs_5_), channel_id=1, source_target_pairs={{0,1},{8,10},{1,3},{9,8},{3,5},{11,9},{5,7},{13,11},{7,6},{15,13},... | collective-permute-start | bytes 700424 | tf_op jit(solution)/shard_map/ppermute | solution.py:489
  9.7 6.1 %collective-permute-start.1 = (bf16[48,2432]{1,0:T(8,128)(2,1)S(1)}, bf16[48,2432]{1,0:T(8,128)(2,1)S(1)}, u32[]{:S(2)}, u32[]{:S(2)}) collective-permute-start(bf16[48,2432]{1,0:T(8,128)(2,1)S(1)} %collective-permute-done.refs_1_), channel_id=1, source_target_pairs={{0,1},{8,10},{1,3},{9,8},{3,5},{11,9},{5,7},{13,11},{7,6},{15,13},... | collective-permute-start | bytes 700424 | tf_op jit(solution)/shard_map/ppermute | solution.py:489
  12.2 7.3 %collective-permute-start.6 = (bf16[48,2432]{1,0:T(8,128)(2,1)S(1)}, bf16[48,2432]{1,0:T(8,128)(2,1)S(1)}, u32[]{:S(2)}, u32[]{:S(2)}) collective-permute-start(bf16[48,2432]{1,0:T(8,128)(2,1)S(1)} %collective-permute-done.5.refs_6_), channel_id=1, source_target_pairs={{0,1},{8,10},{1,3},{9,8},{3,5},{11,9},{5,7},{13,11},{7,6},{15,13},... | collective-permute-start | bytes 700424 | tf_op jit(solution)/shard_map/ppermute | solution.py:489
  15.8 6.1 %collective-permute-start.2 = (bf16[48,2432]{1,0:T(8,128)(2,1)S(1)}, bf16[48,2432]{1,0:T(8,128)(2,1)S(1)}, u32[]{:S(2)}, u32[]{:S(2)}) collective-permute-start(bf16[48,2432]{1,0:T(8,128)(2,1)S(1)} %collective-permute-done.1.refs_2_), channel_id=1, source_target_pairs={{0,1},{8,10},{1,3},{9,8},{3,5},{11,9},{5,7},{13,11},{7,6},{15,13},... | collective-permute-start | bytes 700424 | tf_op jit(solution)/shard_map/ppermute | solution.py:489
  17.7 0.9 %copy-start = (bf16[2,1,82,384]{3,0,2,1:T(2,128)(2,1)S(1)}, bf16[2,1,82,384]{3,0,2,1:T(2,128)(2,1)}, u32[]{:S(2)}) copy-start(bf16[2,1,82,384]{3,0,2,1:T(2,128)(2,1)} %param.11) | copy-start | bytes 377860
  18.9 7.4 %collective-permute-start.8 = (bf16[48,2432]{1,0:T(8,128)(2,1)S(1)}, bf16[48,2432]{1,0:T(8,128)(2,1)S(1)}, u32[]{:S(2)}, u32[]{:S(2)}) collective-permute-start(bf16[48,2432]{1,0:T(8,128)(2,1)S(1)} %collective-permute-done.refs_1_), channel_id=1, source_target_pairs={{0,8},{8,0},{1,9},{9,1},{2,10},{10,2},{3,11},{11,3},{4,12},{12,4},... | collective-permute-start | bytes 700424 | tf_op jit(solution)/shard_map/ppermute | solution.py:507
  19.0 7.8 %collective-permute-start.12 = (bf16[48,2432]{1,0:T(8,128)(2,1)S(1)}, bf16[48,2432]{1,0:T(8,128)(2,1)S(1)}, u32[]{:S(2)}, u32[]{:S(2)}) collective-permute-start(bf16[48,2432]{1,0:T(8,128)(2,1)S(1)} %collective-permute-done.5.refs_6_), channel_id=1, source_target_pairs={{0,8},{8,0},{1,9},{9,1},{2,10},{10,2},{3,11},{11,3},{4,12},{12,4},... | collective-permute-start | bytes 700424 | tf_op jit(solution)/shard_map/ppermute | solution.py:507
  19.5 7.4 %collective-permute-start.7 = (bf16[48,2432]{1,0:T(8,128)(2,1)S(1)}, bf16[48,2432]{1,0:T(8,128)(2,1)S(1)}, u32[]{:S(2)}, u32[]{:S(2)}) collective-permute-start(bf16[48,2432]{1,0:T(8,128)(2,1)S(1)} %collective-permute-done.6.refs_7_), channel_id=1, source_target_pairs={{0,1},{8,10},{1,3},{9,8},{3,5},{11,9},{5,7},{13,11},{7,6},{15,13},... | collective-permute-start | bytes 700424 | tf_op jit(solution)/shard_map/ppermute | solution.py:489
  21.8 6.2 %collective-permute-start.3 = (bf16[48,2432]{1,0:T(8,128)(2,1)S(1)}, bf16[48,2432]{1,0:T(8,128)(2,1)S(1)}, u32[]{:S(2)}, u32[]{:S(2)}) collective-permute-start(bf16[48,2432]{1,0:T(8,128)(2,1)S(1)} %collective-permute-done.2.refs_3_), channel_id=1, source_target_pairs={{0,1},{8,10},{1,3},{9,8},{3,5},{11,9},{5,7},{13,11},{7,6},{15,13},... | collective-permute-start | bytes 700424 | tf_op jit(solution)/shard_map/ppermute | solution.py:489
  23.8 0.9 %copy-start.1 = (bf16[2,1,82,384]{3,0,2,1:T(2,128)(2,1)S(1)}, bf16[2,1,82,384]{3,0,2,1:T(2,128)(2,1)}, u32[]{:S(2)}) copy-start(bf16[2,1,82,384]{3,0,2,1:T(2,128)(2,1)} %param.12) | copy-start | bytes 377860
  24.7 0.7 copy-start.2
  26.2 1.8 %collective-permute-start.9 = (bf16[48,2432]{1,0:T(8,128)(2,1)S(1)}, bf16[48,2432]{1,0:T(8,128)(2,1)S(1)}, u32[]{:S(2)}, u32[]{:S(2)}) collective-permute-start(bf16[48,2432]{1,0:T(8,128)(2,1)S(1)} %collective-permute-done.1.refs_2_), channel_id=1, source_target_pairs={{0,8},{8,0},{1,9},{9,1},{2,10},{10,2},{3,11},{11,3},{4,12},{12,4},... | collective-permute-start | bytes 700424 | tf_op jit(solution)/shard_map/ppermute | solution.py:507
  26.3 2.1 %collective-permute-start.10 = (bf16[48,2432]{1,0:T(8,128)(2,1)S(1)}, bf16[48,2432]{1,0:T(8,128)(2,1)S(1)}, u32[]{:S(2)}, u32[]{:S(2)}) collective-permute-start(bf16[48,2432]{1,0:T(8,128)(2,1)S(1)} %collective-permute-done.2.refs_3_), channel_id=1, source_target_pairs={{0,8},{8,0},{1,9},{9,1},{2,10},{10,2},{3,11},{11,3},{4,12},{12,4},... | collective-permute-start | bytes 700424 | tf_op jit(solution)/shard_map/ppermute | solution.py:507
  26.8 1.6 %collective-permute-start.13 = (bf16[48,2432]{1,0:T(8,128)(2,1)S(1)}, bf16[48,2432]{1,0:T(8,128)(2,1)S(1)}, u32[]{:S(2)}, u32[]{:S(2)}) collective-permute-start(bf16[48,2432]{1,0:T(8,128)(2,1)S(1)} %collective-permute-done.6.refs_7_), channel_id=1, source_target_pairs={{0,8},{8,0},{1,9},{9,1},{2,10},{10,2},{3,11},{11,3},{4,12},{12,4},... | collective-permute-start | bytes 700424 | tf_op jit(solution)/shard_map/ppermute | solution.py:507
  26.9 1.9 %collective-permute-start.14 = (bf16[48,2432]{1,0:T(8,128)(2,1)S(1)}, bf16[48,2432]{1,0:T(8,128)(2,1)S(1)}, u32[]{:S(2)}, u32[]{:S(2)}) collective-permute-start(bf16[48,2432]{1,0:T(8,128)(2,1)S(1)} %collective-permute-done.7.refs_8_), channel_id=1, source_target_pairs={{0,8},{8,0},{1,9},{9,1},{2,10},{10,2},{3,11},{11,3},{4,12},{12,4},... | collective-permute-start | bytes 700424 | tf_op jit(solution)/shard_map/ppermute | solution.py:507
  28.0 1.5 %collective-permute-start.11 = (bf16[48,2432]{1,0:T(8,128)(2,1)S(1)}, bf16[48,2432]{1,0:T(8,128)(2,1)S(1)}, u32[]{:S(2)}, u32[]{:S(2)}) collective-permute-start(bf16[48,2432]{1,0:T(8,128)(2,1)S(1)} %collective-permute-done.3.refs_4_), channel_id=1, source_target_pairs={{0,8},{8,0},{1,9},{9,1},{2,10},{10,2},{3,11},{11,3},{4,12},{12,4},... | collective-permute-start | bytes 700424 | tf_op jit(solution)/shard_map/ppermute | solution.py:507
  33.6 4.7 %collective-permute-start.15 = (bf16[2,1,82,384]{3,2,1,0:T(8,128)(2,1)S(1)}, bf16[2,1,82,384]{3,2,1,0:T(8,128)(2,1)S(1)}, u32[]{:S(2)}, u32[]{:S(2)}) collective-permute-start(bf16[2,1,82,384]{3,2,1,0:T(8,128)(2,1)S(1)} %get-tuple-element.54), channel_id=1, source_target_pairs={{0,16},{1,17},{2,18},{3,19},{4,20},{5,21},{6,22},{7,23},{8,24},{9,... | collective-permute-start | bytes 377864 | tf_op jit(solution)/shard_map/ppermute | solution.py:602
  41.0 9.9 %collective-permute-start.16 = (bf16[2,1,82,384]{3,2,1,0:T(8,128)(2,1)S(1)}, bf16[2,1,82,384]{3,2,1,0:T(8,128)(2,1)S(1)}, u32[]{:S(2)}, u32[]{:S(2)}) collective-permute-start(bf16[2,1,82,384]{3,2,1,0:T(8,128)(2,1)S(1)} %get-tuple-element.57.own), channel_id=1, source_target_pairs={{16,0},{17,1},{18,2},{19,3},{20,4},{21,5},{22,6},{23,7},{24,8},{25... | collective-permute-start | bytes 377864 | tf_op jit(solution)/shard_map/ppermute | solution.py:611
  55.2 2.2 %collective-permute-start.18 = (bf16[3,48,2432]{2,1,0:T(8,128)(2,1)S(1)}, bf16[3,48,2432]{2,1,0:T(8,128)(2,1)S(1)}, u32[]{:S(2)}, u32[]{:S(2)}) collective-permute-start(bf16[3,48,2432]{2,1,0:T(8,128)(2,1)S(1)} %slice.72), channel_id=1, source_target_pairs={{0,8},{8,0},{1,9},{9,1},{2,10},{10,2},{3,11},{11,3},{4,12},{12,4},... | collective-permute-start | bytes 2101256 | tf_op jit(solution)/shard_map/ppermute | solution.py:516
  55.4 10.8 %collective-permute-start.17 = (bf16[5,48,2432]{2,1,0:T(8,128)(2,1)S(1)}, bf16[5,48,2432]{2,1,0:T(8,128)(2,1)S(1)}, u32[]{:S(2)}, u32[]{:S(2)}) collective-permute-start(bf16[5,48,2432]{2,1,0:T(8,128)(2,1)S(1)} %slice.67), channel_id=1, source_target_pairs={{0,8},{8,0},{1,9},{9,1},{2,10},{10,2},{3,11},{11,3},{4,12},{12,4},... | collective-permute-start | bytes 3502088 | tf_op jit(solution)/shard_map/ppermute | solution.py:517
  57.6 6.1 %collective-permute-start.19 = (bf16[48,2432]{1,0:T(8,128)(2,1)S(1)}, bf16[48,2432]{1,0:T(8,128)(2,1)S(1)}, u32[]{:S(2)}, u32[]{:S(2)}) collective-permute-start(bf16[48,2432]{1,0:T(8,128)(2,1)S(1)} %get-tuple-element.101), channel_id=1, source_target_pairs={{0,1},{8,10},{1,3},{9,8},{3,5},{11,9},{5,7},{13,11},{7,6},{15,13},... | collective-permute-start | bytes 700424 | tf_op jit(solution)/shard_map/ppermute | solution.py:489
  59.5 6.7 %collective-permute-start.21 = (bf16[48,2432]{1,0:T(8,128)(2,1)S(1)}, bf16[48,2432]{1,0:T(8,128)(2,1)S(1)}, u32[]{:S(2)}, u32[]{:S(2)}) collective-permute-start(bf16[48,2432]{1,0:T(8,128)(2,1)S(1)} %get-tuple-element.100), channel_id=1, source_target_pairs={{0,1},{8,10},{1,3},{9,8},{3,5},{11,9},{5,7},{13,11},{7,6},{15,13},... | collective-permute-start | bytes 700424 | tf_op jit(solution)/shard_map/ppermute | solution.py:489
  63.8 6.1 %collective-permute-start.20 = (bf16[48,2432]{1,0:T(8,128)(2,1)S(1)}, bf16[48,2432]{1,0:T(8,128)(2,1)S(1)}, u32[]{:S(2)}, u32[]{:S(2)}) collective-permute-start(bf16[48,2432]{1,0:T(8,128)(2,1)S(1)} %fusion.2), channel_id=1, source_target_pairs={{0,1},{8,10},{1,3},{9,8},{3,5},{11,9},{5,7},{13,11},{7,6},{15,13},... | collective-permute-start | bytes 700424 | tf_op jit(solution)/shard_map/ppermute | solution.py:489
  66.3 6.1 %collective-permute-start.23 = (bf16[48,2432]{1,0:T(8,128)(2,1)S(1)}, bf16[48,2432]{1,0:T(8,128)(2,1)S(1)}, u32[]{:S(2)}, u32[]{:S(2)}) collective-permute-start(bf16[48,2432]{1,0:T(8,128)(2,1)S(1)} %fusion.1), channel_id=1, source_target_pairs={{0,1},{8,10},{1,3},{9,8},{3,5},{11,9},{5,7},{13,11},{7,6},{15,13},... | collective-permute-start | bytes 700424 | tf_op jit(solution)/shard_map/ppermute | solution.py:489
  70.0 6.1 %collective-permute-start.22 = (bf16[48,2432]{1,0:T(8,128)(2,1)S(1)}, bf16[48,2432]{1,0:T(8,128)(2,1)S(1)}, u32[]{:S(2)}, u32[]{:S(2)}) collective-permute-start(bf16[48,2432]{1,0:T(8,128)(2,1)S(1)} %fusion.3), channel_id=1, source_target_pairs={{0,1},{8,10},{1,3},{9,8},{3,5},{11,9},{5,7},{13,11},{7,6},{15,13},... | collective-permute-start | bytes 700424 | tf_op jit(solution)/shard_map/ppermute | solution.py:489
  72.5 6.1 %collective-permute-start.25 = (bf16[48,2432]{1,0:T(8,128)(2,1)S(1)}, bf16[48,2432]{1,0:T(8,128)(2,1)S(1)}, u32[]{:S(2)}, u32[]{:S(2)}) collective-permute-start(bf16[48,2432]{1,0:T(8,128)(2,1)S(1)} %fusion), channel_id=1, source_target_pairs={{0,1},{8,10},{1,3},{9,8},{3,5},{11,9},{5,7},{13,11},{7,6},{15,13},... | collective-permute-start | bytes 700424 | tf_op jit(solution)/shard_map/ppermute | solution.py:489
  76.3 6.1 %collective-permute-start.24 = (bf16[48,2432]{1,0:T(8,128)(2,1)S(1)}, bf16[48,2432]{1,0:T(8,128)(2,1)S(1)}, u32[]{:S(2)}, u32[]{:S(2)}) collective-permute-start(bf16[48,2432]{1,0:T(8,128)(2,1)S(1)} %fusion.4), channel_id=1, source_target_pairs={{0,1},{8,10},{1,3},{9,8},{3,5},{11,9},{5,7},{13,11},{7,6},{15,13},... | collective-permute-start | bytes 700424 | tf_op jit(solution)/shard_map/ppermute | solution.py:489
  78.7 3.7 %collective-permute-start.26 = (bf16[48,2432]{1,0:T(8,128)(2,1)S(1)}, bf16[48,2432]{1,0:T(8,128)(2,1)S(1)}, u32[]{:S(2)}, u32[]{:S(2)}) collective-permute-start(bf16[48,2432]{1,0:T(8,128)(2,1)S(1)} %collective-permute-done.25), channel_id=1, source_target_pairs={{0,8},{8,0},{1,9},{9,1},{2,10},{10,2},{3,11},{11,3},{4,12},{12,4},... | collective-permute-start | bytes 700424 | tf_op jit(solution)/shard_map/ppermute | solution.py:535

commit v5 on v4

--- a/solution.py
+++ b/solution.py
@@ -512,9 +512,8 @@
 
 def reduce_ring(blocks, outputs, cycle, swap):
     count = len(cycle)
-    early = 3
+    early = 2
     first = lax.ppermute(blocks[count : count + early], "tensor", swap)
-    later = lax.ppermute(blocks[count + early :], "tensor", swap)
 
     def part(i, *more):
         given = first[i] if i < early else later[i - early]
@@ -523,7 +522,9 @@
     def after(value, sent):
         return lax.optimization_barrier((value, sent))[0]
 
-    own = onward(part(0), cycle)
+    sent = part(0)
+    own = onward(sent, cycle)
+    later = lax.ppermute(after(blocks[count + early :], sent), "tensor", swap)
     sent = part(1)
     other = onward(sent, cycle)
     for i in range(2, count, 2):

time: 83.5 us -> 83.3 us (level)
  no operation moved by 1% of the time
where the time goes in v5:
time: 83.3 us; the launch traced here: 83 us
  starting transfers between devices  31.7 us (38%)
  waiting for transfers between devices  31 us (37%)
  Pallas kernels  13 us (16%)
  local copies, waits for them, and re-layouts  4.9 us (6%)
  other arithmetic  1.68 us (2%)
    ppermute x14, starting transfers between devices, onward(): return lax.ppermute(value, ('tensor', 'fsdp'), route)  26.6 us
    ppermute x14, waiting for transfers between devices, onward(): return lax.ppermute(value, ('tensor', 'fsdp'), route)  15.8 us
    pallas_call x6, Pallas kernels, call(): pl.pallas_call(kernel, in_specs=ins, out_specs=[VM] * len(outs), out_shap...  13 us
    ppermute x1, waiting for transfers between devices, per_device(): incoming = lax.ppermute(grad1, 'section', [(1, 0)])  8.6 us
    unnamed x8, local copies, waits for them, and re-layouts  3.95 us
    ppermute x1, waiting for transfers between devices, per_device(): h1 = lax.ppermute(low0, 'section', [(0, 1)])  3.38 us
    ppermute x1, waiting for transfers between devices, reduce_ring(): first = lax.ppermute(blocks[count:count + early], 'tensor', swap)  1.71 us
  transfers between devices with their start and end apart: 27, of which 18 were waited for; matrix products, arithmetic and copies ran while one was open for 3% of the time, Pallas kernels for 1%

profile of v5, /device:TPU:0, one launch (start us, length us, event | category | flops | bytes accessed | tf_op | source)
XLA Modules:
  0.0 83.0 jit_solution(16223781344303397980)
XLA Ops:
  0.6 0.8 slice_bitcast_fusion.4
  1.4 1.1 %pad_add_fusion.refs_0_ = bf16[48,2432]{1,0:T(8,128)(2,1)S(1)} fusion(bf16[1,96]{1,0:T(2,128)(2,1)} %param.19, bf16[2,24]{1,0:T(2,128)(2,1)} %bitcast.72, bf16[4,24]{1,0:T(4,128)(2,1)} %bitcast.71, bf16[2,24]{1,0:T(2,128)(2,1)} %bitcast.73, bf16[48,768]{1,0:T(8,128)(2,1)} %bitcast.68, bf16[48,768]{1,0:T(8,128)(2,1)} %bitcast.69, ...), kind=kLoop, calls=%fused_computation.16 | loop fusion | flops 2334720 | bytes 455232 | tf_op jit(solution)/shard_map/add | solution.py:566
  2.5 0.5 collective-permute-start.4
  3.0 2.6 %collective-permute-start = (bf16[48,2432]{1,0:T(8,128)(2,1)S(1)}, bf16[48,2432]{1,0:T(8,128)(2,1)S(1)}, u32[]{:S(2)}, u32[]{:S(2)}) collective-permute-start(bf16[48,2432]{1,0:T(8,128)(2,1)S(1)} %pad_add_fusion.refs_0_), channel_id=1, source_target_pairs={{0,1},{8,10},{1,3},{9,8},{3,5},{11,9},{5,7},{13,11},{7,6},{15,13},... | collective-permute-start | bytes 700424 | tf_op jit(solution)/shard_map/ppermute | solution.py:489
  5.6 1.6 %collective-permute-start.5 = (bf16[48,2432]{1,0:T(8,128)(2,1)S(1)}, bf16[48,2432]{1,0:T(8,128)(2,1)S(1)}, u32[]{:S(2)}, u32[]{:S(2)}) collective-permute-start(bf16[48,2432]{1,0:T(8,128)(2,1)S(1)} %collective-permute-done.4.refs_5_), channel_id=1, source_target_pairs={{0,1},{8,10},{1,3},{9,8},{3,5},{11,9},{5,7},{13,11},{7,6},{15,13},... | collective-permute-start | bytes 700424 | tf_op jit(solution)/shard_map/ppermute | solution.py:489
  7.2 2.5 %collective-permute-done.refs_1_ = bf16[48,2432]{1,0:T(8,128)(2,1)S(1)} collective-permute-done((bf16[48,2432]{1,0:T(8,128)(2,1)S(1)}, bf16[48,2432]{1,0:T(8,128)(2,1)S(1)}, u32[]{:S(2)}, u32[]{:S(2)}) %collective-permute-start) | collective-permute-done | bytes 233504 | tf_op jit(solution)/shard_map/ppermute | solution.py:489
  9.7 2.0 %collective-permute-start.1 = (bf16[48,2432]{1,0:T(8,128)(2,1)S(1)}, bf16[48,2432]{1,0:T(8,128)(2,1)S(1)}, u32[]{:S(2)}, u32[]{:S(2)}) collective-permute-start(bf16[48,2432]{1,0:T(8,128)(2,1)S(1)} %collective-permute-done.refs_1_), channel_id=1, source_target_pairs={{0,1},{8,10},{1,3},{9,8},{3,5},{11,9},{5,7},{13,11},{7,6},{15,13},... | collective-permute-start | bytes 700424 | tf_op jit(solution)/shard_map/ppermute | solution.py:489
  11.7 0.5 collective-permute-done.5.refs_6_
  12.2 2.0 %collective-permute-start.6 = (bf16[48,2432]{1,0:T(8,128)(2,1)S(1)}, bf16[48,2432]{1,0:T(8,128)(2,1)S(1)}, u32[]{:S(2)}, u32[]{:S(2)}) collective-permute-start(bf16[48,2432]{1,0:T(8,128)(2,1)S(1)} %collective-permute-done.5.refs_6_), channel_id=1, source_target_pairs={{0,1},{8,10},{1,3},{9,8},{3,5},{11,9},{5,7},{13,11},{7,6},{15,13},... | collective-permute-start | bytes 700424 | tf_op jit(solution)/shard_map/ppermute | solution.py:489
  14.2 1.6 %collective-permute-done.1.refs_2_ = bf16[48,2432]{1,0:T(8,128)(2,1)S(1)} collective-permute-done((bf16[48,2432]{1,0:T(8,128)(2,1)S(1)}, bf16[48,2432]{1,0:T(8,128)(2,1)S(1)}, u32[]{:S(2)}, u32[]{:S(2)}) %collective-permute-start.1) | collective-permute-done | bytes 233504 | tf_op jit(solution)/shard_map/ppermute | solution.py:489
  15.8 2.0 %collective-permute-start.2 = (bf16[48,2432]{1,0:T(8,128)(2,1)S(1)}, bf16[48,2432]{1,0:T(8,128)(2,1)S(1)}, u32[]{:S(2)}, u32[]{:S(2)}) collective-permute-start(bf16[48,2432]{1,0:T(8,128)(2,1)S(1)} %collective-permute-done.1.refs_2_), channel_id=1, source_target_pairs={{0,1},{8,10},{1,3},{9,8},{3,5},{11,9},{5,7},{13,11},{7,6},{15,13},... | collective-permute-start | bytes 700424 | tf_op jit(solution)/shard_map/ppermute | solution.py:489
  17.7 0.9 %copy-done = bf16[2,1,82,384]{3,0,2,1:T(2,128)(2,1)S(1)} copy-done((bf16[2,1,82,384]{3,0,2,1:T(2,128)(2,1)S(1)}, bf16[2,1,82,384]{3,0,2,1:T(2,128)(2,1)}, u32[]{:S(2)}) %copy-start) | copy-done | bytes 125976
  19.0 0.5 collective-permute-start.12
  19.5 1.6 %collective-permute-start.7 = (bf16[48,2432]{1,0:T(8,128)(2,1)S(1)}, bf16[48,2432]{1,0:T(8,128)(2,1)S(1)}, u32[]{:S(2)}, u32[]{:S(2)}) collective-permute-start(bf16[48,2432]{1,0:T(8,128)(2,1)S(1)} %collective-permute-done.6.refs_7_), channel_id=1, source_target_pairs={{0,1},{8,10},{1,3},{9,8},{3,5},{11,9},{5,7},{13,11},{7,6},{15,13},... | collective-permute-start | bytes 700424 | tf_op jit(solution)/shard_map/ppermute | solution.py:489
  21.1 0.8 collective-permute-done.2.refs_3_
  21.8 2.0 %collective-permute-start.3 = (bf16[48,2432]{1,0:T(8,128)(2,1)S(1)}, bf16[48,2432]{1,0:T(8,128)(2,1)S(1)}, u32[]{:S(2)}, u32[]{:S(2)}) collective-permute-start(bf16[48,2432]{1,0:T(8,128)(2,1)S(1)} %collective-permute-done.2.refs_3_), channel_id=1, source_target_pairs={{0,1},{8,10},{1,3},{9,8},{3,5},{11,9},{5,7},{13,11},{7,6},{15,13},... | collective-permute-start | bytes 700424 | tf_op jit(solution)/shard_map/ppermute | solution.py:489
  23.8 0.9 %copy-done.1 = bf16[2,1,82,384]{3,0,2,1:T(2,128)(2,1)S(1)} copy-done((bf16[2,1,82,384]{3,0,2,1:T(2,128)(2,1)S(1)}, bf16[2,1,82,384]{3,0,2,1:T(2,128)(2,1)}, u32[]{:S(2)}) %copy-start.1) | copy-done | bytes 125976
  24.7 0.7 copy-done.2
  25.4 0.8 %shard_map.187.cotangents = bf16[3,96,384]{2,1,0:T(8,128)(2,1)S(1)} custom-call(s32[1,2]{1,0:T(1,128)S(1)} %bitcast.67, bf16[82,2,384]{2,1,0:T(2,128)(2,1)S(1)} %bitcast.66), custom_call_target="tpu_custom_call" | custom-call | tf_op jit(solution)/shard_map/pallas_call | solution.py:473
  26.3 0.5 collective-permute-start.10
  26.9 0.4 collective-permute-start.14
  27.3 0.7 collective-permute-done.3.refs_4_
  28.8 0.8 collective-permute-done.11.refs_12_
  29.5 4.1 %shard_map.188 = (bf16[2,592,2432]{2,1,0:T(8,128)(2,1)S(1)}, bf16[2,1,82,384]{3,2,1,0:T(8,128)(2,1)S(1)}) custom-call(bf16[2,96,384]{2,1,0:T(8,128)(2,1)S(1)} %shard_map.186.images, bf16[3,96,384]{2,1,0:T(8,128)(2,1)S(1)} %shard_map.187.cotangents, bf16[48,2432]{1,0:T(8,128)(2,1)S(1)} %pad_add_fusion.refs_0_, ...), custom_call_target="tpu_custom_call" | custom-call | tf_op jit(solution)/shard_map/pallas_call | solution.py:473
  33.6 1.3 %collective-permute-start.15 = (bf16[2,1,82,384]{3,2,1,0:T(8,128)(2,1)S(1)}, bf16[2,1,82,384]{3,2,1,0:T(8,128)(2,1)S(1)}, u32[]{:S(2)}, u32[]{:S(2)}) collective-permute-start(bf16[2,1,82,384]{3,2,1,0:T(8,128)(2,1)S(1)} %get-tuple-element.55), channel_id=1, source_target_pairs={{0,16},{1,17},{2,18},{3,19},{4,20},{5,21},{6,22},{7,23},{8,24},{9,... | collective-permute-start | bytes 377864 | tf_op jit(solution)/shard_map/ppermute | solution.py:603
  34.9 3.4 %collective-permute-done.15.h1 = bf16[2,1,82,384]{3,2,1,0:T(8,128)(2,1)S(1)} collective-permute-done((bf16[2,1,82,384]{3,2,1,0:T(8,128)(2,1)S(1)}, bf16[2,1,82,384]{3,2,1,0:T(8,128)(2,1)S(1)}, u32[]{:S(2)}, u32[]{:S(2)}) %collective-permute-start.15) | collective-permute-done | bytes 125984 | tf_op jit(solution)/shard_map/ppermute | solution.py:603
  38.3 2.7 %shard_map.189 = (bf16[2,1,82,384]{3,2,1,0:T(8,128)(2,1)S(1)}, bf16[2,1,82,384]{3,2,1,0:T(8,128)(2,1)S(1)}, f32[2,176,576]{2,1,0:T(8,128)S(1)}, f32[12,88,88]{2,...) custom-call(bf16[2,1,82,384]{3,2,1,0:T(8,128)(2,1)S(1)} %collective-, ...), custom_call_target="tpu_custom_call" | custom-call | tf_op jit(solution)/shard_map/pallas_call | solution.py:473
  41.0 1.3 %collective-permute-start.16 = (bf16[2,1,82,384]{3,2,1,0:T(8,128)(2,1)S(1)}, bf16[2,1,82,384]{3,2,1,0:T(8,128)(2,1)S(1)}, u32[]{:S(2)}, u32[]{:S(2)}) collective-permute-start(bf16[2,1,82,384]{3,2,1,0:T(8,128)(2,1)S(1)} %get-tuple-element.58.own), channel_id=1, source_target_pairs={{16,0},{17,1},{18,2},{19,3},{20,4},{21,5},{22,6},{23,7},{24,8},{25... | collective-permute-start | bytes 377864 | tf_op jit(solution)/shard_map/ppermute | solution.py:612
  42.3 8.6 %collective-permute-done.16.incoming = bf16[2,1,82,384]{3,2,1,0:T(8,128)(2,1)S(1)} collective-permute-done((bf16[2,1,82,384]{3,2,1,0:T(8,128)(2,1)S(1)}, bf16[2,1,82,384]{3,2,1,0:T(8,128)(2,1)S(1)}, u32[]{:S(2)}, u32[]{:S(2)}) %collective-permute-start.16) | collective-permute-done | bytes 125984 | tf_op jit(solution)/shard_map/ppermute | solution.py:612
  50.9 4.3 %shard_map.190 = (bf16[2,1,82,384]{3,2,1,0:T(8,128)(2,1)S(1)}, bf16[16,48,2432]{2,1,0:T(8,128)(2,1)S(1)}) custom-call(bf16[2,1,82,384]{3,2,1,0:T(8,128)(2,1)S(1)} %collective-permute-done.16.incoming, bf16[2,592,2432]{2,1,0:T(8,128)(2,1)S(1)} %get-tuple-element.56.w, bf16[2,1,82,384]{3,2,1,0:T(8,128)(2,1)S(1)} %get-tuple-element.58.own, ...), custom_call_target="tpu_custom_call" | custom-call | tf_op jit(solution)/shard_map/pallas_call | solution.py:473
  55.4 1.7 %collective-permute-done.17 = bf16[2,48,2432]{2,1,0:T(8,128)(2,1)S(1)} collective-permute-done((bf16[2,48,2432]{2,1,0:T(8,128)(2,1)S(1)}, bf16[2,48,2432]{2,1,0:T(8,128)(2,1)S(1)}, u32[]{:S(2)}, u32[]{:S(2)}) %collective-permute-start.17) | collective-permute-done | bytes 466976 | tf_op jit(solution)/shard_map/ppermute | solution.py:516
  57.4 1.9 %collective-permute-start.19 = (bf16[48,2432]{1,0:T(8,128)(2,1)S(1)}, bf16[48,2432]{1,0:T(8,128)(2,1)S(1)}, u32[]{:S(2)}, u32[]{:S(2)}) collective-permute-start(bf16[48,2432]{1,0:T(8,128)(2,1)S(1)} %get-tuple-element.103), channel_id=1, source_target_pairs={{0,1},{8,10},{1,3},{9,8},{3,5},{11,9},{5,7},{13,11},{7,6},{15,13},... | collective-permute-start | bytes 700424 | tf_op jit(solution)/shard_map/ppermute | solution.py:489
  59.3 1.6 %collective-permute-start.21 = (bf16[48,2432]{1,0:T(8,128)(2,1)S(1)}, bf16[48,2432]{1,0:T(8,128)(2,1)S(1)}, u32[]{:S(2)}, u32[]{:S(2)}) collective-permute-start(bf16[48,2432]{1,0:T(8,128)(2,1)S(1)} %get-tuple-element.102), channel_id=1, source_target_pairs={{0,1},{8,10},{1,3},{9,8},{3,5},{11,9},{5,7},{13,11},{7,6},{15,13},... | collective-permute-start | bytes 700424 | tf_op jit(solution)/shard_map/ppermute | solution.py:489
  60.9 2.6 %collective-permute-done.19 = bf16[48,2432]{1,0:T(8,128)(2,1)S(1)} collective-permute-done((bf16[48,2432]{1,0:T(8,128)(2,1)S(1)}, bf16[48,2432]{1,0:T(8,128)(2,1)S(1)}, u32[]{:S(2)}, u32[]{:S(2)}) %collective-permute-start.19) | collective-permute-done | bytes 233504 | tf_op jit(solution)/shard_map/ppermute | solution.py:489
  63.6 1.9 %collective-permute-start.20 = (bf16[48,2432]{1,0:T(8,128)(2,1)S(1)}, bf16[48,2432]{1,0:T(8,128)(2,1)S(1)}, u32[]{:S(2)}, u32[]{:S(2)}) collective-permute-start(bf16[48,2432]{1,0:T(8,128)(2,1)S(1)} %fusion.2), channel_id=1, source_target_pairs={{0,1},{8,10},{1,3},{9,8},{3,5},{11,9},{5,7},{13,11},{7,6},{15,13},... | collective-permute-start | bytes 700424 | tf_op jit(solution)/shard_map/ppermute | solution.py:489
  65.5 0.5 collective-permute-done.21
  66.1 1.9 %collective-permute-start.23 = (bf16[48,2432]{1,0:T(8,128)(2,1)S(1)}, bf16[48,2432]{1,0:T(8,128)(2,1)S(1)}, u32[]{:S(2)}, u32[]{:S(2)}) collective-permute-start(bf16[48,2432]{1,0:T(8,128)(2,1)S(1)} %fusion.1), channel_id=1, source_target_pairs={{0,1},{8,10},{1,3},{9,8},{3,5},{11,9},{5,7},{13,11},{7,6},{15,13},... | collective-permute-start | bytes 700424 | tf_op jit(solution)/shard_map/ppermute | solution.py:489
  68.0 1.7 %collective-permute-done.20 = bf16[48,2432]{1,0:T(8,128)(2,1)S(1)} collective-permute-done((bf16[48,2432]{1,0:T(8,128)(2,1)S(1)}, bf16[48,2432]{1,0:T(8,128)(2,1)S(1)}, u32[]{:S(2)}, u32[]{:S(2)}) %collective-permute-start.20) | collective-permute-done | bytes 233504 | tf_op jit(solution)/shard_map/ppermute | solution.py:489
  69.8 1.9 %collective-permute-start.22 = (bf16[48,2432]{1,0:T(8,128)(2,1)S(1)}, bf16[48,2432]{1,0:T(8,128)(2,1)S(1)}, u32[]{:S(2)}, u32[]{:S(2)}) collective-permute-start(bf16[48,2432]{1,0:T(8,128)(2,1)S(1)} %fusion.3), channel_id=1, source_target_pairs={{0,1},{8,10},{1,3},{9,8},{3,5},{11,9},{5,7},{13,11},{7,6},{15,13},... | collective-permute-start | bytes 700424 | tf_op jit(solution)/shard_map/ppermute | solution.py:489
  71.8 0.5 collective-permute-done.23
  72.3 1.9 %collective-permute-start.25 = (bf16[48,2432]{1,0:T(8,128)(2,1)S(1)}, bf16[48,2432]{1,0:T(8,128)(2,1)S(1)}, u32[]{:S(2)}, u32[]{:S(2)}) collective-permute-start(bf16[48,2432]{1,0:T(8,128)(2,1)S(1)} %fusion), channel_id=1, source_target_pairs={{0,1},{8,10},{1,3},{9,8},{3,5},{11,9},{5,7},{13,11},{7,6},{15,13},... | collective-permute-start | bytes 700424 | tf_op jit(solution)/shard_map/ppermute | solution.py:489
  74.3 1.7 %collective-permute-done.22 = bf16[48,2432]{1,0:T(8,128)(2,1)S(1)} collective-permute-done((bf16[48,2432]{1,0:T(8,128)(2,1)S(1)}, bf16[48,2432]{1,0:T(8,128)(2,1)S(1)}, u32[]{:S(2)}, u32[]{:S(2)}) %collective-permute-start.22) | collective-permute-done | bytes 233504 | tf_op jit(solution)/shard_map/ppermute | solution.py:489
  76.1 1.9 %collective-permute-start.24 = (bf16[48,2432]{1,0:T(8,128)(2,1)S(1)}, bf16[48,2432]{1,0:T(8,128)(2,1)S(1)}, u32[]{:S(2)}, u32[]{:S(2)}) collective-permute-start(bf16[48,2432]{1,0:T(8,128)(2,1)S(1)} %fusion.4), channel_id=1, source_target_pairs={{0,1},{8,10},{1,3},{9,8},{3,5},{11,9},{5,7},{13,11},{7,6},{15,13},... | collective-permute-start | bytes 700424 | tf_op jit(solution)/shard_map/ppermute | solution.py:489
  78.0 0.5 collective-permute-done.25
  78.5 0.7 copy.21
  79.2 0.7 copy.22
  80.0 2.2 %collective-permute-done.24.refs_2_ = bf16[48,2432]{1,0:T(8,128)(2,1)S(1)} collective-permute-done((bf16[48,2432]{1,0:T(8,128)(2,1)S(1)}, bf16[48,2432]{1,0:T(8,128)(2,1)S(1)}, u32[]{:S(2)}, u32[]{:S(2)}) %collective-permute-start.24) | collective-permute-done | bytes 233504 | tf_op jit(solution)/shard_map/ppermute | solution.py:489
  82.2 0.9 %shard_map.191 = (f32[3,48,192]{2,1,0:T(8,128)}, f32[48,192]{1,0:T(8,128)}, f32[48,768]{1,0:T(8,128)}, f32[48,768]{1,0:T(8,128)}, f32[1,2,24]{2,1,0:T(2,128)}, /...) custom-call(bf16[48,2432]{1,0:T(8,128)(2,1)S(1)} %slice_bitcast_fusion.1.refs_0_, ...), custom_call_target="tpu_custom_call" | custom-call | tf_op jit(solution)/shard_map/pallas_call | solution.py:473
  (32 shorter events, 2.3 us)
Async XLA Ops:
  2.5 3.1 %collective-permute-start.4 = (bf16[48,2432]{1,0:T(8,128)(2,1)S(1)}, bf16[48,2432]{1,0:T(8,128)(2,1)S(1)}, u32[]{:S(2)}, u32[]{:S(2)}) collective-permute-start(bf16[48,2432]{1,0:T(8,128)(2,1)S(1)} %pad_add_fusion.refs_0_), channel_id=1, source_target_pairs={{0,8},{8,0},{1,9},{9,1},{2,10},{10,2},{3,11},{11,3},{4,12},{12,4},... | collective-permute-start | bytes 700424 | tf_op jit(solution)/shard_map/ppermute | solution.py:494
  3.0 6.7 %collective-permute-start = (bf16[48,2432]{1,0:T(8,128)(2,1)S(1)}, bf16[48,2432]{1,0:T(8,128)(2,1)S(1)}, u32[]{:S(2)}, u32[]{:S(2)}) collective-permute-start(bf16[48,2432]{1,0:T(8,128)(2,1)S(1)} %pad_add_fusion.refs_0_), channel_id=1, source_target_pairs={{0,1},{8,10},{1,3},{9,8},{3,5},{11,9},{5,7},{13,11},{7,6},{15,13},... | collective-permute-start | bytes 700424 | tf_op jit(solution)/shard_map/ppermute | solution.py:489
  5.6 6.6 %collective-permute-start.5 = (bf16[48,2432]{1,0:T(8,128)(2,1)S(1)}, bf16[48,2432]{1,0:T(8,128)(2,1)S(1)}, u32[]{:S(2)}, u32[]{:S(2)}) collective-permute-start(bf16[48,2432]{1,0:T(8,128)(2,1)S(1)} %collective-permute-done.4.refs_5_), channel_id=1, source_target_pairs={{0,1},{8,10},{1,3},{9,8},{3,5},{11,9},{5,7},{13,11},{7,6},{15,13},... | collective-permute-start | bytes 700424 | tf_op jit(solution)/shard_map/ppermute | solution.py:489
  9.7 6.1 %collective-permute-start.1 = (bf16[48,2432]{1,0:T(8,128)(2,1)S(1)}, bf16[48,2432]{1,0:T(8,128)(2,1)S(1)}, u32[]{:S(2)}, u32[]{:S(2)}) collective-permute-start(bf16[48,2432]{1,0:T(8,128)(2,1)S(1)} %collective-permute-done.refs_1_), channel_id=1, source_target_pairs={{0,1},{8,10},{1,3},{9,8},{3,5},{11,9},{5,7},{13,11},{7,6},{15,13},... | collective-permute-start | bytes 700424 | tf_op jit(solution)/shard_map/ppermute | solution.py:489
  12.2 7.3 %collective-permute-start.6 = (bf16[48,2432]{1,0:T(8,128)(2,1)S(1)}, bf16[48,2432]{1,0:T(8,128)(2,1)S(1)}, u32[]{:S(2)}, u32[]{:S(2)}) collective-permute-start(bf16[48,2432]{1,0:T(8,128)(2,1)S(1)} %collective-permute-done.5.refs_6_), channel_id=1, source_target_pairs={{0,1},{8,10},{1,3},{9,8},{3,5},{11,9},{5,7},{13,11},{7,6},{15,13},... | collective-permute-start | bytes 700424 | tf_op jit(solution)/shard_map/ppermute | solution.py:489
  15.8 6.1 %collective-permute-start.2 = (bf16[48,2432]{1,0:T(8,128)(2,1)S(1)}, bf16[48,2432]{1,0:T(8,128)(2,1)S(1)}, u32[]{:S(2)}, u32[]{:S(2)}) collective-permute-start(bf16[48,2432]{1,0:T(8,128)(2,1)S(1)} %collective-permute-done.1.refs_2_), channel_id=1, source_target_pairs={{0,1},{8,10},{1,3},{9,8},{3,5},{11,9},{5,7},{13,11},{7,6},{15,13},... | collective-permute-start | bytes 700424 | tf_op jit(solution)/shard_map/ppermute | solution.py:489
  17.7 0.9 %copy-start = (bf16[2,1,82,384]{3,0,2,1:T(2,128)(2,1)S(1)}, bf16[2,1,82,384]{3,0,2,1:T(2,128)(2,1)}, u32[]{:S(2)}) copy-start(bf16[2,1,82,384]{3,0,2,1:T(2,128)(2,1)} %param.11) | copy-start | bytes 377860
  18.9 7.4 %collective-permute-start.8 = (bf16[48,2432]{1,0:T(8,128)(2,1)S(1)}, bf16[48,2432]{1,0:T(8,128)(2,1)S(1)}, u32[]{:S(2)}, u32[]{:S(2)}) collective-permute-start(bf16[48,2432]{1,0:T(8,128)(2,1)S(1)} %collective-permute-done.refs_1_), channel_id=1, source_target_pairs={{0,8},{8,0},{1,9},{9,1},{2,10},{10,2},{3,11},{11,3},{4,12},{12,4},... | collective-permute-start | bytes 700424 | tf_op jit(solution)/shard_map/ppermute | solution.py:507
  19.0 7.8 %collective-permute-start.12 = (bf16[48,2432]{1,0:T(8,128)(2,1)S(1)}, bf16[48,2432]{1,0:T(8,128)(2,1)S(1)}, u32[]{:S(2)}, u32[]{:S(2)}) collective-permute-start(bf16[48,2432]{1,0:T(8,128)(2,1)S(1)} %collective-permute-done.5.refs_6_), channel_id=1, source_target_pairs={{0,8},{8,0},{1,9},{9,1},{2,10},{10,2},{3,11},{11,3},{4,12},{12,4},... | collective-permute-start | bytes 700424 | tf_op jit(solution)/shard_map/ppermute | solution.py:507
  19.5 7.4 %collective-permute-start.7 = (bf16[48,2432]{1,0:T(8,128)(2,1)S(1)}, bf16[48,2432]{1,0:T(8,128)(2,1)S(1)}, u32[]{:S(2)}, u32[]{:S(2)}) collective-permute-start(bf16[48,2432]{1,0:T(8,128)(2,1)S(1)} %collective-permute-done.6.refs_7_), channel_id=1, source_target_pairs={{0,1},{8,10},{1,3},{9,8},{3,5},{11,9},{5,7},{13,11},{7,6},{15,13},... | collective-permute-start | bytes 700424 | tf_op jit(solution)/shard_map/ppermute | solution.py:489
  21.8 6.2 %collective-permute-start.3 = (bf16[48,2432]{1,0:T(8,128)(2,1)S(1)}, bf16[48,2432]{1,0:T(8,128)(2,1)S(1)}, u32[]{:S(2)}, u32[]{:S(2)}) collective-permute-start(bf16[48,2432]{1,0:T(8,128)(2,1)S(1)} %collective-permute-done.2.refs_3_), channel_id=1, source_target_pairs={{0,1},{8,10},{1,3},{9,8},{3,5},{11,9},{5,7},{13,11},{7,6},{15,13},... | collective-permute-start | bytes 700424 | tf_op jit(solution)/shard_map/ppermute | solution.py:489
  23.8 0.9 %copy-start.1 = (bf16[2,1,82,384]{3,0,2,1:T(2,128)(2,1)S(1)}, bf16[2,1,82,384]{3,0,2,1:T(2,128)(2,1)}, u32[]{:S(2)}) copy-start(bf16[2,1,82,384]{3,0,2,1:T(2,128)(2,1)} %param.12) | copy-start | bytes 377860
  24.7 0.7 copy-start.2
  26.2 1.8 %collective-permute-start.9 = (bf16[48,2432]{1,0:T(8,128)(2,1)S(1)}, bf16[48,2432]{1,0:T(8,128)(2,1)S(1)}, u32[]{:S(2)}, u32[]{:S(2)}) collective-permute-start(bf16[48,2432]{1,0:T(8,128)(2,1)S(1)} %collective-permute-done.1.refs_2_), channel_id=1, source_target_pairs={{0,8},{8,0},{1,9},{9,1},{2,10},{10,2},{3,11},{11,3},{4,12},{12,4},... | collective-permute-start | bytes 700424 | tf_op jit(solution)/shard_map/ppermute | solution.py:507
  26.3 2.1 %collective-permute-start.10 = (bf16[48,2432]{1,0:T(8,128)(2,1)S(1)}, bf16[48,2432]{1,0:T(8,128)(2,1)S(1)}, u32[]{:S(2)}, u32[]{:S(2)}) collective-permute-start(bf16[48,2432]{1,0:T(8,128)(2,1)S(1)} %collective-permute-done.2.refs_3_), channel_id=1, source_target_pairs={{0,8},{8,0},{1,9},{9,1},{2,10},{10,2},{3,11},{11,3},{4,12},{12,4},... | collective-permute-start | bytes 700424 | tf_op jit(solution)/shard_map/ppermute | solution.py:507
  26.8 1.6 %collective-permute-start.13 = (bf16[48,2432]{1,0:T(8,128)(2,1)S(1)}, bf16[48,2432]{1,0:T(8,128)(2,1)S(1)}, u32[]{:S(2)}, u32[]{:S(2)}) collective-permute-start(bf16[48,2432]{1,0:T(8,128)(2,1)S(1)} %collective-permute-done.6.refs_7_), channel_id=1, source_target_pairs={{0,8},{8,0},{1,9},{9,1},{2,10},{10,2},{3,11},{11,3},{4,12},{12,4},... | collective-permute-start | bytes 700424 | tf_op jit(solution)/shard_map/ppermute | solution.py:507
  26.9 1.9 %collective-permute-start.14 = (bf16[48,2432]{1,0:T(8,128)(2,1)S(1)}, bf16[48,2432]{1,0:T(8,128)(2,1)S(1)}, u32[]{:S(2)}, u32[]{:S(2)}) collective-permute-start(bf16[48,2432]{1,0:T(8,128)(2,1)S(1)} %collective-permute-done.7.refs_8_), channel_id=1, source_target_pairs={{0,8},{8,0},{1,9},{9,1},{2,10},{10,2},{3,11},{11,3},{4,12},{12,4},... | collective-permute-start | bytes 700424 | tf_op jit(solution)/shard_map/ppermute | solution.py:507
  28.0 1.5 %collective-permute-start.11 = (bf16[48,2432]{1,0:T(8,128)(2,1)S(1)}, bf16[48,2432]{1,0:T(8,128)(2,1)S(1)}, u32[]{:S(2)}, u32[]{:S(2)}) collective-permute-start(bf16[48,2432]{1,0:T(8,128)(2,1)S(1)} %collective-permute-done.3.refs_4_), channel_id=1, source_target_pairs={{0,8},{8,0},{1,9},{9,1},{2,10},{10,2},{3,11},{11,3},{4,12},{12,4},... | collective-permute-start | bytes 700424 | tf_op jit(solution)/shard_map/ppermute | solution.py:507
  33.6 4.7 %collective-permute-start.15 = (bf16[2,1,82,384]{3,2,1,0:T(8,128)(2,1)S(1)}, bf16[2,1,82,384]{3,2,1,0:T(8,128)(2,1)S(1)}, u32[]{:S(2)}, u32[]{:S(2)}) collective-permute-start(bf16[2,1,82,384]{3,2,1,0:T(8,128)(2,1)S(1)} %get-tuple-element.55), channel_id=1, source_target_pairs={{0,16},{1,17},{2,18},{3,19},{4,20},{5,21},{6,22},{7,23},{8,24},{9,... | collective-permute-start | bytes 377864 | tf_op jit(solution)/shard_map/ppermute | solution.py:603
  41.0 9.9 %collective-permute-start.16 = (bf16[2,1,82,384]{3,2,1,0:T(8,128)(2,1)S(1)}, bf16[2,1,82,384]{3,2,1,0:T(8,128)(2,1)S(1)}, u32[]{:S(2)}, u32[]{:S(2)}) collective-permute-start(bf16[2,1,82,384]{3,2,1,0:T(8,128)(2,1)S(1)} %get-tuple-element.58.own), channel_id=1, source_target_pairs={{16,0},{17,1},{18,2},{19,3},{20,4},{21,5},{22,6},{23,7},{24,8},{25... | collective-permute-start | bytes 377864 | tf_op jit(solution)/shard_map/ppermute | solution.py:612
  55.2 1.9 %collective-permute-start.17 = (bf16[2,48,2432]{2,1,0:T(8,128)(2,1)S(1)}, bf16[2,48,2432]{2,1,0:T(8,128)(2,1)S(1)}, u32[]{:S(2)}, u32[]{:S(2)}) collective-permute-start(bf16[2,48,2432]{2,1,0:T(8,128)(2,1)S(1)} %slice.69), channel_id=1, source_target_pairs={{0,8},{8,0},{1,9},{9,1},{2,10},{10,2},{3,11},{11,3},{4,12},{12,4},... | collective-permute-start | bytes 1400840 | tf_op jit(solution)/shard_map/ppermute | solution.py:516
  57.2 6.3 %collective-permute-start.18 = (bf16[6,48,2432]{2,1,0:T(8,128)(2,1)S(1)}, bf16[6,48,2432]{2,1,0:T(8,128)(2,1)S(1)}, u32[]{:S(2)}, u32[]{:S(2)}) collective-permute-start(bf16[6,48,2432]{2,1,0:T(8,128)(2,1)S(1)} %slice.67), channel_id=1, source_target_pairs={{0,8},{8,0},{1,9},{9,1},{2,10},{10,2},{3,11},{11,3},{4,12},{12,4},... | collective-permute-start | bytes 4202504 | tf_op jit(solution)/shard_map/ppermute | solution.py:527
  57.4 6.1 %collective-permute-start.19 = (bf16[48,2432]{1,0:T(8,128)(2,1)S(1)}, bf16[48,2432]{1,0:T(8,128)(2,1)S(1)}, u32[]{:S(2)}, u32[]{:S(2)}) collective-permute-start(bf16[48,2432]{1,0:T(8,128)(2,1)S(1)} %get-tuple-element.103), channel_id=1, source_target_pairs={{0,1},{8,10},{1,3},{9,8},{3,5},{11,9},{5,7},{13,11},{7,6},{15,13},... | collective-permute-start | bytes 700424 | tf_op jit(solution)/shard_map/ppermute | solution.py:489
  59.3 6.7 %collective-permute-start.21 = (bf16[48,2432]{1,0:T(8,128)(2,1)S(1)}, bf16[48,2432]{1,0:T(8,128)(2,1)S(1)}, u32[]{:S(2)}, u32[]{:S(2)}) collective-permute-start(bf16[48,2432]{1,0:T(8,128)(2,1)S(1)} %get-tuple-element.102), channel_id=1, source_target_pairs={{0,1},{8,10},{1,3},{9,8},{3,5},{11,9},{5,7},{13,11},{7,6},{15,13},... | collective-permute-start | bytes 700424 | tf_op jit(solution)/shard_map/ppermute | solution.py:489
  63.6 6.1 %collective-permute-start.20 = (bf16[48,2432]{1,0:T(8,128)(2,1)S(1)}, bf16[48,2432]{1,0:T(8,128)(2,1)S(1)}, u32[]{:S(2)}, u32[]{:S(2)}) collective-permute-start(bf16[48,2432]{1,0:T(8,128)(2,1)S(1)} %fusion.2), channel_id=1, source_target_pairs={{0,1},{8,10},{1,3},{9,8},{3,5},{11,9},{5,7},{13,11},{7,6},{15,13},... | collective-permute-start | bytes 700424 | tf_op jit(solution)/shard_map/ppermute | solution.py:489
  66.1 6.1 %collective-permute-start.23 = (bf16[48,2432]{1,0:T(8,128)(2,1)S(1)}, bf16[48,2432]{1,0:T(8,128)(2,1)S(1)}, u32[]{:S(2)}, u32[]{:S(2)}) collective-permute-start(bf16[48,2432]{1,0:T(8,128)(2,1)S(1)} %fusion.1), channel_id=1, source_target_pairs={{0,1},{8,10},{1,3},{9,8},{3,5},{11,9},{5,7},{13,11},{7,6},{15,13},... | collective-permute-start | bytes 700424 | tf_op jit(solution)/shard_map/ppermute | solution.py:489
  69.8 6.1 %collective-permute-start.22 = (bf16[48,2432]{1,0:T(8,128)(2,1)S(1)}, bf16[48,2432]{1,0:T(8,128)(2,1)S(1)}, u32[]{:S(2)}, u32[]{:S(2)}) collective-permute-start(bf16[48,2432]{1,0:T(8,128)(2,1)S(1)} %fusion.3), channel_id=1, source_target_pairs={{0,1},{8,10},{1,3},{9,8},{3,5},{11,9},{5,7},{13,11},{7,6},{15,13},... | collective-permute-start | bytes 700424 | tf_op jit(solution)/shard_map/ppermute | solution.py:489
  72.3 6.1 %collective-permute-start.25 = (bf16[48,2432]{1,0:T(8,128)(2,1)S(1)}, bf16[48,2432]{1,0:T(8,128)(2,1)S(1)}, u32[]{:S(2)}, u32[]{:S(2)}) collective-permute-start(bf16[48,2432]{1,0:T(8,128)(2,1)S(1)} %fusion), channel_id=1, source_target_pairs={{0,1},{8,10},{1,3},{9,8},{3,5},{11,9},{5,7},{13,11},{7,6},{15,13},... | collective-permute-start | bytes 700424 | tf_op jit(solution)/shard_map/ppermute | solution.py:489
  76.1 6.1 %collective-permute-start.24 = (bf16[48,2432]{1,0:T(8,128)(2,1)S(1)}, bf16[48,2432]{1,0:T(8,128)(2,1)S(1)}, u32[]{:S(2)}, u32[]{:S(2)}) collective-permute-start(bf16[48,2432]{1,0:T(8,128)(2,1)S(1)} %fusion.4), channel_id=1, source_target_pairs={{0,1},{8,10},{1,3},{9,8},{3,5},{11,9},{5,7},{13,11},{7,6},{15,13},... | collective-permute-start | bytes 700424 | tf_op jit(solution)/shard_map/ppermute | solution.py:489
  78.5 1.5 %collective-permute-start.26 = (bf16[48,2432]{1,0:T(8,128)(2,1)S(1)}, bf16[48,2432]{1,0:T(8,128)(2,1)S(1)}, u32[]{:S(2)}, u32[]{:S(2)}) collective-permute-start(bf16[48,2432]{1,0:T(8,128)(2,1)S(1)} %collective-permute-done.25), channel_id=1, source_target_pairs={{0,8},{8,0},{1,9},{9,1},{2,10},{10,2},{3,11},{11,3},{4,12},{12,4},... | collective-permute-start | bytes 700424 | tf_op jit(solution)/shard_map/ppermute | solution.py:536

commit v6 on v5

--- a/solution.py
+++ b/solution.py
@@ -72,6 +72,8 @@
         self.o_up = self.o_ext + EXT
         self.o_down = self.o_up + self.fh
         self.packed = self.o_down + self.fh
+        self.w_up = 2 * self.o_up
+        self.w_down = self.w_up + hidden
         self.rows = 2 * ROW_STEP
         self.o_vecs = width
         self.o_image = width + 16
@@ -89,15 +91,15 @@
             first=((r, w), BF),
             unit_two=((r, w), F32),
             second=((r, w), BF),
-            slope=((2, r, self.fh), F32),
-            active=((2, r, self.fh), BF),
+            slope=((r, 2 * self.fh), F32),
+            active=((r, 2 * self.fh), BF),
         )
 
     def cotangent_shapes(self):
         r, w = self.rows, self.width
         return dict(
             branch=((r, w), BF),
-            hidden=((2, r, self.fh), BF),
+            hidden=((r, 2 * self.fh), BF),
             attn=((r, w), BF),
             proj=((2, r, 3 * self.half), F32),
             vecs=((16, w), F32),
@@ -128,7 +130,7 @@
         st["first"][...] = first
     proj, mixed = st["proj"], st["mixed"]
     for t in range(2):
-        value = nn(first, w[t, 0 : dm.width, 0 : 3 * half])
+        value = nn(first, w[0 : dm.width, t * dm.o_up : t * dm.o_up + 3 * half])
         proj[t, :, 0:half] = value[:, 0:half] + vecs[6:7, t * half : (t + 1) * half]
         proj[t, :, half : 2 * half] = value[:, half : 2 * half]
         proj[t, :, 2 * half :] = value[:, 2 * half :] + vecs[7:8, t * half : (t + 1) * half]
@@ -145,7 +147,7 @@
         mixed[t, rows, c : c + HD] = nn(st["probs"][i].astype(BF), values.astype(BF))
     resid = state + vecs[3:4, :]
     for t in range(2):
-        resid += nt(mixed[t].astype(BF), w[t, 0 : dm.width, dm.o_out : dm.o_out + half])
+        resid += nt(mixed[t].astype(BF), w[0 : dm.width, t * dm.o_up + dm.o_out : t * dm.o_up + dm.o_ext])
     return resid
 
 
@@ -158,17 +160,14 @@
         st["factors"][1] = factor
         st["second"][...] = second
     output = resid + vecs[5:6, :]
-    per = fh // dm.width
-    for t in range(2):
-        bias = jnp.concatenate([vecs[8 + t * per + j : 9 + t * per + j, :] for j in range(per)], axis=1)
-        hidden = nn(second, w[t, 0 : dm.width, dm.o_up : dm.o_up + fh]) + bias
-        curve = 0.5 * (1.0 + lax.erf(hidden * INV_ROOT_TWO))
-        active = (hidden * curve).astype(BF)
-        if keep:
-            st["slope"][t] = curve + hidden * jnp.exp(-0.5 * hidden * hidden) * INV_ROOT_TWO_PI
-            st["active"][t] = active
-        output += nt(active, w[t, 0 : dm.width, dm.o_down : dm.o_down + fh])
-    return output
+    bias = jnp.concatenate([vecs[8 + j : 9 + j, :] for j in range(2 * fh // dm.width)], axis=1)
+    hidden = nn(second, w[0 : dm.width, dm.w_up : dm.w_down]) + bias
+    curve = 0.5 * (1.0 + lax.erf(hidden * INV_ROOT_TWO))
+    active = (hidden * curve).astype(BF)
+    if keep:
+        st["slope"][...] = curve + hidden * jnp.exp(-0.5 * hidden * hidden) * INV_ROOT_TWO_PI
+        st["active"][...] = active
+    return output + nt(active, w[0 : dm.width, dm.w_down :])
 
 
 def total_rows(value):
@@ -180,17 +179,13 @@
     low = grad.astype(BF)
     ct["branch"][...] = low
     shift_branch = total_rows(low.astype(F32))
-    per = fh // dm.width
-    grad_second = None
-    for t in range(2):
-        raw = nn(low, w[t, 0 : dm.width, dm.o_down : dm.o_down + fh]) * st["slope"][t]
-        up_bias = total_rows(raw)
-        for j in range(per):
-            ct["vecs"][8 + t * per + j : 9 + t * per + j, :] = up_bias[:, j * dm.width : (j + 1) * dm.width]
-        grad_hidden = raw.astype(BF)
-        ct["hidden"][t] = grad_hidden
-        part = nt(grad_hidden, w[t, 0 : dm.width, dm.o_up : dm.o_up + fh])
-        grad_second = part if grad_second is None else grad_second + part
+    raw = nn(low, w[0 : dm.width, dm.w_down :]) * st["slope"][...]
+    up_bias = total_rows(raw)
+    for j in range(2 * fh // dm.width):
+        ct["vecs"][8 + j : 9 + j, :] = up_bias[:, j * dm.width : (j + 1) * dm.width]
+    grad_hidden = raw.astype(BF)
+    ct["hidden"][...] = grad_hidden
+    grad_second = nt(grad_hidden, w[0 : dm.width, dm.w_up : dm.w_down])
     unit = st["unit_two"][...]
     gain_two, shift_two = total_rows(grad_second * unit), total_rows(grad_second)
     grad_resid = grad + norm_back(grad_second, unit, st["factors"][1], vecs[1:2, :])
@@ -199,7 +194,7 @@
     shift_attn = total_rows(low.astype(F32))
     proj, gproj, gmix, scores = st["proj"], ct["proj"], work["mixed"], work["scores"]
     for t in range(2):
-        gmix[t] = nn(low, w[t, 0 : dm.width, dm.o_out : dm.o_out + half])
+        gmix[t] = nn(low, w[0 : dm.width, t * dm.o_up + dm.o_out : t * dm.o_up + dm.o_ext])
     for i, t, rows, c in dm.cells():
         values = proj[t, rows, 2 * half + c : 2 * half + c + HD].astype(BF)
         gm = gmix[t, rows, c : c + HD].astype(BF)
@@ -217,7 +212,7 @@
     for t in range(2):
         ct["vecs"][6:7, t * half : (t + 1) * half] = total_rows(gproj[t, :, 0:half])
         ct["vecs"][7:8, t * half : (t + 1) * half] = total_rows(gproj[t, :, 2 * half :])
-        part = nt(gproj[t].astype(BF), w[t, 0 : dm.width, 0 : 3 * half])
+        part = nt(gproj[t].astype(BF), w[0 : dm.width, t * dm.o_up : t * dm.o_up + 3 * half])
         grad_first = part if grad_first is None else grad_first + part
     unit = st["unit_one"][...]
     gain_one, shift_one = total_rows(grad_first * unit), total_rows(grad_first)
@@ -235,9 +230,11 @@
             rows = value[f * block : (f + 1) * block].astype(BF)
             grads[slots[t][f], :, column : column + value.shape[1]] = rows
 
+    down = tn(ct["branch"][...], st["active"][...])
+    up = tn(st["second"][...], ct["hidden"][...])
     for t in range(2):
-        keep(t, dm.o_down, tn(ct["branch"][...], st["active"][t]))
-        keep(t, dm.o_up, tn(st["second"][...], ct["hidden"][t]))
+        keep(t, dm.o_down, down[:, t * fh : (t + 1) * fh])
+        keep(t, dm.o_up, up[:, t * fh : (t + 1) * fh])
         keep(t, dm.o_out, tn(ct["attn"][...], st["mixed"][t].astype(BF)))
         keep(t, 0, tn(st["first"][...], ct["proj"][t].astype(BF)))
     own_first = lax.axis_index("tensor") == 0
@@ -313,20 +310,23 @@
             where = pl.ds(owners[key], block)
         else:
             where = pl.ds(offset * block, block)
-        for j, (lo, hi) in enumerate(((0, dm.o_up), (dm.o_up, dm.packed))):
-            source = pieces[array].at[pl.ds(row, block), pl.ds(lo, hi - lo)]
-            copy = pltpu.make_async_copy(source, w.at[t, where, pl.ds(lo, hi - lo)], sems.at[j, n])
-            (early, late)[j].append(copy)
+        cuts = ((0, dm.o_up, t * dm.o_up), (dm.o_up, dm.fh, dm.w_up + t * dm.fh), (dm.o_down, dm.fh, dm.w_down + t * dm.fh))
+        for j, (start, columns, target) in enumerate(cuts):
+            source = pieces[array].at[pl.ds(row, block), pl.ds(start, columns)]
+            copy = pltpu.make_async_copy(source, w.at[where, pl.ds(target, columns)], sems.at[j, n])
+            (late if j else early).append(copy)
     for copy in early + late:
         copy.start()
     for m in range(2):
-        w[m, dm.o_image : dm.o_grad, 0 : dm.width] = images[m]
-        w[m, dm.o_grad : dm.w_rows, 0 : dm.width] = cotangents[m]
+        columns = slice(m * dm.o_up, m * dm.o_up + dm.width)
+        w[dm.o_image : dm.o_grad, columns] = images[m]
+        w[dm.o_grad : dm.w_rows, columns] = cotangents[m]
         rows[m * ROW_STEP : (m + 1) * ROW_STEP, :] = images[m].astype(F32)[0:ROW_STEP]
     for copy in early:
         copy.wait()
     extra = [
-        [w[t, f * block : f * block + 16, dm.o_ext : dm.o_up].astype(F32) for f in range(dm.shards)] for t in range(2)
+        [w[f * block : f * block + 16, t * dm.o_up + dm.o_ext : (t + 1) * dm.o_up].astype(F32) for f in range(dm.shards)]
+        for t in range(2)
     ]
     share, up_share = dm.half // dm.shards, dm.fh // dm.shards
     small = [
@@ -343,7 +343,7 @@
     vecs.append(cotangents[2, 0:16, :].astype(F32)[0:2])
     vecs.append(jnp.zeros((6 - 2 * per, dm.width), F32))
     vecs = jnp.concatenate(vecs, axis=0)
-    w[0, dm.o_vecs : dm.o_image, 0 : dm.width] = vecs.astype(BF)
+    w[dm.o_vecs : dm.o_image, 0 : dm.width] = vecs.astype(BF)
     used = lax.axis_index("section") == 0
 
     @pl.when(used)
@@ -361,7 +361,7 @@
 
 
 def vectors_of(dm, w):
-    return w[0, dm.o_vecs : dm.o_image, 0 : dm.width].astype(F32)
+    return w[dm.o_vecs : dm.o_image, 0 : dm.width].astype(F32)
 
 
 def live_of(count_ref, m):
@@ -390,7 +390,7 @@
 
     def take(start):
         for m in range(2):
-            value = w[m, start : start + 96, 0 : dm.width].astype(F32)
+            value = w[start : start + 96, m * dm.o_up : m * dm.o_up + dm.width].astype(F32)
             rows[m * ROW_STEP : (m + 1) * ROW_STEP, :] = value[0:ROW_STEP]
 
     @pl.when(jnp.logical_not(last))
@@ -595,10 +595,10 @@
     w, low0 = call(
         functools.partial(kernel_first, dm, layout, ring),
         [VM, VM] + [AN] * len(found),
-        [((2, dm.w_rows, dm.packed), BF), (shape, BF)],
+        [((dm.w_rows, 2 * dm.packed), BF), (shape, BF)],
         (*images, *found),
         scratch=buffers([states["proj"], states["probs"], states["mixed"], ((dm.rows, width), F32)])
-        + [pltpu.SemaphoreType.DMA((2, len(layout)))],
+        + [pltpu.SemaphoreType.DMA((3, len(layout)))],
     )
     h1 = lax.ppermute(low0, "section", [(0, 1)])
     kept = list(states.values()) + list(cotangents.values())

time: 83.3 us -> 83.3 us (level)
  no operation moved by 1% of the time
where the time goes in v6:
time: 83.3 us; the launch traced here: 82.9 us
  waiting for transfers between devices  31.4 us (38%)
  starting transfers between devices  31.3 us (38%)
  Pallas kernels  12.9 us (15%)
  local copies, waits for them, and re-layouts  4.9 us (6%)
  other arithmetic  1.68 us (2%)
    ppermute x14, starting transfers between devices, onward(): return lax.ppermute(value, ('tensor', 'fsdp'), route)  26.3 us
    ppermute x14, waiting for transfers between devices, onward(): return lax.ppermute(value, ('tensor', 'fsdp'), route)  16.2 us
    pallas_call x6, Pallas kernels, call(): pl.pallas_call(kernel, in_specs=ins, out_specs=[VM] * len(outs), out_shap...  12.9 us
    ppermute x1, waiting for transfers between devices, per_device(): incoming = lax.ppermute(grad1, 'section', [(1, 0)])  8.6 us
    unnamed x8, local copies, waits for them, and re-layouts  3.95 us
    ppermute x1, waiting for transfers between devices, per_device(): h1 = lax.ppermute(low0, 'section', [(0, 1)])  3.41 us
    ppermute x1, waiting for transfers between devices, reduce_ring(): first = lax.ppermute(blocks[count:count + early], 'tensor', swap)  1.71 us
  transfers between devices with their start and end apart: 27, of which 18 were waited for; matrix products, arithmetic and copies ran while one was open for 3% of the time, Pallas kernels for 1%

profile of v6, /device:TPU:0, one launch (start us, length us, event | category | flops | bytes accessed | tf_op | source)
XLA Modules:
  0.0 82.9 jit_solution(672421142371288864)
XLA Ops:
  0.6 0.8 slice_bitcast_fusion.4
  1.4 1.1 %pad_add_fusion.refs_0_ = bf16[48,2432]{1,0:T(8,128)(2,1)S(1)} fusion(bf16[1,96]{1,0:T(2,128)(2,1)} %param.19, bf16[2,24]{1,0:T(2,128)(2,1)} %bitcast.72, bf16[4,24]{1,0:T(4,128)(2,1)} %bitcast.71, bf16[2,24]{1,0:T(2,128)(2,1)} %bitcast.73, bf16[48,768]{1,0:T(8,128)(2,1)} %bitcast.68, bf16[48,768]{1,0:T(8,128)(2,1)} %bitcast.69, ...), kind=kLoop, calls=%fused_computation.16 | loop fusion | flops 2334720 | bytes 455232 | tf_op jit(solution)/shard_map/add | solution.py:566
  2.5 0.5 collective-permute-start.4
  3.0 2.6 %collective-permute-start = (bf16[48,2432]{1,0:T(8,128)(2,1)S(1)}, bf16[48,2432]{1,0:T(8,128)(2,1)S(1)}, u32[]{:S(2)}, u32[]{:S(2)}) collective-permute-start(bf16[48,2432]{1,0:T(8,128)(2,1)S(1)} %pad_add_fusion.refs_0_), channel_id=1, source_target_pairs={{0,1},{8,10},{1,3},{9,8},{3,5},{11,9},{5,7},{13,11},{7,6},{15,13},... | collective-permute-start | bytes 700424 | tf_op jit(solution)/shard_map/ppermute | solution.py:489
  5.6 1.6 %collective-permute-start.5 = (bf16[48,2432]{1,0:T(8,128)(2,1)S(1)}, bf16[48,2432]{1,0:T(8,128)(2,1)S(1)}, u32[]{:S(2)}, u32[]{:S(2)}) collective-permute-start(bf16[48,2432]{1,0:T(8,128)(2,1)S(1)} %collective-permute-done.4.refs_5_), channel_id=1, source_target_pairs={{0,1},{8,10},{1,3},{9,8},{3,5},{11,9},{5,7},{13,11},{7,6},{15,13},... | collective-permute-start | bytes 700424 | tf_op jit(solution)/shard_map/ppermute | solution.py:489
  7.2 2.5 %collective-permute-done.refs_1_ = bf16[48,2432]{1,0:T(8,128)(2,1)S(1)} collective-permute-done((bf16[48,2432]{1,0:T(8,128)(2,1)S(1)}, bf16[48,2432]{1,0:T(8,128)(2,1)S(1)}, u32[]{:S(2)}, u32[]{:S(2)}) %collective-permute-start) | collective-permute-done | bytes 233504 | tf_op jit(solution)/shard_map/ppermute | solution.py:489
  9.7 2.0 %collective-permute-start.1 = (bf16[48,2432]{1,0:T(8,128)(2,1)S(1)}, bf16[48,2432]{1,0:T(8,128)(2,1)S(1)}, u32[]{:S(2)}, u32[]{:S(2)}) collective-permute-start(bf16[48,2432]{1,0:T(8,128)(2,1)S(1)} %collective-permute-done.refs_1_), channel_id=1, source_target_pairs={{0,1},{8,10},{1,3},{9,8},{3,5},{11,9},{5,7},{13,11},{7,6},{15,13},... | collective-permute-start | bytes 700424 | tf_op jit(solution)/shard_map/ppermute | solution.py:489
  11.7 0.5 collective-permute-done.5.refs_6_
  12.2 2.0 %collective-permute-start.6 = (bf16[48,2432]{1,0:T(8,128)(2,1)S(1)}, bf16[48,2432]{1,0:T(8,128)(2,1)S(1)}, u32[]{:S(2)}, u32[]{:S(2)}) collective-permute-start(bf16[48,2432]{1,0:T(8,128)(2,1)S(1)} %collective-permute-done.5.refs_6_), channel_id=1, source_target_pairs={{0,1},{8,10},{1,3},{9,8},{3,5},{11,9},{5,7},{13,11},{7,6},{15,13},... | collective-permute-start | bytes 700424 | tf_op jit(solution)/shard_map/ppermute | solution.py:489
  14.2 1.6 %collective-permute-done.1.refs_2_ = bf16[48,2432]{1,0:T(8,128)(2,1)S(1)} collective-permute-done((bf16[48,2432]{1,0:T(8,128)(2,1)S(1)}, bf16[48,2432]{1,0:T(8,128)(2,1)S(1)}, u32[]{:S(2)}, u32[]{:S(2)}) %collective-permute-start.1) | collective-permute-done | bytes 233504 | tf_op jit(solution)/shard_map/ppermute | solution.py:489
  15.8 2.0 %collective-permute-start.2 = (bf16[48,2432]{1,0:T(8,128)(2,1)S(1)}, bf16[48,2432]{1,0:T(8,128)(2,1)S(1)}, u32[]{:S(2)}, u32[]{:S(2)}) collective-permute-start(bf16[48,2432]{1,0:T(8,128)(2,1)S(1)} %collective-permute-done.1.refs_2_), channel_id=1, source_target_pairs={{0,1},{8,10},{1,3},{9,8},{3,5},{11,9},{5,7},{13,11},{7,6},{15,13},... | collective-permute-start | bytes 700424 | tf_op jit(solution)/shard_map/ppermute | solution.py:489
  17.7 0.9 %copy-done = bf16[2,1,82,384]{3,0,2,1:T(2,128)(2,1)S(1)} copy-done((bf16[2,1,82,384]{3,0,2,1:T(2,128)(2,1)S(1)}, bf16[2,1,82,384]{3,0,2,1:T(2,128)(2,1)}, u32[]{:S(2)}) %copy-start) | copy-done | bytes 125976
  19.0 0.5 collective-permute-start.12
  19.5 1.6 %collective-permute-start.7 = (bf16[48,2432]{1,0:T(8,128)(2,1)S(1)}, bf16[48,2432]{1,0:T(8,128)(2,1)S(1)}, u32[]{:S(2)}, u32[]{:S(2)}) collective-permute-start(bf16[48,2432]{1,0:T(8,128)(2,1)S(1)} %collective-permute-done.6.refs_7_), channel_id=1, source_target_pairs={{0,1},{8,10},{1,3},{9,8},{3,5},{11,9},{5,7},{13,11},{7,6},{15,13},... | collective-permute-start | bytes 700424 | tf_op jit(solution)/shard_map/ppermute | solution.py:489
  21.1 0.8 collective-permute-done.2.refs_3_
  21.8 2.0 %collective-permute-start.3 = (bf16[48,2432]{1,0:T(8,128)(2,1)S(1)}, bf16[48,2432]{1,0:T(8,128)(2,1)S(1)}, u32[]{:S(2)}, u32[]{:S(2)}) collective-permute-start(bf16[48,2432]{1,0:T(8,128)(2,1)S(1)} %collective-permute-done.2.refs_3_), channel_id=1, source_target_pairs={{0,1},{8,10},{1,3},{9,8},{3,5},{11,9},{5,7},{13,11},{7,6},{15,13},... | collective-permute-start | bytes 700424 | tf_op jit(solution)/shard_map/ppermute | solution.py:489
  23.8 0.9 %copy-done.1 = bf16[2,1,82,384]{3,0,2,1:T(2,128)(2,1)S(1)} copy-done((bf16[2,1,82,384]{3,0,2,1:T(2,128)(2,1)S(1)}, bf16[2,1,82,384]{3,0,2,1:T(2,128)(2,1)}, u32[]{:S(2)}) %copy-start.1) | copy-done | bytes 125976
  24.7 0.7 copy-done.2
  25.4 0.8 %shard_map.187.cotangents = bf16[3,96,384]{2,1,0:T(8,128)(2,1)S(1)} custom-call(s32[1,2]{1,0:T(1,128)S(1)} %bitcast.67, bf16[82,2,384]{2,1,0:T(2,128)(2,1)S(1)} %bitcast.66), custom_call_target="tpu_custom_call" | custom-call | tf_op jit(solution)/shard_map/pallas_call | solution.py:473
  26.3 0.5 collective-permute-start.10
  26.9 0.4 collective-permute-start.14
  27.3 0.7 collective-permute-done.3.refs_4_
  28.8 0.8 collective-permute-done.11.refs_12_
  29.5 4.1 %shard_map.188 = (bf16[592,4864]{1,0:T(8,128)(2,1)S(1)}, bf16[2,1,82,384]{3,2,1,0:T(8,128)(2,1)S(1)}) custom-call(bf16[2,96,384]{2,1,0:T(8,128)(2,1)S(1)} %shard_map.186.images, bf16[3,96,384]{2,1,0:T(8,128)(2,1)S(1)} %shard_map.187.cotangents, bf16[48,2432]{1,0:T(8,128)(2,1)S(1)} %pad_add_fusion.refs_0_, bf16[48,2432]{1,0:T(8,128)(2,1)S(1)} %collective-permute-done.refs_1_, ...), custom_call_target="tpu_custom_call" | custom-call | tf_op jit(solution)/shard_map/pallas_call | solution.py:473
  33.7 1.3 %collective-permute-start.15 = (bf16[2,1,82,384]{3,2,1,0:T(8,128)(2,1)S(1)}, bf16[2,1,82,384]{3,2,1,0:T(8,128)(2,1)S(1)}, u32[]{:S(2)}, u32[]{:S(2)}) collective-permute-start(bf16[2,1,82,384]{3,2,1,0:T(8,128)(2,1)S(1)} %get-tuple-element.55), channel_id=1, source_target_pairs={{0,16},{1,17},{2,18},{3,19},{4,20},{5,21},{6,22},{7,23},{8,24},{9,... | collective-permute-start | bytes 377864 | tf_op jit(solution)/shard_map/ppermute | solution.py:603
  35.0 3.4 %collective-permute-done.15.h1 = bf16[2,1,82,384]{3,2,1,0:T(8,128)(2,1)S(1)} collective-permute-done((bf16[2,1,82,384]{3,2,1,0:T(8,128)(2,1)S(1)}, bf16[2,1,82,384]{3,2,1,0:T(8,128)(2,1)S(1)}, u32[]{:S(2)}, u32[]{:S(2)}) %collective-permute-start.15) | collective-permute-done | bytes 125984 | tf_op jit(solution)/shard_map/ppermute | solution.py:603
  38.4 2.6 %shard_map.189 = (bf16[2,1,82,384]{3,2,1,0:T(8,128)(2,1)S(1)}, bf16[2,1,82,384]{3,2,1,0:T(8,128)(2,1)S(1)}, f32[2,176,576]{2,1,0:T(8,128)S(1)}, f32[12,88,88]{2,...) custom-call(bf16[2,1,82,384]{3,2,1,0:T(8,128)(2,1)S(1)} %collective-, ...), custom_call_target="tpu_custom_call" | custom-call | tf_op jit(solution)/shard_map/pallas_call | solution.py:473
  41.0 1.3 %collective-permute-start.16 = (bf16[2,1,82,384]{3,2,1,0:T(8,128)(2,1)S(1)}, bf16[2,1,82,384]{3,2,1,0:T(8,128)(2,1)S(1)}, u32[]{:S(2)}, u32[]{:S(2)}) collective-permute-start(bf16[2,1,82,384]{3,2,1,0:T(8,128)(2,1)S(1)} %get-tuple-element.58.own), channel_id=1, source_target_pairs={{16,0},{17,1},{18,2},{19,3},{20,4},{21,5},{22,6},{23,7},{24,8},{25... | collective-permute-start | bytes 377864 | tf_op jit(solution)/shard_map/ppermute | solution.py:612
  42.3 8.6 %collective-permute-done.16.incoming = bf16[2,1,82,384]{3,2,1,0:T(8,128)(2,1)S(1)} collective-permute-done((bf16[2,1,82,384]{3,2,1,0:T(8,128)(2,1)S(1)}, bf16[2,1,82,384]{3,2,1,0:T(8,128)(2,1)S(1)}, u32[]{:S(2)}, u32[]{:S(2)}) %collective-permute-start.16) | collective-permute-done | bytes 125984 | tf_op jit(solution)/shard_map/ppermute | solution.py:612
  50.9 4.2 %shard_map.190 = (bf16[2,1,82,384]{3,2,1,0:T(8,128)(2,1)S(1)}, bf16[16,48,2432]{2,1,0:T(8,128)(2,1)S(1)}) custom-call(bf16[2,1,82,384]{3,2,1,0:T(8,128)(2,1)S(1)} %collective-permute-done.16.incoming, bf16[592,4864]{1,0:T(8,128)(2,1)S(1)} %get-tuple-element.56.w, bf16[2,1,82,384]{3,2,1,0:T(8,128)(2,1)S(1)} %get-tuple-element.58.own, ...), custom_call_target="tpu_custom_call" | custom-call | tf_op jit(solution)/shard_map/pallas_call | solution.py:473
  55.3 1.7 %collective-permute-done.17 = bf16[2,48,2432]{2,1,0:T(8,128)(2,1)S(1)} collective-permute-done((bf16[2,48,2432]{2,1,0:T(8,128)(2,1)S(1)}, bf16[2,48,2432]{2,1,0:T(8,128)(2,1)S(1)}, u32[]{:S(2)}, u32[]{:S(2)}) %collective-permute-start.17) | collective-permute-done | bytes 466976 | tf_op jit(solution)/shard_map/ppermute | solution.py:516
  57.4 1.8 %collective-permute-start.19 = (bf16[48,2432]{1,0:T(8,128)(2,1)S(1)}, bf16[48,2432]{1,0:T(8,128)(2,1)S(1)}, u32[]{:S(2)}, u32[]{:S(2)}) collective-permute-start(bf16[48,2432]{1,0:T(8,128)(2,1)S(1)} %get-tuple-element.103), channel_id=1, source_target_pairs={{0,1},{8,10},{1,3},{9,8},{3,5},{11,9},{5,7},{13,11},{7,6},{15,13},... | collective-permute-start | bytes 700424 | tf_op jit(solution)/shard_map/ppermute | solution.py:489
  59.2 1.6 %collective-permute-start.21 = (bf16[48,2432]{1,0:T(8,128)(2,1)S(1)}, bf16[48,2432]{1,0:T(8,128)(2,1)S(1)}, u32[]{:S(2)}, u32[]{:S(2)}) collective-permute-start(bf16[48,2432]{1,0:T(8,128)(2,1)S(1)} %get-tuple-element.102), channel_id=1, source_target_pairs={{0,1},{8,10},{1,3},{9,8},{3,5},{11,9},{5,7},{13,11},{7,6},{15,13},... | collective-permute-start | bytes 700424 | tf_op jit(solution)/shard_map/ppermute | solution.py:489
  60.8 2.6 %collective-permute-done.19 = bf16[48,2432]{1,0:T(8,128)(2,1)S(1)} collective-permute-done((bf16[48,2432]{1,0:T(8,128)(2,1)S(1)}, bf16[48,2432]{1,0:T(8,128)(2,1)S(1)}, u32[]{:S(2)}, u32[]{:S(2)}) %collective-permute-start.19) | collective-permute-done | bytes 233504 | tf_op jit(solution)/shard_map/ppermute | solution.py:489
  63.5 1.8 %collective-permute-start.20 = (bf16[48,2432]{1,0:T(8,128)(2,1)S(1)}, bf16[48,2432]{1,0:T(8,128)(2,1)S(1)}, u32[]{:S(2)}, u32[]{:S(2)}) collective-permute-start(bf16[48,2432]{1,0:T(8,128)(2,1)S(1)} %fusion.2), channel_id=1, source_target_pairs={{0,1},{8,10},{1,3},{9,8},{3,5},{11,9},{5,7},{13,11},{7,6},{15,13},... | collective-permute-start | bytes 700424 | tf_op jit(solution)/shard_map/ppermute | solution.py:489
  65.4 0.5 collective-permute-done.21
  66.0 1.8 %collective-permute-start.23 = (bf16[48,2432]{1,0:T(8,128)(2,1)S(1)}, bf16[48,2432]{1,0:T(8,128)(2,1)S(1)}, u32[]{:S(2)}, u32[]{:S(2)}) collective-permute-start(bf16[48,2432]{1,0:T(8,128)(2,1)S(1)} %fusion.1), channel_id=1, source_target_pairs={{0,1},{8,10},{1,3},{9,8},{3,5},{11,9},{5,7},{13,11},{7,6},{15,13},... | collective-permute-start | bytes 700424 | tf_op jit(solution)/shard_map/ppermute | solution.py:489
  67.9 1.8 %collective-permute-done.20 = bf16[48,2432]{1,0:T(8,128)(2,1)S(1)} collective-permute-done((bf16[48,2432]{1,0:T(8,128)(2,1)S(1)}, bf16[48,2432]{1,0:T(8,128)(2,1)S(1)}, u32[]{:S(2)}, u32[]{:S(2)}) %collective-permute-start.20) | collective-permute-done | bytes 233504 | tf_op jit(solution)/shard_map/ppermute | solution.py:489
  69.7 1.8 %collective-permute-start.22 = (bf16[48,2432]{1,0:T(8,128)(2,1)S(1)}, bf16[48,2432]{1,0:T(8,128)(2,1)S(1)}, u32[]{:S(2)}, u32[]{:S(2)}) collective-permute-start(bf16[48,2432]{1,0:T(8,128)(2,1)S(1)} %fusion.3), channel_id=1, source_target_pairs={{0,1},{8,10},{1,3},{9,8},{3,5},{11,9},{5,7},{13,11},{7,6},{15,13},... | collective-permute-start | bytes 700424 | tf_op jit(solution)/shard_map/ppermute | solution.py:489
  71.6 0.6 collective-permute-done.23
  72.3 1.8 %collective-permute-start.25 = (bf16[48,2432]{1,0:T(8,128)(2,1)S(1)}, bf16[48,2432]{1,0:T(8,128)(2,1)S(1)}, u32[]{:S(2)}, u32[]{:S(2)}) collective-permute-start(bf16[48,2432]{1,0:T(8,128)(2,1)S(1)} %fusion), channel_id=1, source_target_pairs={{0,1},{8,10},{1,3},{9,8},{3,5},{11,9},{5,7},{13,11},{7,6},{15,13},... | collective-permute-start | bytes 700424 | tf_op jit(solution)/shard_map/ppermute | solution.py:489
  74.1 1.8 %collective-permute-done.22 = bf16[48,2432]{1,0:T(8,128)(2,1)S(1)} collective-permute-done((bf16[48,2432]{1,0:T(8,128)(2,1)S(1)}, bf16[48,2432]{1,0:T(8,128)(2,1)S(1)}, u32[]{:S(2)}, u32[]{:S(2)}) %collective-permute-start.22) | collective-permute-done | bytes 233504 | tf_op jit(solution)/shard_map/ppermute | solution.py:489
  76.0 1.8 %collective-permute-start.24 = (bf16[48,2432]{1,0:T(8,128)(2,1)S(1)}, bf16[48,2432]{1,0:T(8,128)(2,1)S(1)}, u32[]{:S(2)}, u32[]{:S(2)}) collective-permute-start(bf16[48,2432]{1,0:T(8,128)(2,1)S(1)} %fusion.4), channel_id=1, source_target_pairs={{0,1},{8,10},{1,3},{9,8},{3,5},{11,9},{5,7},{13,11},{7,6},{15,13},... | collective-permute-start | bytes 700424 | tf_op jit(solution)/shard_map/ppermute | solution.py:489
  77.8 0.6 collective-permute-done.25
  78.4 0.7 copy.21
  79.1 0.7 copy.22
  79.9 2.2 %collective-permute-done.24.refs_2_ = bf16[48,2432]{1,0:T(8,128)(2,1)S(1)} collective-permute-done((bf16[48,2432]{1,0:T(8,128)(2,1)S(1)}, bf16[48,2432]{1,0:T(8,128)(2,1)S(1)}, u32[]{:S(2)}, u32[]{:S(2)}) %collective-permute-start.24) | collective-permute-done | bytes 233504 | tf_op jit(solution)/shard_map/ppermute | solution.py:489
  82.1 0.9 %shard_map.191 = (f32[3,48,192]{2,1,0:T(8,128)}, f32[48,192]{1,0:T(8,128)}, f32[48,768]{1,0:T(8,128)}, f32[48,768]{1,0:T(8,128)}, f32[1,2,24]{2,1,0:T(2,128)}, /...) custom-call(bf16[48,2432]{1,0:T(8,128)(2,1)S(1)} %slice_bitcast_fusion.1.refs_0_, ...), custom_call_target="tpu_custom_call" | custom-call | tf_op jit(solution)/shard_map/pallas_call | solution.py:473
  (32 shorter events, 2.3 us)
Async XLA Ops:
  2.5 3.1 %collective-permute-start.4 = (bf16[48,2432]{1,0:T(8,128)(2,1)S(1)}, bf16[48,2432]{1,0:T(8,128)(2,1)S(1)}, u32[]{:S(2)}, u32[]{:S(2)}) collective-permute-start(bf16[48,2432]{1,0:T(8,128)(2,1)S(1)} %pad_add_fusion.refs_0_), channel_id=1, source_target_pairs={{0,8},{8,0},{1,9},{9,1},{2,10},{10,2},{3,11},{11,3},{4,12},{12,4},... | collective-permute-start | bytes 700424 | tf_op jit(solution)/shard_map/ppermute | solution.py:494
  3.0 6.7 %collective-permute-start = (bf16[48,2432]{1,0:T(8,128)(2,1)S(1)}, bf16[48,2432]{1,0:T(8,128)(2,1)S(1)}, u32[]{:S(2)}, u32[]{:S(2)}) collective-permute-start(bf16[48,2432]{1,0:T(8,128)(2,1)S(1)} %pad_add_fusion.refs_0_), channel_id=1, source_target_pairs={{0,1},{8,10},{1,3},{9,8},{3,5},{11,9},{5,7},{13,11},{7,6},{15,13},... | collective-permute-start | bytes 700424 | tf_op jit(solution)/shard_map/ppermute | solution.py:489
  5.6 6.6 %collective-permute-start.5 = (bf16[48,2432]{1,0:T(8,128)(2,1)S(1)}, bf16[48,2432]{1,0:T(8,128)(2,1)S(1)}, u32[]{:S(2)}, u32[]{:S(2)}) collective-permute-start(bf16[48,2432]{1,0:T(8,128)(2,1)S(1)} %collective-permute-done.4.refs_5_), channel_id=1, source_target_pairs={{0,1},{8,10},{1,3},{9,8},{3,5},{11,9},{5,7},{13,11},{7,6},{15,13},... | collective-permute-start | bytes 700424 | tf_op jit(solution)/shard_map/ppermute | solution.py:489
  9.7 6.1 %collective-permute-start.1 = (bf16[48,2432]{1,0:T(8,128)(2,1)S(1)}, bf16[48,2432]{1,0:T(8,128)(2,1)S(1)}, u32[]{:S(2)}, u32[]{:S(2)}) collective-permute-start(bf16[48,2432]{1,0:T(8,128)(2,1)S(1)} %collective-permute-done.refs_1_), channel_id=1, source_target_pairs={{0,1},{8,10},{1,3},{9,8},{3,5},{11,9},{5,7},{13,11},{7,6},{15,13},... | collective-permute-start | bytes 700424 | tf_op jit(solution)/shard_map/ppermute | solution.py:489
  12.2 7.3 %collective-permute-start.6 = (bf16[48,2432]{1,0:T(8,128)(2,1)S(1)}, bf16[48,2432]{1,0:T(8,128)(2,1)S(1)}, u32[]{:S(2)}, u32[]{:S(2)}) collective-permute-start(bf16[48,2432]{1,0:T(8,128)(2,1)S(1)} %collective-permute-done.5.refs_6_), channel_id=1, source_target_pairs={{0,1},{8,10},{1,3},{9,8},{3,5},{11,9},{5,7},{13,11},{7,6},{15,13},... | collective-permute-start | bytes 700424 | tf_op jit(solution)/shard_map/ppermute | solution.py:489
  15.8 6.1 %collective-permute-start.2 = (bf16[48,2432]{1,0:T(8,128)(2,1)S(1)}, bf16[48,2432]{1,0:T(8,128)(2,1)S(1)}, u32[]{:S(2)}, u32[]{:S(2)}) collective-permute-start(bf16[48,2432]{1,0:T(8,128)(2,1)S(1)} %collective-permute-done.1.refs_2_), channel_id=1, source_target_pairs={{0,1},{8,10},{1,3},{9,8},{3,5},{11,9},{5,7},{13,11},{7,6},{15,13},... | collective-permute-start | bytes 700424 | tf_op jit(solution)/shard_map/ppermute | solution.py:489
  17.7 0.9 %copy-start = (bf16[2,1,82,384]{3,0,2,1:T(2,128)(2,1)S(1)}, bf16[2,1,82,384]{3,0,2,1:T(2,128)(2,1)}, u32[]{:S(2)}) copy-start(bf16[2,1,82,384]{3,0,2,1:T(2,128)(2,1)} %param.11) | copy-start | bytes 377860
  18.9 7.4 %collective-permute-start.8 = (bf16[48,2432]{1,0:T(8,128)(2,1)S(1)}, bf16[48,2432]{1,0:T(8,128)(2,1)S(1)}, u32[]{:S(2)}, u32[]{:S(2)}) collective-permute-start(bf16[48,2432]{1,0:T(8,128)(2,1)S(1)} %collective-permute-done.refs_1_), channel_id=1, source_target_pairs={{0,8},{8,0},{1,9},{9,1},{2,10},{10,2},{3,11},{11,3},{4,12},{12,4},... | collective-permute-start | bytes 700424 | tf_op jit(solution)/shard_map/ppermute | solution.py:507
  19.0 7.8 %collective-permute-start.12 = (bf16[48,2432]{1,0:T(8,128)(2,1)S(1)}, bf16[48,2432]{1,0:T(8,128)(2,1)S(1)}, u32[]{:S(2)}, u32[]{:S(2)}) collective-permute-start(bf16[48,2432]{1,0:T(8,128)(2,1)S(1)} %collective-permute-done.5.refs_6_), channel_id=1, source_target_pairs={{0,8},{8,0},{1,9},{9,1},{2,10},{10,2},{3,11},{11,3},{4,12},{12,4},... | collective-permute-start | bytes 700424 | tf_op jit(solution)/shard_map/ppermute | solution.py:507
  19.5 7.4 %collective-permute-start.7 = (bf16[48,2432]{1,0:T(8,128)(2,1)S(1)}, bf16[48,2432]{1,0:T(8,128)(2,1)S(1)}, u32[]{:S(2)}, u32[]{:S(2)}) collective-permute-start(bf16[48,2432]{1,0:T(8,128)(2,1)S(1)} %collective-permute-done.6.refs_7_), channel_id=1, source_target_pairs={{0,1},{8,10},{1,3},{9,8},{3,5},{11,9},{5,7},{13,11},{7,6},{15,13},... | collective-permute-start | bytes 700424 | tf_op jit(solution)/shard_map/ppermute | solution.py:489
  21.8 6.2 %collective-permute-start.3 = (bf16[48,2432]{1,0:T(8,128)(2,1)S(1)}, bf16[48,2432]{1,0:T(8,128)(2,1)S(1)}, u32[]{:S(2)}, u32[]{:S(2)}) collective-permute-start(bf16[48,2432]{1,0:T(8,128)(2,1)S(1)} %collective-permute-done.2.refs_3_), channel_id=1, source_target_pairs={{0,1},{8,10},{1,3},{9,8},{3,5},{11,9},{5,7},{13,11},{7,6},{15,13},... | collective-permute-start | bytes 700424 | tf_op jit(solution)/shard_map/ppermute | solution.py:489
  23.8 0.9 %copy-start.1 = (bf16[2,1,82,384]{3,0,2,1:T(2,128)(2,1)S(1)}, bf16[2,1,82,384]{3,0,2,1:T(2,128)(2,1)}, u32[]{:S(2)}) copy-start(bf16[2,1,82,384]{3,0,2,1:T(2,128)(2,1)} %param.12) | copy-start | bytes 377860
  24.7 0.7 copy-start.2
  26.2 1.8 %collective-permute-start.9 = (bf16[48,2432]{1,0:T(8,128)(2,1)S(1)}, bf16[48,2432]{1,0:T(8,128)(2,1)S(1)}, u32[]{:S(2)}, u32[]{:S(2)}) collective-permute-start(bf16[48,2432]{1,0:T(8,128)(2,1)S(1)} %collective-permute-done.1.refs_2_), channel_id=1, source_target_pairs={{0,8},{8,0},{1,9},{9,1},{2,10},{10,2},{3,11},{11,3},{4,12},{12,4},... | collective-permute-start | bytes 700424 | tf_op jit(solution)/shard_map/ppermute | solution.py:507
  26.3 2.1 %collective-permute-start.10 = (bf16[48,2432]{1,0:T(8,128)(2,1)S(1)}, bf16[48,2432]{1,0:T(8,128)(2,1)S(1)}, u32[]{:S(2)}, u32[]{:S(2)}) collective-permute-start(bf16[48,2432]{1,0:T(8,128)(2,1)S(1)} %collective-permute-done.2.refs_3_), channel_id=1, source_target_pairs={{0,8},{8,0},{1,9},{9,1},{2,10},{10,2},{3,11},{11,3},{4,12},{12,4},... | collective-permute-start | bytes 700424 | tf_op jit(solution)/shard_map/ppermute | solution.py:507
  26.8 1.6 %collective-permute-start.13 = (bf16[48,2432]{1,0:T(8,128)(2,1)S(1)}, bf16[48,2432]{1,0:T(8,128)(2,1)S(1)}, u32[]{:S(2)}, u32[]{:S(2)}) collective-permute-start(bf16[48,2432]{1,0:T(8,128)(2,1)S(1)} %collective-permute-done.6.refs_7_), channel_id=1, source_target_pairs={{0,8},{8,0},{1,9},{9,1},{2,10},{10,2},{3,11},{11,3},{4,12},{12,4},... | collective-permute-start | bytes 700424 | tf_op jit(solution)/shard_map/ppermute | solution.py:507
  26.9 1.9 %collective-permute-start.14 = (bf16[48,2432]{1,0:T(8,128)(2,1)S(1)}, bf16[48,2432]{1,0:T(8,128)(2,1)S(1)}, u32[]{:S(2)}, u32[]{:S(2)}) collective-permute-start(bf16[48,2432]{1,0:T(8,128)(2,1)S(1)} %collective-permute-done.7.refs_8_), channel_id=1, source_target_pairs={{0,8},{8,0},{1,9},{9,1},{2,10},{10,2},{3,11},{11,3},{4,12},{12,4},... | collective-permute-start | bytes 700424 | tf_op jit(solution)/shard_map/ppermute | solution.py:507
  28.0 1.5 %collective-permute-start.11 = (bf16[48,2432]{1,0:T(8,128)(2,1)S(1)}, bf16[48,2432]{1,0:T(8,128)(2,1)S(1)}, u32[]{:S(2)}, u32[]{:S(2)}) collective-permute-start(bf16[48,2432]{1,0:T(8,128)(2,1)S(1)} %collective-permute-done.3.refs_4_), channel_id=1, source_target_pairs={{0,8},{8,0},{1,9},{9,1},{2,10},{10,2},{3,11},{11,3},{4,12},{12,4},... | collective-permute-start | bytes 700424 | tf_op jit(solution)/shard_map/ppermute | solution.py:507
  33.7 4.7 %collective-permute-start.15 = (bf16[2,1,82,384]{3,2,1,0:T(8,128)(2,1)S(1)}, bf16[2,1,82,384]{3,2,1,0:T(8,128)(2,1)S(1)}, u32[]{:S(2)}, u32[]{:S(2)}) collective-permute-start(bf16[2,1,82,384]{3,2,1,0:T(8,128)(2,1)S(1)} %get-tuple-element.55), channel_id=1, source_target_pairs={{0,16},{1,17},{2,18},{3,19},{4,20},{5,21},{6,22},{7,23},{8,24},{9,... | collective-permute-start | bytes 377864 | tf_op jit(solution)/shard_map/ppermute | solution.py:603
  41.0 9.9 %collective-permute-start.16 = (bf16[2,1,82,384]{3,2,1,0:T(8,128)(2,1)S(1)}, bf16[2,1,82,384]{3,2,1,0:T(8,128)(2,1)S(1)}, u32[]{:S(2)}, u32[]{:S(2)}) collective-permute-start(bf16[2,1,82,384]{3,2,1,0:T(8,128)(2,1)S(1)} %get-tuple-element.58.own), channel_id=1, source_target_pairs={{16,0},{17,1},{18,2},{19,3},{20,4},{21,5},{22,6},{23,7},{24,8},{25... | collective-permute-start | bytes 377864 | tf_op jit(solution)/shard_map/ppermute | solution.py:612
  55.1 1.9 %collective-permute-start.17 = (bf16[2,48,2432]{2,1,0:T(8,128)(2,1)S(1)}, bf16[2,48,2432]{2,1,0:T(8,128)(2,1)S(1)}, u32[]{:S(2)}, u32[]{:S(2)}) collective-permute-start(bf16[2,48,2432]{2,1,0:T(8,128)(2,1)S(1)} %slice.69), channel_id=1, source_target_pairs={{0,8},{8,0},{1,9},{9,1},{2,10},{10,2},{3,11},{11,3},{4,12},{12,4},... | collective-permute-start | bytes 1400840 | tf_op jit(solution)/shard_map/ppermute | solution.py:516
  57.2 6.3 %collective-permute-start.18 = (bf16[6,48,2432]{2,1,0:T(8,128)(2,1)S(1)}, bf16[6,48,2432]{2,1,0:T(8,128)(2,1)S(1)}, u32[]{:S(2)}, u32[]{:S(2)}) collective-permute-start(bf16[6,48,2432]{2,1,0:T(8,128)(2,1)S(1)} %slice.67), channel_id=1, source_target_pairs={{0,8},{8,0},{1,9},{9,1},{2,10},{10,2},{3,11},{11,3},{4,12},{12,4},... | collective-permute-start | bytes 4202504 | tf_op jit(solution)/shard_map/ppermute | solution.py:527
  57.4 6.1 %collective-permute-start.19 = (bf16[48,2432]{1,0:T(8,128)(2,1)S(1)}, bf16[48,2432]{1,0:T(8,128)(2,1)S(1)}, u32[]{:S(2)}, u32[]{:S(2)}) collective-permute-start(bf16[48,2432]{1,0:T(8,128)(2,1)S(1)} %get-tuple-element.103), channel_id=1, source_target_pairs={{0,1},{8,10},{1,3},{9,8},{3,5},{11,9},{5,7},{13,11},{7,6},{15,13},... | collective-permute-start | bytes 700424 | tf_op jit(solution)/shard_map/ppermute | solution.py:489
  59.2 6.7 %collective-permute-start.21 = (bf16[48,2432]{1,0:T(8,128)(2,1)S(1)}, bf16[48,2432]{1,0:T(8,128)(2,1)S(1)}, u32[]{:S(2)}, u32[]{:S(2)}) collective-permute-start(bf16[48,2432]{1,0:T(8,128)(2,1)S(1)} %get-tuple-element.102), channel_id=1, source_target_pairs={{0,1},{8,10},{1,3},{9,8},{3,5},{11,9},{5,7},{13,11},{7,6},{15,13},... | collective-permute-start | bytes 700424 | tf_op jit(solution)/shard_map/ppermute | solution.py:489
  63.5 6.1 %collective-permute-start.20 = (bf16[48,2432]{1,0:T(8,128)(2,1)S(1)}, bf16[48,2432]{1,0:T(8,128)(2,1)S(1)}, u32[]{:S(2)}, u32[]{:S(2)}) collective-permute-start(bf16[48,2432]{1,0:T(8,128)(2,1)S(1)} %fusion.2), channel_id=1, source_target_pairs={{0,1},{8,10},{1,3},{9,8},{3,5},{11,9},{5,7},{13,11},{7,6},{15,13},... | collective-permute-start | bytes 700424 | tf_op jit(solution)/shard_map/ppermute | solution.py:489
  66.0 6.1 %collective-permute-start.23 = (bf16[48,2432]{1,0:T(8,128)(2,1)S(1)}, bf16[48,2432]{1,0:T(8,128)(2,1)S(1)}, u32[]{:S(2)}, u32[]{:S(2)}) collective-permute-start(bf16[48,2432]{1,0:T(8,128)(2,1)S(1)} %fusion.1), channel_id=1, source_target_pairs={{0,1},{8,10},{1,3},{9,8},{3,5},{11,9},{5,7},{13,11},{7,6},{15,13},... | collective-permute-start | bytes 700424 | tf_op jit(solution)/shard_map/ppermute | solution.py:489
  69.7 6.1 %collective-permute-start.22 = (bf16[48,2432]{1,0:T(8,128)(2,1)S(1)}, bf16[48,2432]{1,0:T(8,128)(2,1)S(1)}, u32[]{:S(2)}, u32[]{:S(2)}) collective-permute-start(bf16[48,2432]{1,0:T(8,128)(2,1)S(1)} %fusion.3), channel_id=1, source_target_pairs={{0,1},{8,10},{1,3},{9,8},{3,5},{11,9},{5,7},{13,11},{7,6},{15,13},... | collective-permute-start | bytes 700424 | tf_op jit(solution)/shard_map/ppermute | solution.py:489
  72.3 6.1 %collective-permute-start.25 = (bf16[48,2432]{1,0:T(8,128)(2,1)S(1)}, bf16[48,2432]{1,0:T(8,128)(2,1)S(1)}, u32[]{:S(2)}, u32[]{:S(2)}) collective-permute-start(bf16[48,2432]{1,0:T(8,128)(2,1)S(1)} %fusion), channel_id=1, source_target_pairs={{0,1},{8,10},{1,3},{9,8},{3,5},{11,9},{5,7},{13,11},{7,6},{15,13},... | collective-permute-start | bytes 700424 | tf_op jit(solution)/shard_map/ppermute | solution.py:489
  76.0 6.1 %collective-permute-start.24 = (bf16[48,2432]{1,0:T(8,128)(2,1)S(1)}, bf16[48,2432]{1,0:T(8,128)(2,1)S(1)}, u32[]{:S(2)}, u32[]{:S(2)}) collective-permute-start(bf16[48,2432]{1,0:T(8,128)(2,1)S(1)} %fusion.4), channel_id=1, source_target_pairs={{0,1},{8,10},{1,3},{9,8},{3,5},{11,9},{5,7},{13,11},{7,6},{15,13},... | collective-permute-start | bytes 700424 | tf_op jit(solution)/shard_map/ppermute | solution.py:489
  78.4 1.5 %collective-permute-start.26 = (bf16[48,2432]{1,0:T(8,128)(2,1)S(1)}, bf16[48,2432]{1,0:T(8,128)(2,1)S(1)}, u32[]{:S(2)}, u32[]{:S(2)}) collective-permute-start(bf16[48,2432]{1,0:T(8,128)(2,1)S(1)} %collective-permute-done.25), channel_id=1, source_target_pairs={{0,8},{8,0},{1,9},{9,1},{2,10},{10,2},{3,11},{11,3},{4,12},{12,4},... | collective-permute-start | bytes 700424 | tf_op jit(solution)/shard_map/ppermute | solution.py:536
